TPU v7x, 32 devices: a whole 2x2x4 slice. The times are simulated.
32 devices in a mesh: ty: 8 (over y, x, core), tx: 4 (over z).
Axes of the slice: x: 2, y: 2, z: 4, core: 2. Of those that a mesh axis runs over, the one named last changes fastest.
Arguments:
- object_field: float32 [2, 2048, 1024], P(None, 'ty', 'tx'), may hold values from -6 to 6
- probe_modes: float32 [2, 2, 256, 256], replicated, may hold values from -6 to 6
- intensities: float32 [8, 4, 3, 256, 256], P('ty', 'tx'), may hold values from 0.25 to 16
- offsets: int32 [8, 4, 3, 2], P('ty', 'tx'), may hold values from 0 to 256
- counts: int32 [8, 4], replicated, may hold values from 1 to 3, as said below
Outputs:
- object_grad: float32 [2, 2048, 1024], P(None, 'ty', 'tx')
- probe_grad: float32 [2, 2, 256, 256], replicated
Inputs may be any that keep to these rules, and one draw needn't show every extreme that they name: Tile (a, b) uses slots 0 to counts[a, b] - 1 of intensities and offsets; its other slots are ignored. In every draw some tile uses all 3 slots.
All inputs are finite; a program needn't handle non-finite values.
Results may differ from a plain program's by a relative error of at most 0.0003.
Values sent between devices are 32-bit elements; how exact they have to be, the bound alone decides.
No kernel may reach another device: no remote copies, remote signals or barrier semaphores. Data moves between devices by JAX's collectives and lax.ppermute only.
A program may use at most 64 MiB of HBM per device.

v0:
```python
import math

import jax
import jax.numpy as jnp
from jax import lax
from jax.sharding import PartitionSpec as P

FLOOR = 0.5
exact_mode = lax.Precision.HIGHEST


def shifted(value, axis, steps):
    count = lax.axis_size(axis)
    initial, last = (max(0, -steps), min(count, count - steps))
    return lax.ppermute(value, axis, [(source, source + steps) for source in range(initial, last)])


def padded_2(shard, sides, width):
    for axis, dim in sides:
        count, length = (lax.axis_size(axis), shard.shape[dim])
        up = [(i, (i + 1) % count) for i in range(count - 1)]
        down = [(j, i) for i, j in up]
        last = lax.slice_in_dim(shard, length - width, length, axis=dim)
        initial = lax.slice_in_dim(shard, 0, width, axis=dim)
        before = lax.ppermute(last, axis, up)
        after = lax.ppermute(initial, axis, down)
        shard = jnp.concatenate([before, shard, after], axis=dim)
    return shard


def fourier_tables(pattern):
    steps_range = jnp.arange(pattern, dtype=jnp.int32)
    product = steps_range[:, None] * steps_range[None, :] % pattern
    angle = 2.0 * math.pi / pattern * product.astype(jnp.float32)
    norm_factor = 1.0 / math.sqrt(pattern)
    return (jnp.cos(angle) * norm_factor, jnp.sin(angle) * norm_factor)


def transform(real_part, imag_part, cosine, sine, direction):
    left_real = jnp.einsum(
        "kn,mnj->mkj", cosine, real_part, precision=exact_mode
    ) - direction * jnp.einsum("kn,mnj->mkj", sine, imag_part, precision=exact_mode)
    left_imag = jnp.einsum(
        "kn,mnj->mkj", cosine, imag_part, precision=exact_mode
    ) + direction * jnp.einsum("kn,mnj->mkj", sine, real_part, precision=exact_mode)
    out_real = jnp.einsum(
        "mkn,nj->mkj", left_real, cosine, precision=exact_mode
    ) - direction * jnp.einsum("mkn,nj->mkj", left_imag, sine, precision=exact_mode)
    out_imag = jnp.einsum(
        "mkn,nj->mkj", left_imag, cosine, precision=exact_mode
    ) + direction * jnp.einsum("mkn,nj->mkj", left_real, sine, precision=exact_mode)
    return (out_real, out_imag)


def slot_gradient(patch, measured, probe_modes, cosine, sine):
    probe_real, probe_imag = (probe_modes[0], probe_modes[1])
    patch_real, patch_imag = (patch[0], patch[1])
    wave_real = probe_real * patch_real - probe_imag * patch_imag
    wave_imag = probe_real * patch_imag + probe_imag * patch_real
    far_real, far_imag = transform(wave_real, wave_imag, cosine, sine, -1.0)
    amplitude = jnp.sqrt(jnp.sum(far_real * far_real + far_imag * far_imag, axis=0))
    factor = 1.0 - jnp.sqrt(measured) / jnp.maximum(amplitude, FLOOR)
    back_real, back_imag = transform(far_real * factor, far_imag * factor, cosine, sine, 1.0)
    object_part = jnp.stack(
        [
            jnp.sum(probe_real * back_real + probe_imag * back_imag, axis=0),
            jnp.sum(probe_real * back_imag - probe_imag * back_real, axis=0),
        ]
    )
    probe_part = jnp.stack(
        [
            patch_real * back_real + patch_imag * back_imag,
            patch_real * back_imag - patch_imag * back_real,
        ]
    )
    return (object_part, probe_part)


def pass_columns(piece, offset):
    return shifted(piece, "tx", offset)


def pass_rows(piece, offset):
    return shifted(piece, "ty", offset)


def shards(object_field, probe_modes, intensities, offsets, counts):
    tile_cells = object_field.shape[1]
    pattern = probe_modes.shape[2]
    margin = pattern // 2
    cosine, sine = fourier_tables(pattern)
    widened = padded_2(object_field, (("tx", 2),), margin)
    padded = padded_2(widened, (("ty", 1),), margin)
    tile_row = lax.axis_index("ty")
    tile_col = lax.axis_index("tx")
    listed = counts[tile_row, tile_col]
    measured_all = intensities[0, 0]
    spots = offsets[0, 0]

    def window(field, slot_index):
        return lax.dynamic_slice(
            field, (0, spots[slot_index, 0], spots[slot_index, 1]), (2, pattern, pattern)
        )

    def add_patch(grid, part, slot_index):
        start = (0, spots[slot_index, 0], spots[slot_index, 1])
        current = lax.dynamic_slice(grid, start, part.shape)
        return lax.dynamic_update_slice(grid, current + part, start)

    def home_step(slot_index, carry):
        grid, probe_sum = carry
        object_part, probe_part = slot_gradient(
            window(padded, slot_index), measured_all[slot_index], probe_modes, cosine, sine
        )
        return (add_patch(grid, object_part, slot_index), probe_sum + probe_part)

    start_carry = (jnp.zeros(padded.shape, jnp.float32), jnp.zeros(probe_modes.shape, jnp.float32))
    grid, probe_sum = lax.fori_loop(0, listed, home_step, start_carry)
    from_right = pass_columns(grid[:, :, :margin], -1)
    from_left = pass_columns(grid[:, :, tile_cells + margin :], 1)
    middle = grid[:, :, margin : tile_cells + margin]
    middle = middle.at[:, :, tile_cells - margin :].add(from_right)
    middle = middle.at[:, :, :margin].add(from_left)
    from_below = pass_rows(middle[:, :margin, :], -1)
    from_above = pass_rows(middle[:, tile_cells + margin :, :], 1)
    inner = middle[:, margin : tile_cells + margin, :]
    inner = inner.at[:, tile_cells - margin :, :].add(from_below)
    inner = inner.at[:, :margin, :].add(from_above)
    probe_total = lax.psum(probe_sum, ("ty", "tx"))
    return (inner, probe_total / (lax.axis_size("ty") * lax.axis_size("tx")))


def solution(mesh):
    placed = (
        P(None, "ty", "tx"),
        P(),
        P("ty", "tx", None, None, None),
        P("ty", "tx", None, None),
        P(),
    )
    return jax.shard_map(
        shards, mesh=mesh, in_specs=placed, out_specs=(P(None, "ty", "tx"), P()), check_vma=False
    )
```

profile of v0, /device:TPU:0, one launch (start us, length us, event | category | flops | bytes accessed | tf_op | source)
XLA Modules:
  0.0 329.3 jit_solution(8172643540502661335)
XLA Ops:
  7.2 0.0 all-reduce.2.cloned.1.call-start
  7.2 1.1 fusion.148
  8.3 4.9 %collective-permute-start = (f32[2,256,128]{2,1,0:T(8,128)S(1)}, f32[2,256,128]{2,1,0:T(8,128)S(1)}, u32[]{:S(2)}, u32[]{:S(2)}) collective-permute-start(f32[2,256,128]{2,1,0:T(8,128)S(1)} %get-tuple-element.243), channel_id=1, source_target_pairs={{0,1},{1,2},{2,3},{4,5},{5,6},{6,7},{8,9},{9,10},{10,11},{12,13},{... | collective-permute-start | bytes 786440 | tf_op jit(solution)/shard_map/ppermute | solution.py:25
  13.2 1.3 collective-permute-start.1
  14.5 4.2 %collective-permute-done = f32[2,256,128]{2,1,0:T(8,128)S(1)} collective-permute-done((f32[2,256,128]{2,1,0:T(8,128)S(1)}, f32[2,256,128]{2,1,0:T(8,128)S(1)}, u32[]{:S(2)}, u32[]{:S(2)}) %collective-permute-start) | collective-permute-done | bytes 262176 | tf_op jit(solution)/shard_map/ppermute | solution.py:25
  18.8 1.1 constant_dynamic-update-slice_fusion.1
  19.9 3.0 collective-permute-done.1
  22.9 0.1 fusion.147
  23.0 1.3 collective-permute-start.2
  24.3 1.3 collective-permute-start.3
  25.6 1.3 dynamic_slice.20
  26.9 0.0 collective-permute-done.2
  26.9 2.9 collective-permute-done.3
  29.8 1.5 pad_maximum_fusion
  31.3 0.0 copy-start.2
  31.3 0.1 broadcast_in_dim.5
  31.4 1.6 broadcast_in_dim.4
  33.0 0.0 copy-done.2
  33.0 0.0 copy-done.4
  33.0 46.3 %while.18 = (s32[]{:T(128)}, f32[2,512,512]{2,1,0:T(8,128)}, f32[2,2,256,256]{3,2,1,0:T(8,128)S(1)}, s32[]{:T(128)}, s32[3,2]{0,1:T(2,128)S(1)}, /*index=5*/f32[...) while((s32[]{:T(128)}, f32[2,512,512]{2,1,0:T(8,128)}, ...), condition=%wide.region_4.5_spmd.clone.clone, body=%wide.region_0.4_spmd.clone.clone.sunk | while | flops 6464995328 | bytes 37749028 | solution.py:118
  33.7 0.7 constant_dynamic-slice_fusion.3
  38.0 1.3 dynamic-slice_bitcast_fusion.3
  39.3 1.9 fusion.238
  41.2 1.9 fusion.239
  43.1 1.8 fusion.241
  45.0 1.9 fusion.235
  46.9 1.9 fusion.236
  48.8 1.8 fusion.237
  50.6 1.8 fusion.240
  52.5 1.8 add_reduce_fusion.2
  54.3 1.1 fusion.242
  55.4 1.8 fusion.246
  57.3 1.9 fusion.247
  59.1 1.8 fusion.243
  61.0 1.9 fusion.244
  62.8 1.8 fusion.245
  64.7 1.9 convolution_add_fusion.3
  66.5 1.8 fusion.248
  68.4 2.1 add_bitcast_fusion.2
  70.5 1.4 maximum_add_fusion.4
  71.9 0.3 maximum_add_fusion.5
  72.1 6.5 %dynamic_update_slice.6 = f32[2,512,512]{2,1,0:T(8,128)} dynamic-update-slice(f32[2,512,512]{2,1,0:T(8,128)} %get-tuple-element.328, f32[2,256,256]{2,1,0:T(8,128)S(1)} %maximum_add_fusion.4, s32[]{:T(128)} %constant.147.clone.1..sunk, s32[]{:T(128)S(6)} %select_n.174, s32[]{:T(128)S(6)} %select_n.175) | dynamic-update-slice | bytes 1048580 | tf_op jit(solution)/shard_map/while/body/dynamic_update_slice | solution.py:108
  79.3 0.0 copy-start
  79.3 0.0 copy-start.1
  79.3 1.5 slice.146
  80.8 1.3 collective-permute-start.4
  82.1 1.3 slice.144
  83.4 51.6 %collective-permute-done.4 = f32[2,512,128]{2,1,0:T(8,128)S(1)} collective-permute-done((f32[2,512,128]{2,1,0:T(8,128)S(1)}, f32[2,512,128]{2,1,0:T(8,128)S(1)}, u32[]{:S(2)}, u32[]{:S(2)}) %collective-permute-start.4) | collective-permute-done | bytes 524320 | tf_op jit(solution)/shard_map/ppermute | solution.py:15
  135.0 0.0 copy-done.1
  135.0 0.1 fusion.145
  135.1 0.0 copy-done
  135.1 4.0 %collective-permute-start.5 = (f32[2,512,128]{2,1,0:T(8,128)S(1)}, f32[2,512,128]{2,1,0:T(8,128)S(1)}, u32[]{:S(2)}, u32[]{:S(2)}) collective-permute-start(f32[2,512,128]{2,1,0:T(8,128)S(1)} %get-tuple-element.236), channel_id=1, source_target_pairs={{0,1},{1,2},{2,3},{4,5},{5,6},{6,7},{8,9},{9,10},{10,11},{12,13},{... | collective-permute-start | bytes 1572872 | tf_op jit(solution)/shard_map/ppermute | solution.py:15
  139.1 0.0 all-reduce.2.cloned.1.call-update
  139.1 6.6 %collective-permute-done.5 = f32[2,512,128]{2,1,0:T(8,128)S(1)} collective-permute-done((f32[2,512,128]{2,1,0:T(8,128)S(1)}, f32[2,512,128]{2,1,0:T(8,128)S(1)}, u32[]{:S(2)}, u32[]{:S(2)}) %collective-permute-start.5) | collective-permute-done | bytes 524320 | tf_op jit(solution)/shard_map/ppermute | solution.py:15
  145.7 0.1 fusion.142
  145.9 9.9 %collective-permute-start.7 = (f32[2,128,256]{2,1,0:T(8,128)S(1)}, f32[2,128,256]{2,1,0:T(8,128)S(1)}, u32[]{:S(2)}, u32[]{:S(2)}) collective-permute-start(f32[2,128,256]{2,1,0:T(8,128)S(1)} %get-tuple-element.238), channel_id=1, source_target_pairs={{0,4},{4,8},{8,12},{12,16},{16,20},{20,24},{24,28},{1,5},{5,9},{9,... | collective-permute-start | bytes 786440 | tf_op jit(solution)/shard_map/ppermute | solution.py:15
  155.8 1.3 collective-permute-start.6
  157.1 162.1 %all-reduce.2.cloned.1.call-done = f32[2,2,256,256]{3,2,1,0:T(8,128)} async-done(((f32[2,2,256,256]{3,2,1,0:T(8,128)}), f32[2,2,256,256]{3,2,1,0:T(8,128)}) %all-reduce.2.cloned.1.call-update) | async-done | bytes 1048592 | tf_op jit(solution)/shard_map/psum | solution.py:129
  319.3 2.3 broadcast_multiply_fusion
  321.6 0.0 collective-permute-done.6
  321.6 0.0 collective-permute-done.7
  321.6 0.1 fusion.143
  321.7 0.0 copy-start.3
  321.7 0.8 copy-done.3
  (6 shorter events, 0.1 us)
Async XLA Ops:
  7.2 312.1 %all-reduce.2.cloned.1.call-start = ((), (), s32[]{:S(2)}) async-start(), calls=%async_computation | async-start | bytes 2097152 | tf_op jit(solution)/shard_map/psum | solution.py:129
  8.3 10.5 %collective-permute-start = (f32[2,256,128]{2,1,0:T(8,128)S(1)}, f32[2,256,128]{2,1,0:T(8,128)S(1)}, u32[]{:S(2)}, u32[]{:S(2)}) collective-permute-start(f32[2,256,128]{2,1,0:T(8,128)S(1)} %get-tuple-element.243), channel_id=1, source_target_pairs={{0,1},{1,2},{2,3},{4,5},{5,6},{6,7},{8,9},{9,10},{10,11},{12,13},{... | collective-permute-start | bytes 786440 | tf_op jit(solution)/shard_map/ppermute | solution.py:25
  13.2 9.7 %collective-permute-start.1 = (f32[2,256,128]{2,1,0:T(8,128)S(1)}, f32[2,256,128]{2,1,0:T(8,128)S(1)}, u32[]{:S(2)}, u32[]{:S(2)}) collective-permute-start(f32[2,256,128]{2,1,0:T(8,128)S(1)} %get-tuple-element.242), channel_id=1, source_target_pairs={{1,0},{2,1},{3,2},{5,4},{6,5},{7,6},{9,8},{10,9},{11,10},{13,12},{... | collective-permute-start | bytes 786440 | tf_op jit(solution)/shard_map/ppermute | solution.py:26
  23.0 3.9 %collective-permute-start.2 = (f32[2,128,512]{2,1,0:T(8,128)S(1)}, f32[2,128,512]{2,1,0:T(8,128)S(1)}, u32[]{:S(2)}, u32[]{:S(2)}) collective-permute-start(f32[2,128,512]{2,1,0:T(8,128)S(1)} %get-tuple-element.240), channel_id=1, source_target_pairs={{0,4},{4,8},{8,12},{12,16},{16,20},{20,24},{24,28},{1,5},{5,9},{9,... | collective-permute-start | bytes 1572872 | tf_op jit(solution)/shard_map/ppermute | solution.py:25
  24.3 5.5 %collective-permute-start.3 = (f32[2,128,512]{2,1,0:T(8,128)S(1)}, f32[2,128,512]{2,1,0:T(8,128)S(1)}, u32[]{:S(2)}, u32[]{:S(2)}) collective-permute-start(f32[2,128,512]{2,1,0:T(8,128)S(1)} %get-tuple-element.241), channel_id=1, source_target_pairs={{4,0},{8,4},{12,8},{16,12},{20,16},{24,20},{28,24},{5,1},{9,5},{13... | collective-permute-start | bytes 1572872 | tf_op jit(solution)/shard_map/ppermute | solution.py:26
  31.3 1.7 copy-start.2
  31.3 1.7 copy-start.4
  79.3 55.8 %copy-start = (f32[2,2,256,256]{3,2,1,0:T(8,128)}, f32[2,2,256,256]{3,2,1,0:T(8,128)S(1)}, u32[]{:S(2)}) copy-start(f32[2,2,256,256]{3,2,1,0:T(8,128)S(1)} %get-tuple-element.147) | copy-start | bytes 3145732
  79.3 55.7 %copy-start.1 = (f32[2,512,512]{2,1,0:T(8,128)S(1)}, f32[2,512,512]{2,1,0:T(8,128)}, u32[]{:S(2)}) copy-start(f32[2,512,512]{2,1,0:T(8,128)} %get-tuple-element.146) | copy-start | bytes 6291460
  80.8 54.2 %collective-permute-start.4 = (f32[2,512,128]{2,1,0:T(8,128)S(1)}, f32[2,512,128]{2,1,0:T(8,128)S(1)}, u32[]{:S(2)}, u32[]{:S(2)}) collective-permute-start(f32[2,512,128]{2,1,0:T(8,128)S(1)} %slice.146), channel_id=1, source_target_pairs={{1,0},{2,1},{3,2},{5,4},{6,5},{7,6},{9,8},{10,9},{11,10},{13,12},{... | collective-permute-start | bytes 1572872 | tf_op jit(solution)/shard_map/ppermute | solution.py:15
  135.1 10.6 %collective-permute-start.5 = (f32[2,512,128]{2,1,0:T(8,128)S(1)}, f32[2,512,128]{2,1,0:T(8,128)S(1)}, u32[]{:S(2)}, u32[]{:S(2)}) collective-permute-start(f32[2,512,128]{2,1,0:T(8,128)S(1)} %get-tuple-element.236), channel_id=1, source_target_pairs={{0,1},{1,2},{2,3},{4,5},{5,6},{6,7},{8,9},{9,10},{10,11},{12,13},{... | collective-permute-start | bytes 1572872 | tf_op jit(solution)/shard_map/ppermute | solution.py:15
  145.9 175.7 %collective-permute-start.7 = (f32[2,128,256]{2,1,0:T(8,128)S(1)}, f32[2,128,256]{2,1,0:T(8,128)S(1)}, u32[]{:S(2)}, u32[]{:S(2)}) collective-permute-start(f32[2,128,256]{2,1,0:T(8,128)S(1)} %get-tuple-element.238), channel_id=1, source_target_pairs={{0,4},{4,8},{8,12},{12,16},{16,20},{20,24},{24,28},{1,5},{5,9},{9,... | collective-permute-start | bytes 786440 | tf_op jit(solution)/shard_map/ppermute | solution.py:15
  155.8 165.8 %collective-permute-start.6 = (f32[2,128,256]{2,1,0:T(8,128)S(1)}, f32[2,128,256]{2,1,0:T(8,128)S(1)}, u32[]{:S(2)}, u32[]{:S(2)}) collective-permute-start(f32[2,128,256]{2,1,0:T(8,128)S(1)} %get-tuple-element.239), channel_id=1, source_target_pairs={{4,0},{8,4},{12,8},{16,12},{20,16},{24,20},{28,24},{5,1},{9,5},{13... | collective-permute-start | bytes 786440 | tf_op jit(solution)/shard_map/ppermute | solution.py:15
  321.7 0.8 copy-start.3
Sparse Core Ops, SparseCore 0:
  139.2 179.9 all-reduce.1
where the time goes:
time: 333 us; the launch traced here: 329 us
  waiting for transfers between devices  231 us (69%)
  matrix products  29.9 us (9%)
  starting transfers between devices  25.3 us (8%)
  local copies, waits for them, and re-layouts  17.4 us (5%)
  between operations  14.2 us (4%)
  other arithmetic  6.81 us (2%)
  loops' own time  5.13 us (2%)
    psum x1, waiting for transfers between devices, shards(): probe_total = lax.psum(probe_sum, ('ty', 'tx'))  162 us
    ppermute x4, waiting for transfers between devices, shifted(): lax.ppermute(value, axis, [(source, source + steps) for source in range(i...  58.3 us
    ppermute x4, starting transfers between devices, shifted(): lax.ppermute(value, axis, [(source, source + steps) for source in range(i...  16.4 us
  transfers between devices with their start and end apart: 9, of which 6 were waited for; matrix products, arithmetic and copies ran while one was open for 2% of the time, Pallas kernels for 0%

commit v1 on v0

v1 whole, which is shorter than its diff:
```python
import functools
import math

import jax
import jax.numpy as jnp
import ml_dtypes
import numpy as np
from jax import lax
from jax.experimental import pallas as pl
from jax.experimental.pallas import tpu as pltpu
from jax.sharding import PartitionSpec as P

FLOOR = 0.5
LANES = 128
CHUNK = 32
VMEM_LIMIT = 40 * 1024 * 1024


def split_table(table):
    high = table.astype(ml_dtypes.bfloat16)
    low = (table - high.astype(np.float64)).astype(ml_dtypes.bfloat16)
    return high, low


def complex_block(matrix):
    return np.block([[matrix.real, matrix.imag], [-matrix.imag, matrix.real]])


@functools.lru_cache(maxsize=None)
def fourier_tables(pattern):
    half = pattern // 2
    n = np.arange(half)
    tables = []
    for parity in (0, 1):
        k = 2 * np.arange(half) + parity
        tables.append(np.exp(-2j * np.pi * ((n[:, None] * k[None, :]) % pattern) / pattern) / math.sqrt(pattern))
    forward = [complex_block(t) for t in tables]
    inverse = [complex_block(np.conj(t).T) for t in tables]
    every = forward + [t.T for t in forward] + [t.T for t in inverse] + inverse
    return np.stack([np.stack(split_table(t)) for t in every])


def split(value):
    high = value.astype(jnp.bfloat16)
    low = (value - high.astype(jnp.float32)).astype(jnp.bfloat16)
    return high, low


def mul(a, b):
    return jnp.dot(a, b, preferred_element_type=jnp.float32)


def slots_kernel(
    scalars, spots, center, left, right, above, below, probe, root, tables,
    grad_left, grad_mid, grad_right, probe_out,
    pad, grid, patch, rows_high, rows_low, freq, sums,
):
    half = LANES
    modes = probe.shape[1]
    length = center.shape[1]
    margin = left.shape[2]
    top, bottom = slice(0, half), slice(half, 2 * half)

    pad[:, 0, margin : margin + length, :] = left[...]
    pad[:, 3, margin : margin + length, :] = right[...]
    for b in range(2):
        pad[:, 1 + b, margin : margin + length, :] = center[:, :, b * half : (b + 1) * half]
    for b in range(4):
        pad[:, b, :margin, :] = above[:, :, b * half : (b + 1) * half]
        pad[:, b, margin + length :, :] = below[:, :, b * half : (b + 1) * half]
    grid[...] = jnp.zeros_like(grid)
    sums[...] = jnp.zeros_like(sums)
    lane = lax.broadcasted_iota(jnp.int32, (CHUNK, half), 1)

    def slot_step(slot, carry):
        row0 = spots[slot, 0]
        col0 = spots[slot, 1]
        block = jnp.minimum(col0 // half, 1)
        shift = col0 - block * half
        back_shift = lax.rem(half - shift, half)
        fore_shift = lax.rem(shift, half)

        for chunk in range(half // CHUNK):
            spectra = []
            for part in range(2):
                rows = part * half + chunk * CHUNK
                here = slice(rows, rows + CHUNK)
                cells = []
                for c in range(2):
                    rolled = [
                        pltpu.roll(pad[c, block + b, pl.ds(row0 + rows, CHUNK), :], back_shift, 1) for b in range(3)
                    ]
                    for b in range(2):
                        cell = jnp.where(lane < half - shift, rolled[b], rolled[b + 1])
                        patch[c, b, here, :] = cell
                        cells.append(cell)
                lefts = []
                for m in range(modes):
                    waves = []
                    for b in range(2):
                        pr = probe[0, m, here, b * half : (b + 1) * half]
                        pi = probe[1, m, here, b * half : (b + 1) * half]
                        waves.append((pr * cells[b] - pi * cells[2 + b], pr * cells[2 + b] + pi * cells[b]))
                    (ra, ia), (rb, ib) = waves
                    lefts.append((jnp.concatenate([ra + rb, ia + ib], axis=1), jnp.concatenate([ra - rb, ia - ib], axis=1)))
                spectra.append(lefts)
            for parity in range(2):
                stacked = jnp.concatenate([spectra[part][m][parity] for m in range(modes) for part in range(2)], axis=0)
                high, low = split(stacked)
                out = mul(high, tables[parity, 0]) + (mul(low, tables[parity, 0]) + mul(high, tables[parity, 1]))
                for m in range(modes):
                    a = out[(2 * m) * CHUNK : (2 * m + 1) * CHUNK]
                    b = out[(2 * m + 1) * CHUNK : (2 * m + 2) * CHUNK]
                    for row_parity, value in enumerate((a + b, a - b)):
                        vh, vl = split(value)
                        for c in range(2):
                            at = slice(c * half + chunk * CHUNK, c * half + (chunk + 1) * CHUNK)
                            to = slice(parity * half, (parity + 1) * half)
                            rows_high[m, row_parity, at, to] = vh[:, c * half : (c + 1) * half]
                            rows_low[m, row_parity, at, to] = vl[:, c * half : (c + 1) * half]

        def row_transform(table):
            for m in range(modes):
                for parity in range(2):
                    high = rows_high[m, parity]
                    low = rows_low[m, parity]
                    freq[m, parity] = mul(tables[table + parity, 0], high) + (
                        mul(tables[table + parity, 1], high) + mul(tables[table + parity, 0], low)
                    )

        row_transform(2)

        for parity in range(2):
            for chunk in range(half // CHUNK):
                real = slice(chunk * CHUNK, (chunk + 1) * CHUNK)
                imag = slice(half + chunk * CHUNK, half + (chunk + 1) * CHUNK)
                values = [(freq[m, parity, real, :], freq[m, parity, imag, :]) for m in range(modes)]
                power = sum(re * re + im * im for re, im in values)
                factor = 1.0 - root[slot, parity, real, :] * lax.rsqrt(jnp.maximum(power, FLOOR * FLOOR))
                for m in range(modes):
                    for at, value in zip((real, imag), values[m]):
                        vh, vl = split(value * factor)
                        rows_high[m, parity, at, :] = vh
                        rows_low[m, parity, at, :] = vl

        row_transform(4)

        for chunk in range(half // CHUNK):
            real = slice(chunk * CHUNK, (chunk + 1) * CHUNK)
            imag = slice(half + chunk * CHUNK, half + (chunk + 1) * CHUNK)
            backs = []
            for q in range(2):
                cols = slice(q * half, (q + 1) * half)
                pieces = []
                for m in range(modes):
                    even = jnp.concatenate([freq[m, 0, real, cols], freq[m, 0, imag, cols]], axis=1)
                    odd = jnp.concatenate([freq[m, 1, real, cols], freq[m, 1, imag, cols]], axis=1)
                    pieces += [even + odd, even - odd]
                high, low = split(jnp.concatenate(pieces, axis=0))
                backs.append(mul(high, tables[6 + q, 0]) + (mul(low, tables[6 + q, 0]) + mul(high, tables[6 + q, 1])))
            halves = (backs[0] + backs[1], backs[0] - backs[1])
            for part in range(2):
                rows = part * half + chunk * CHUNK
                here = slice(rows, rows + CHUNK)
                total = [[0.0, 0.0], [0.0, 0.0]]
                for b in range(2):
                    xr = patch[0, b, here, :]
                    xi = patch[1, b, here, :]
                    for m in range(modes):
                        at = (2 * m + part) * CHUNK
                        br = halves[b][at : at + CHUNK, :half]
                        bi = halves[b][at : at + CHUNK, half:]
                        pr = probe[0, m, here, b * half : (b + 1) * half]
                        pi = probe[1, m, here, b * half : (b + 1) * half]
                        total[0][b] += pr * br + pi * bi
                        total[1][b] += pr * bi - pi * br
                        sums[b, 0, m, here, :] += xr * br + xi * bi
                        sums[b, 1, m, here, :] += xr * bi - xi * br
                for c in range(2):
                    ra = pltpu.roll(total[c][0], fore_shift, 1)
                    rb = pltpu.roll(total[c][1], fore_shift, 1)
                    beyond = lane >= shift
                    zero = jnp.zeros_like(ra)
                    placed = (jnp.where(beyond, ra, zero), jnp.where(beyond, rb, ra), jnp.where(beyond, zero, rb))
                    for b in range(3):
                        grid[c, block + b, pl.ds(row0 + rows, CHUNK), :] += placed[b]
        return carry

    lax.fori_loop(0, scalars[0], slot_step, 0)

    grad_left[...] = grid[:, 0]
    grad_right[...] = grid[:, 3]
    for b in range(2):
        grad_mid[:, :, b * half : (b + 1) * half] = grid[:, 1 + b]
    pieces, rows, _ = probe_out.shape
    code = scalars[1]
    for b in range(2):
        for c in range(2):
            for m in range(modes):
                first = ((b * 2 + c) * modes + m) * length
                for at in range(0, length, rows):
                    probe_out[(first + at) // rows ^ code] = sums[b, c, m, at : at + rows, :]


def join_kernel(scalars, ordered, out):
    pieces, rows, _ = ordered.shape
    _, modes, length, _ = out.shape
    code = scalars[1]
    for b in range(2):
        for c in range(2):
            for m in range(modes):
                first = ((b * 2 + c) * modes + m) * length
                for at in range(0, length, rows):
                    out[c, m, at : at + rows, b * LANES : (b + 1) * LANES] = ordered[(first + at) // rows ^ code]


def shifted(value, axis, steps):
    count = lax.axis_size(axis)
    initial, last = (max(0, -steps), min(count, count - steps))
    return lax.ppermute(value, axis, [(source, source + steps) for source in range(initial, last)])


def exchanged(value, axis, mask):
    return lax.ppermute(value, axis, [(i, i ^ mask) for i in range(lax.axis_size(axis))])


def digit_groups():
    groups = [("ty", [1])]
    for axis, first in (("ty", 1), ("tx", 0)):
        bits = [1 << i for i in range(first, lax.axis_size(axis).bit_length() - 1)]
        groups += [(axis, bits[i : i + 2]) for i in range(0, len(bits), 2)]
    return groups


def masks(bits):
    return [sum(bit for i, bit in enumerate(reversed(bits)) if j >> i & 1) for j in range(1 << len(bits))]


def own_code(groups):
    code = 0
    for axis, bits in groups:
        index = lax.axis_index(axis)
        for bit in bits:
            code = code * 2 + (index // bit) % 2
    return code


def sum_everywhere(value, groups, scale):
    for axis, bits in groups:
        places = masks(bits)
        count = value.shape[0] // len(places)
        taken = [exchanged(value[j * count : (j + 1) * count], axis, places[j]) for j in range(1, len(places))]
        value = value[:count] + sum(taken[1:], taken[0])
    value = value * scale
    for axis, bits in reversed(groups):
        value = jnp.concatenate([value] + [exchanged(value, axis, mask) for mask in masks(bits)[1:]], axis=0)
    return value


def shards(object_field, probe_modes, intensities, offsets, counts):
    length = object_field.shape[1]
    modes, pattern = probe_modes.shape[1:3]
    margin = pattern // 2
    half = LANES
    devices = lax.axis_size("ty") * lax.axis_size("tx")
    groups = digit_groups()
    vmem = pl.BlockSpec(memory_space=pltpu.VMEM)
    smem = pl.BlockSpec(memory_space=pltpu.SMEM)
    params = pltpu.CompilerParams(vmem_limit_bytes=VMEM_LIMIT)

    left = shifted(object_field[:, :, length - margin :], "tx", 1)
    right = shifted(object_field[:, :, :margin], "tx", -1)
    wide = jnp.concatenate([left, object_field, right], axis=2)
    above = shifted(wide[:, length - margin :, :], "ty", 1)
    below = shifted(wide[:, :margin, :], "ty", -1)

    listed = counts[lax.axis_index("ty"), lax.axis_index("tx")]
    scalars = jnp.stack([listed, own_code(groups)]).astype(jnp.int32)
    slots = intensities.shape[2]
    root = jnp.sqrt(intensities[0, 0]).reshape(slots, half, 2, half, 2).transpose(0, 2, 1, 4, 3).reshape(slots, 2, half, pattern)
    tables = jnp.asarray(fourier_tables(pattern))
    rows = 2 * 2 * modes * pattern // devices
    f32, bf16 = jnp.float32, jnp.bfloat16
    grad_left, grad_mid, grad_right, probe_part = pl.pallas_call(
        slots_kernel,
        out_shape=(
            jax.ShapeDtypeStruct((2, length + 2 * margin, margin), f32),
            jax.ShapeDtypeStruct((2, length + 2 * margin, length), f32),
            jax.ShapeDtypeStruct((2, length + 2 * margin, margin), f32),
            jax.ShapeDtypeStruct((devices, rows, half), f32),
        ),
        in_specs=[smem, smem] + [vmem] * 8,
        out_specs=(vmem,) * 4,
        scratch_shapes=[
            pltpu.VMEM((2, 4, length + 2 * margin, half), f32),
            pltpu.VMEM((2, 4, length + 2 * margin, half), f32),
            pltpu.VMEM((2, 2, pattern, half), f32),
            pltpu.VMEM((modes, 2, pattern, pattern), bf16),
            pltpu.VMEM((modes, 2, pattern, pattern), bf16),
            pltpu.VMEM((modes, 2, pattern, pattern), f32),
            pltpu.VMEM((2, 2, modes, pattern, half), f32),
        ],
        compiler_params=params,
        name="slots",
    )(scalars, offsets[0, 0], object_field, left, right, above, below, probe_modes, root, tables)

    from_right = shifted(grad_left, "tx", -1)
    from_left = shifted(grad_right, "tx", 1)
    middle = grad_mid + jnp.concatenate([from_left, from_right], axis=2)
    from_below = shifted(middle[:, :margin, :], "ty", -1)
    from_above = shifted(middle[:, margin + length :, :], "ty", 1)
    inner = middle[:, margin : margin + length, :] + jnp.concatenate([from_above, from_below], axis=1)

    ordered = sum_everywhere(probe_part, groups, 1.0 / devices)
    probe_grad = pl.pallas_call(
        join_kernel,
        out_shape=jax.ShapeDtypeStruct(probe_modes.shape, f32),
        in_specs=[smem, vmem],
        out_specs=vmem,
        compiler_params=params,
        name="join",
    )(scalars, ordered)
    return (inner, probe_grad)


def solution(mesh):
    placed = (
        P(None, "ty", "tx"),
        P(),
        P("ty", "tx", None, None, None),
        P("ty", "tx", None, None),
        P(),
    )
    return jax.shard_map(
        shards, mesh=mesh, in_specs=placed, out_specs=(P(None, "ty", "tx"), P()), check_vma=False
    )
```

time: 333 us -> 176 us (0.53)
  the two profiles are of different devices: /device:TPU:0 before, /device:TPU:1 now
where the time goes in v1:
time: 176 us
  local copies, waits for them, and re-layouts  90.7 us (52%)
  starting transfers between devices  39.3 us (22%)
  waiting for transfers between devices  33.6 us (19%)
  Pallas kernels  9.29 us (5%)
    sqrt x2, local copies, waits for them, and re-layouts, shards(): jnp.sqrt(intensities[0, 0]).reshape(slots, half, 2, half, 2)  53 us
    transpose x1, local copies, waits for them, and re-layouts, shards(): jnp.sqrt(intensities[0, 0]).reshape(slots, half, 2, half, 2)  26.6 us
    ppermute x14, starting transfers between devices, exchanged(): lax.ppermute(value, axis, [(i, i ^ mask) for i in range(lax.axis_size(axi...  20.2 us
    ppermute x8, starting transfers between devices, shifted(): lax.ppermute(value, axis, [(source, source + steps) for source in range(i...  19.1 us
    ppermute x14, waiting for transfers between devices, exchanged(): lax.ppermute(value, axis, [(i, i ^ mask) for i in range(lax.axis_size(axi...  17.8 us
    ppermute x8, waiting for transfers between devices, shifted(): lax.ppermute(value, axis, [(source, source + steps) for source in range(i...  15.8 us
    pallas_call x1, Pallas kernels, shards(): pl.pallas_call(slots_kernel, out_shape=(jax.ShapeDtypeStruct((2, length +...  7.69 us
    unnamed x24, local copies, waits for them, and re-layouts  5.73 us
  transfers between devices with their start and end apart: 22, of which 16 were waited for; matrix products, arithmetic and copies ran while one was open for 49% of the time, Pallas kernels for 0%

profile of v1, /device:TPU:1, one launch (start us, length us, event | category | flops | bytes accessed | tf_op | source)
XLA Modules:
  0.0 175.7 jit_solution(8058091587758045311)
XLA Ops:
  0.6 1.1 fusion.5
  1.7 4.0 %collective-permute-start = (f32[2,256,128]{2,1,0:T(8,128)S(1)}, f32[2,256,128]{2,1,0:T(8,128)S(1)}, u32[]{:S(2)}, u32[]{:S(2)}) collective-permute-start(f32[2,256,128]{2,1,0:T(8,128)S(1)} %get-tuple-element.20), channel_id=1, source_target_pairs={{0,1},{1,2},{2,3},{4,5},{5,6},{6,7},{8,9},{9,10},{10,11},{12,13},{... | collective-permute-start | bytes 786440 | tf_op jit(solution)/shard_map/ppermute | solution.py:220
  5.8 1.3 collective-permute-start.1
  7.1 3.6 %collective-permute-done.left = f32[2,256,128]{2,1,0:T(8,128)S(1)} collective-permute-done((f32[2,256,128]{2,1,0:T(8,128)S(1)}, f32[2,256,128]{2,1,0:T(8,128)S(1)}, u32[]{:S(2)}, u32[]{:S(2)}) %collective-permute-start) | collective-permute-done | bytes 262176 | tf_op jit(solution)/shard_map/ppermute | solution.py:220
  10.7 0.7 copy-done.2
  11.4 1.1 constant_dynamic-update-slice_fusion.1
  12.5 2.0 %collective-permute-done.1.right = f32[2,256,128]{2,1,0:T(8,128)S(1)} collective-permute-done((f32[2,256,128]{2,1,0:T(8,128)S(1)}, f32[2,256,128]{2,1,0:T(8,128)S(1)}, u32[]{:S(2)}, u32[]{:S(2)}) %collective-permute-start.1) | collective-permute-done | bytes 262176 | tf_op jit(solution)/shard_map/ppermute | solution.py:220
  14.5 0.7 copy-done.4
  15.3 1.0 fusion.3
  16.3 4.9 %collective-permute-start.2 = (f32[2,128,512]{2,1,0:T(8,128)}, f32[2,128,512]{2,1,0:T(8,128)}, u32[]{:S(2)}, u32[]{:S(2)}) collective-permute-start(f32[2,128,512]{2,1,0:T(8,128)} %get-tuple-element.15), channel_id=1, source_target_pairs={{0,4},{4,8},{8,12},{12,16},{16,20},{20,24},{24,28},{1,5},{5,9},{9,... | collective-permute-start | bytes 1572872 | tf_op jit(solution)/shard_map/ppermute | solution.py:220
  21.2 1.9 %collective-permute-start.3 = (f32[2,128,512]{2,1,0:T(8,128)}, f32[2,128,512]{2,1,0:T(8,128)}, u32[]{:S(2)}, u32[]{:S(2)}) collective-permute-start(f32[2,128,512]{2,1,0:T(8,128)} %get-tuple-element.14), channel_id=1, source_target_pairs={{4,0},{8,4},{12,8},{16,12},{20,16},{24,20},{28,24},{5,1},{9,5},{13... | collective-permute-start | bytes 1572872 | tf_op jit(solution)/shard_map/ppermute | solution.py:220
  23.2 1.3 sqrt.7
  24.5 0.0 copy-start.7
  24.5 0.0 copy-start
  24.5 0.0 copy-start.1
  24.5 51.7 %sqrt.8 = f32[3,128,2,128,2]{4,3,2,1,0:T(8,128)} reshape(f32[1,1,3,256,256]{4,3,2,1,0:T(8,128)S(1)} %sqrt.7) | data formatting | bytes 1572864 | tf_op jit(solution)/shard_map/sqrt | solution.py:280
  76.2 26.6 %copy.10 = f32[3,2,128,2,128]{4,3,2,1,0:T(2,128)} copy(f32[3,2,128,2,128]{3,4,1,2,0:T(8,128)} %bitcast.6) | data formatting | bytes 1572864 | tf_op jit(solution)/shard_map/transpose | solution.py:280
  102.8 1.8 %reshape.10.root = f32[3,2,128,256]{3,2,1,0:T(8,128)S(1)} reshape(f32[3,2,128,2,128]{4,3,2,1,0:T(2,128)} %copy.10) | data formatting | bytes 1572864 | tf_op jit(solution)/shard_map/reshape | solution.py:280
  104.6 0.1 copy.11.spots
  104.7 1.3 dynamic_slice.3
  105.9 0.6 pad_add_fusion.scalars
  106.6 0.0 collective-permute-done.2.above
  106.6 0.0 collective-permute-done.3.below
  106.6 0.9 copy-done.3
  107.6 0.9 copy-done.5
  108.5 1.2 copy-done.6
  109.7 7.7 %slots.1 = (f32[2,512,128]{2,1,0:T(8,128)S(1)}, f32[2,512,256]{2,1,0:T(8,128)S(1)}, f32[2,512,128]{2,1,0:T(8,128)S(1)}, f32[32,64,128]{2,1,0:T(8,128)S(1)}) custom-call(s32[2]{0:T(128)S(1)} %pad_add_fusion.scalars, s32[3,2]{1,0:T(4,128)S(1)} %copy.11.spots, f32[2,256,256]{2,1,0:T(8,128)S(1)} %copy-done, f32[2,256,128]{2,1,0:T(8,128)S(1)} %copy-done.3, ...), custom_call_target="tpu_custom_call" | custom-call | tf_op jit(solution)/shard_map/slots/pallas_call | solution.py:284
  117.5 0.1 collective-permute-start.8
  117.6 1.9 %collective-permute-done.8 = f32[16,64,128]{2,1,0:T(8,128)S(1)} collective-permute-done((f32[16,64,128]{2,1,0:T(8,128)S(1)}, f32[16,64,128]{2,1,0:T(8,128)S(1)}, u32[]{:S(2)}, u32[]{:S(2)}) %collective-permute-start.8) | collective-permute-done | bytes 524320 | tf_op jit(solution)/shard_map/ppermute | solution.py:224
  119.5 0.1 slice_add_fusion.1
  119.6 1.3 collective-permute-start.10
  120.9 2.3 %collective-permute-start.11 = (f32[4,64,128]{2,1,0:T(8,128)S(1)}, f32[4,64,128]{2,1,0:T(8,128)S(1)}, u32[]{:S(2)}, u32[]{:S(2)}) collective-permute-start(f32[4,64,128]{2,1,0:T(8,128)S(1)} %get-tuple-element.17), channel_id=1, source_target_pairs={{0,24},{4,28},{8,16},{12,20},{16,8},{20,12},{24,0},{28,4},{1,25},{... | collective-permute-start | bytes 393224 | tf_op jit(solution)/shard_map/ppermute | solution.py:224
  123.2 0.0 collective-permute-start.9
  123.2 1.3 collective-permute-start.4
  124.5 1.3 collective-permute-start.5
  125.8 0.0 collective-permute-done.10
  125.8 3.5 %collective-permute-done.11 = f32[4,64,128]{2,1,0:T(8,128)S(1)} collective-permute-done((f32[4,64,128]{2,1,0:T(8,128)S(1)}, f32[4,64,128]{2,1,0:T(8,128)S(1)}, u32[]{:S(2)}, u32[]{:S(2)}) %collective-permute-start.11) | collective-permute-done | bytes 131104 | tf_op jit(solution)/shard_map/ppermute | solution.py:224
  129.3 1.2 collective-permute-done.9
  130.5 1.5 collective-permute-start.12
  132.0 2.9 %collective-permute-start.13 = (f32[1,64,128]{2,1,0:T(8,128)S(1)}, f32[1,64,128]{2,1,0:T(8,128)S(1)}, u32[]{:S(2)}, u32[]{:S(2)}) collective-permute-start(f32[1,64,128]{2,1,0:T(8,128)S(1)} %get-tuple-element.27), channel_id=1, source_target_pairs={{0,1},{1,0},{2,3},{3,2},{4,5},{5,4},{6,7},{7,6},{8,9},{9,8},{10,11... | collective-permute-start | bytes 98312 | tf_op jit(solution)/shard_map/ppermute | solution.py:224
  134.9 0.0 collective-permute-start.14
  134.9 0.2 collective-permute-done.4
  135.1 4.7 %collective-permute-done.5 = f32[2,512,128]{2,1,0:T(8,128)S(1)} collective-permute-done((f32[2,512,128]{2,1,0:T(8,128)S(1)}, f32[2,512,128]{2,1,0:T(8,128)S(1)}, u32[]{:S(2)}, u32[]{:S(2)}) %collective-permute-start.5) | collective-permute-done | bytes 524320 | tf_op jit(solution)/shard_map/ppermute | solution.py:220
  139.8 0.1 maximum_add_fusion
  139.9 2.9 %collective-permute-done.12 = f32[1,64,128]{2,1,0:T(8,128)S(1)} collective-permute-done((f32[1,64,128]{2,1,0:T(8,128)S(1)}, f32[1,64,128]{2,1,0:T(8,128)S(1)}, u32[]{:S(2)}, u32[]{:S(2)}) %collective-permute-start.12) | collective-permute-done | bytes 32800 | tf_op jit(solution)/shard_map/ppermute | solution.py:224
  142.8 2.3 %collective-permute-done.14 = f32[1,64,128]{2,1,0:T(8,128)S(1)} collective-permute-done((f32[1,64,128]{2,1,0:T(8,128)S(1)}, f32[1,64,128]{2,1,0:T(8,128)S(1)}, u32[]{:S(2)}, u32[]{:S(2)}) %collective-permute-start.14) | collective-permute-done | bytes 32800 | tf_op jit(solution)/shard_map/ppermute | solution.py:224
  145.1 0.1 collective-permute-start.15
  145.2 0.1 collective-permute-start.16
  145.3 3.5 %collective-permute-start.17 = (f32[1,64,128]{2,1,0:T(8,128)S(1)}, f32[1,64,128]{2,1,0:T(8,128)S(1)}, u32[]{:S(2)}, u32[]{:S(2)}) collective-permute-start(f32[1,64,128]{2,1,0:T(8,128)S(1)} %get-tuple-element.11), channel_id=1, source_target_pairs={{0,3},{1,2},{2,1},{3,0},{4,7},{5,6},{6,5},{7,4},{8,11},{9,10},{10,... | collective-permute-start | bytes 98312 | tf_op jit(solution)/shard_map/ppermute | solution.py:224
  148.8 0.1 collective-permute-done.15
  148.9 1.5 collective-permute-done.17
  150.4 1.3 collective-permute-start.18
  151.7 1.1 collective-permute-start.19
  152.8 0.3 collective-permute-start.20
  153.2 1.1 collective-permute-done.18
  154.3 1.2 collective-permute-done.19
  155.6 2.0 %collective-permute-done.20 = f32[4,64,128]{2,1,0:T(8,128)S(1)} collective-permute-done((f32[4,64,128]{2,1,0:T(8,128)S(1)}, f32[4,64,128]{2,1,0:T(8,128)S(1)}, u32[]{:S(2)}, u32[]{:S(2)}) %collective-permute-start.20) | collective-permute-done | bytes 131104 | tf_op jit(solution)/shard_map/ppermute | solution.py:224
  157.6 5.9 %collective-permute-start.21 = (f32[16,64,128]{2,1,0:T(8,128)S(1)}, f32[16,64,128]{2,1,0:T(8,128)S(1)}, u32[]{:S(2)}, u32[]{:S(2)}) collective-permute-start(f32[16,64,128]{2,1,0:T(8,128)S(1)} %get-tuple-element.21), channel_id=1, source_target_pairs={{0,4},{4,0},{8,12},{12,8},{16,20},{20,16},{24,28},{28,24},{1,5},{5... | collective-permute-start | bytes 1572872 | tf_op jit(solution)/shard_map/ppermute | solution.py:224
  163.5 1.9 %collective-permute-start.6 = (f32[2,128,256]{2,1,0:T(8,128)S(1)}, f32[2,128,256]{2,1,0:T(8,128)S(1)}, u32[]{:S(2)}, u32[]{:S(2)}) collective-permute-start(f32[2,128,256]{2,1,0:T(8,128)S(1)} %get-tuple-element.12), channel_id=1, source_target_pairs={{0,4},{4,8},{8,12},{12,16},{16,20},{20,24},{24,28},{1,5},{5,9},{9,... | collective-permute-start | bytes 786440 | tf_op jit(solution)/shard_map/ppermute | solution.py:220
  165.5 2.4 %collective-permute-start.7 = (f32[2,128,256]{2,1,0:T(8,128)S(1)}, f32[2,128,256]{2,1,0:T(8,128)S(1)}, u32[]{:S(2)}, u32[]{:S(2)}) collective-permute-start(f32[2,128,256]{2,1,0:T(8,128)S(1)} %get-tuple-element.13), channel_id=1, source_target_pairs={{4,0},{8,4},{12,8},{16,12},{20,16},{24,20},{28,24},{5,1},{9,5},{13... | collective-permute-start | bytes 786440 | tf_op jit(solution)/shard_map/ppermute | solution.py:220
  167.9 0.9 collective-permute-done.6
  168.8 4.4 %collective-permute-done.7 = f32[2,128,256]{2,1,0:T(8,128)S(1)} collective-permute-done((f32[2,128,256]{2,1,0:T(8,128)S(1)}, f32[2,128,256]{2,1,0:T(8,128)S(1)}, u32[]{:S(2)}, u32[]{:S(2)}) %collective-permute-start.7) | collective-permute-done | bytes 262176 | tf_op jit(solution)/shard_map/ppermute | solution.py:220
  173.2 0.9 slice_add_fusion
  174.1 1.6 join.1
  (28 shorter events, 0.3 us)
Async XLA Ops:
  1.7 9.0 %collective-permute-start = (f32[2,256,128]{2,1,0:T(8,128)S(1)}, f32[2,256,128]{2,1,0:T(8,128)S(1)}, u32[]{:S(2)}, u32[]{:S(2)}) collective-permute-start(f32[2,256,128]{2,1,0:T(8,128)S(1)} %get-tuple-element.20), channel_id=1, source_target_pairs={{0,1},{1,2},{2,3},{4,5},{5,6},{6,7},{8,9},{9,10},{10,11},{12,13},{... | collective-permute-start | bytes 786440 | tf_op jit(solution)/shard_map/ppermute | solution.py:220
  5.8 8.8 %collective-permute-start.1 = (f32[2,256,128]{2,1,0:T(8,128)S(1)}, f32[2,256,128]{2,1,0:T(8,128)S(1)}, u32[]{:S(2)}, u32[]{:S(2)}) collective-permute-start(f32[2,256,128]{2,1,0:T(8,128)S(1)} %get-tuple-element.19), channel_id=1, source_target_pairs={{1,0},{2,1},{3,2},{5,4},{6,5},{7,6},{9,8},{10,9},{11,10},{13,12},{... | collective-permute-start | bytes 786440 | tf_op jit(solution)/shard_map/ppermute | solution.py:220
  10.7 0.7 copy-start.2
  14.5 0.7 copy-start.4
  16.3 90.3 %collective-permute-start.2 = (f32[2,128,512]{2,1,0:T(8,128)}, f32[2,128,512]{2,1,0:T(8,128)}, u32[]{:S(2)}, u32[]{:S(2)}) collective-permute-start(f32[2,128,512]{2,1,0:T(8,128)} %get-tuple-element.15), channel_id=1, source_target_pairs={{0,4},{4,8},{8,12},{12,16},{16,20},{20,24},{24,28},{1,5},{5,9},{9,... | collective-permute-start | bytes 1572872 | tf_op jit(solution)/shard_map/ppermute | solution.py:220
  21.2 85.4 %collective-permute-start.3 = (f32[2,128,512]{2,1,0:T(8,128)}, f32[2,128,512]{2,1,0:T(8,128)}, u32[]{:S(2)}, u32[]{:S(2)}) collective-permute-start(f32[2,128,512]{2,1,0:T(8,128)} %get-tuple-element.14), channel_id=1, source_target_pairs={{4,0},{8,4},{12,8},{16,12},{20,16},{24,20},{28,24},{5,1},{9,5},{13... | collective-permute-start | bytes 1572872 | tf_op jit(solution)/shard_map/ppermute | solution.py:220
  24.5 80.1 %copy-start.7 = (s32[1,1,3,2]{2,3,1,0:T(2,128)S(1)}, s32[1,1,3,2]{2,3,1,0:T(2,128)}, u32[]{:S(2)}) copy-start(s32[1,1,3,2]{2,3,1,0:T(2,128)} %param.9) | copy-start | bytes 76
  24.5 82.1 %copy-start = (f32[2,256,256]{2,1,0:T(8,128)S(1)}, f32[2,256,256]{2,1,0:T(8,128)}, u32[]{:S(2)}) copy-start(f32[2,256,256]{2,1,0:T(8,128)} %center.1) | copy-start | bytes 1572868
  24.5 82.1 %copy-start.1 = (bf16[8,2,256,256]{3,2,1,0:T(8,128)(2,1)S(1)}, bf16[8,2,256,256]{3,2,1,0:T(8,128)(2,1)}, u32[]{:S(2)}) copy-start(bf16[8,2,256,256]{3,2,1,0:T(8,128)(2,1)} %constant.90.clone.tables) | copy-start | bytes 6291460
  106.6 1.0 copy-start.3
  107.6 0.9 copy-start.5
  108.5 1.2 copy-start.6
  117.5 2.0 %collective-permute-start.8 = (f32[16,64,128]{2,1,0:T(8,128)S(1)}, f32[16,64,128]{2,1,0:T(8,128)S(1)}, u32[]{:S(2)}, u32[]{:S(2)}) collective-permute-start(f32[16,64,128]{2,1,0:T(8,128)S(1)} %slice.59), channel_id=1, source_target_pairs={{0,4},{4,0},{8,12},{12,8},{16,20},{20,16},{24,28},{28,24},{1,5},{5... | collective-permute-start | bytes 1572872 | tf_op jit(solution)/shard_map/ppermute | solution.py:224
  119.6 6.2 %collective-permute-start.10 = (f32[4,64,128]{2,1,0:T(8,128)S(1)}, f32[4,64,128]{2,1,0:T(8,128)S(1)}, u32[]{:S(2)}, u32[]{:S(2)}) collective-permute-start(f32[4,64,128]{2,1,0:T(8,128)S(1)} %get-tuple-element.16), channel_id=1, source_target_pairs={{0,8},{4,12},{8,0},{12,4},{16,24},{20,28},{24,16},{28,20},{1,9},{5... | collective-permute-start | bytes 393224 | tf_op jit(solution)/shard_map/ppermute | solution.py:224
  120.9 8.4 %collective-permute-start.11 = (f32[4,64,128]{2,1,0:T(8,128)S(1)}, f32[4,64,128]{2,1,0:T(8,128)S(1)}, u32[]{:S(2)}, u32[]{:S(2)}) collective-permute-start(f32[4,64,128]{2,1,0:T(8,128)S(1)} %get-tuple-element.17), channel_id=1, source_target_pairs={{0,24},{4,28},{8,16},{12,20},{16,8},{20,12},{24,0},{28,4},{1,25},{... | collective-permute-start | bytes 393224 | tf_op jit(solution)/shard_map/ppermute | solution.py:224
  123.2 7.3 %collective-permute-start.9 = (f32[4,64,128]{2,1,0:T(8,128)S(1)}, f32[4,64,128]{2,1,0:T(8,128)S(1)}, u32[]{:S(2)}, u32[]{:S(2)}) collective-permute-start(f32[4,64,128]{2,1,0:T(8,128)S(1)} %get-tuple-element.18), channel_id=1, source_target_pairs={{0,16},{4,20},{8,24},{12,28},{16,0},{20,4},{24,8},{28,12},{1,17},{... | collective-permute-start | bytes 393224 | tf_op jit(solution)/shard_map/ppermute | solution.py:224
  123.2 11.9 %collective-permute-start.4 = (f32[2,512,128]{2,1,0:T(8,128)S(1)}, f32[2,512,128]{2,1,0:T(8,128)S(1)}, u32[]{:S(2)}, u32[]{:S(2)}) collective-permute-start(f32[2,512,128]{2,1,0:T(8,128)S(1)} %get-tuple-element.7), channel_id=1, source_target_pairs={{0,1},{1,2},{2,3},{4,5},{5,6},{6,7},{8,9},{9,10},{10,11},{12,13},{... | collective-permute-start | bytes 1572872 | tf_op jit(solution)/shard_map/ppermute | solution.py:220
  124.5 15.3 %collective-permute-start.5 = (f32[2,512,128]{2,1,0:T(8,128)S(1)}, f32[2,512,128]{2,1,0:T(8,128)S(1)}, u32[]{:S(2)}, u32[]{:S(2)}) collective-permute-start(f32[2,512,128]{2,1,0:T(8,128)S(1)} %get-tuple-element.8), channel_id=1, source_target_pairs={{1,0},{2,1},{3,2},{5,4},{6,5},{7,6},{9,8},{10,9},{11,10},{13,12},{... | collective-permute-start | bytes 1572872 | tf_op jit(solution)/shard_map/ppermute | solution.py:220
  130.5 12.3 %collective-permute-start.12 = (f32[1,64,128]{2,1,0:T(8,128)S(1)}, f32[1,64,128]{2,1,0:T(8,128)S(1)}, u32[]{:S(2)}, u32[]{:S(2)}) collective-permute-start(f32[1,64,128]{2,1,0:T(8,128)S(1)} %get-tuple-element.29), channel_id=1, source_target_pairs={{0,2},{1,3},{2,0},{3,1},{4,6},{5,7},{6,4},{7,5},{8,10},{9,11},{10,... | collective-permute-start | bytes 98312 | tf_op jit(solution)/shard_map/ppermute | solution.py:224
  132.0 10.8 %collective-permute-start.13 = (f32[1,64,128]{2,1,0:T(8,128)S(1)}, f32[1,64,128]{2,1,0:T(8,128)S(1)}, u32[]{:S(2)}, u32[]{:S(2)}) collective-permute-start(f32[1,64,128]{2,1,0:T(8,128)S(1)} %get-tuple-element.27), channel_id=1, source_target_pairs={{0,1},{1,0},{2,3},{3,2},{4,5},{5,4},{6,7},{7,6},{8,9},{9,8},{10,11... | collective-permute-start | bytes 98312 | tf_op jit(solution)/shard_map/ppermute | solution.py:224
  134.9 10.3 %collective-permute-start.14 = (f32[1,64,128]{2,1,0:T(8,128)S(1)}, f32[1,64,128]{2,1,0:T(8,128)S(1)}, u32[]{:S(2)}, u32[]{:S(2)}) collective-permute-start(f32[1,64,128]{2,1,0:T(8,128)S(1)} %get-tuple-element.28), channel_id=1, source_target_pairs={{0,3},{1,2},{2,1},{3,0},{4,7},{5,6},{6,5},{7,4},{8,11},{9,10},{10,... | collective-permute-start | bytes 98312 | tf_op jit(solution)/shard_map/ppermute | solution.py:224
  145.1 3.7 %collective-permute-start.15 = (f32[1,64,128]{2,1,0:T(8,128)S(1)}, f32[1,64,128]{2,1,0:T(8,128)S(1)}, u32[]{:S(2)}, u32[]{:S(2)}) collective-permute-start(f32[1,64,128]{2,1,0:T(8,128)S(1)} %get-tuple-element.11), channel_id=1, source_target_pairs={{0,2},{1,3},{2,0},{3,1},{4,6},{5,7},{6,4},{7,5},{8,10},{9,11},{10,... | collective-permute-start | bytes 98312 | tf_op jit(solution)/shard_map/ppermute | solution.py:224
  145.2 3.7 %collective-permute-start.16 = (f32[1,64,128]{2,1,0:T(8,128)S(1)}, f32[1,64,128]{2,1,0:T(8,128)S(1)}, u32[]{:S(2)}, u32[]{:S(2)}) collective-permute-start(f32[1,64,128]{2,1,0:T(8,128)S(1)} %get-tuple-element.11), channel_id=1, source_target_pairs={{0,1},{1,0},{2,3},{3,2},{4,5},{5,4},{6,7},{7,6},{8,9},{9,8},{10,11... | collective-permute-start | bytes 98312 | tf_op jit(solution)/shard_map/ppermute | solution.py:224
  145.3 5.1 %collective-permute-start.17 = (f32[1,64,128]{2,1,0:T(8,128)S(1)}, f32[1,64,128]{2,1,0:T(8,128)S(1)}, u32[]{:S(2)}, u32[]{:S(2)}) collective-permute-start(f32[1,64,128]{2,1,0:T(8,128)S(1)} %get-tuple-element.11), channel_id=1, source_target_pairs={{0,3},{1,2},{2,1},{3,0},{4,7},{5,6},{6,5},{7,4},{8,11},{9,10},{10,... | collective-permute-start | bytes 98312 | tf_op jit(solution)/shard_map/ppermute | solution.py:224
  150.4 3.9 %collective-permute-start.18 = (f32[4,64,128]{2,1,0:T(8,128)S(1)}, f32[4,64,128]{2,1,0:T(8,128)S(1)}, u32[]{:S(2)}, u32[]{:S(2)}) collective-permute-start(f32[4,64,128]{2,1,0:T(8,128)S(1)} %pad_maximum_fusion), channel_id=1, source_target_pairs={{0,16},{4,20},{8,24},{12,28},{16,0},{20,4},{24,8},{28,12},{1,17},{... | collective-permute-start | bytes 393224 | tf_op jit(solution)/shard_map/ppermute | solution.py:224
  151.7 3.8 %collective-permute-start.19 = (f32[4,64,128]{2,1,0:T(8,128)S(1)}, f32[4,64,128]{2,1,0:T(8,128)S(1)}, u32[]{:S(2)}, u32[]{:S(2)}) collective-permute-start(f32[4,64,128]{2,1,0:T(8,128)S(1)} %pad_maximum_fusion), channel_id=1, source_target_pairs={{0,8},{4,12},{8,0},{12,4},{16,24},{20,28},{24,16},{28,20},{1,9},{5... | collective-permute-start | bytes 393224 | tf_op jit(solution)/shard_map/ppermute | solution.py:224
  152.8 4.8 %collective-permute-start.20 = (f32[4,64,128]{2,1,0:T(8,128)S(1)}, f32[4,64,128]{2,1,0:T(8,128)S(1)}, u32[]{:S(2)}, u32[]{:S(2)}) collective-permute-start(f32[4,64,128]{2,1,0:T(8,128)S(1)} %pad_maximum_fusion), channel_id=1, source_target_pairs={{0,24},{4,28},{8,16},{12,20},{16,8},{20,12},{24,0},{28,4},{1,25},{... | collective-permute-start | bytes 393224 | tf_op jit(solution)/shard_map/ppermute | solution.py:224
  157.6 16.4 %collective-permute-start.21 = (f32[16,64,128]{2,1,0:T(8,128)S(1)}, f32[16,64,128]{2,1,0:T(8,128)S(1)}, u32[]{:S(2)}, u32[]{:S(2)}) collective-permute-start(f32[16,64,128]{2,1,0:T(8,128)S(1)} %get-tuple-element.21), channel_id=1, source_target_pairs={{0,4},{4,0},{8,12},{12,8},{16,20},{20,16},{24,28},{28,24},{1,5},{5... | collective-permute-start | bytes 1572872 | tf_op jit(solution)/shard_map/ppermute | solution.py:224
  163.5 5.2 %collective-permute-start.6 = (f32[2,128,256]{2,1,0:T(8,128)S(1)}, f32[2,128,256]{2,1,0:T(8,128)S(1)}, u32[]{:S(2)}, u32[]{:S(2)}) collective-permute-start(f32[2,128,256]{2,1,0:T(8,128)S(1)} %get-tuple-element.12), channel_id=1, source_target_pairs={{0,4},{4,8},{8,12},{12,16},{16,20},{20,24},{24,28},{1,5},{5,9},{9,... | collective-permute-start | bytes 786440 | tf_op jit(solution)/shard_map/ppermute | solution.py:220
  165.5 7.7 %collective-permute-start.7 = (f32[2,128,256]{2,1,0:T(8,128)S(1)}, f32[2,128,256]{2,1,0:T(8,128)S(1)}, u32[]{:S(2)}, u32[]{:S(2)}) collective-permute-start(f32[2,128,256]{2,1,0:T(8,128)S(1)} %get-tuple-element.13), channel_id=1, source_target_pairs={{4,0},{8,4},{12,8},{16,12},{20,16},{24,20},{28,24},{5,1},{9,5},{13... | collective-permute-start | bytes 786440 | tf_op jit(solution)/shard_map/ppermute | solution.py:220

commit v2 on v1

--- a/solution.py
+++ b/solution.py
@@ -13,7 +13,8 @@
 FLOOR = 0.5
 LANES = 128
 CHUNK = 32
-VMEM_LIMIT = 40 * 1024 * 1024
+VMEM_LIMIT = 28 * 1024 * 1024
+SMALL_LIMIT = 8 * 1024 * 1024
 
 
 def split_table(table):
@@ -40,6 +41,11 @@
     return np.stack([np.stack(split_table(t)) for t in every])
 
 
+@functools.lru_cache(maxsize=None)
+def column_order(pattern):
+    return np.eye(pattern)[:, np.r_[0:pattern:2, 1:pattern:2]].astype(ml_dtypes.bfloat16)
+
+
 def split(value):
     high = value.astype(jnp.bfloat16)
     low = (value - high.astype(jnp.float32)).astype(jnp.bfloat16)
@@ -50,24 +56,58 @@
     return jnp.dot(a, b, preferred_element_type=jnp.float32)
 
 
+def edges_kernel(center, to_right, to_left, to_core, to_chip):
+    half = LANES
+    to_right[...] = center[:, :, half:]
+    to_left[...] = center[:, :, :half]
+    odd = lax.axis_index("ty") % 2
+    near = pl.multiple_of((1 - odd) * half, half)
+    far = pl.multiple_of(odd * half, half)
+    to_core[...] = center[:, pl.ds(near, half), :]
+    to_chip[...] = center[:, pl.ds(far, half), :]
+
+
+def corners_kernel(left, right, to_core, to_chip):
+    half = LANES
+    odd = lax.axis_index("ty") % 2
+    near = pl.multiple_of((1 - odd) * half, half)
+    far = pl.multiple_of(odd * half, half)
+    for side, cols in enumerate((left, right)):
+        to_core[side] = cols[:, pl.ds(near, half), :]
+        to_chip[side] = cols[:, pl.ds(far, half), :]
+
+
+def root_kernel(measured, order, root, halves):
+    for slot in range(measured.shape[0]):
+        for b in range(2):
+            halves[slot, b] = jnp.sqrt(measured[slot, :, b * LANES : (b + 1) * LANES])
+        for parity in range(2):
+            rows = pl.ds(parity, LANES, stride=2)
+            high, low = split(jnp.concatenate([halves[slot, 0, rows, :], halves[slot, 1, rows, :]], axis=1))
+            root[slot, parity] = mul(high, order[...]) + mul(low, order[...])
+
+
 def slots_kernel(
-    scalars, spots, center, left, right, above, below, probe, root, tables,
-    grad_left, grad_mid, grad_right, probe_out,
+    counts, spots, center, left, right, core_rows, chip_rows, core_corners, chip_corners, probe, root, tables,
+    core_out, chip_out, grad_mid, probe_keep,
     pad, grid, patch, rows_high, rows_low, freq, sums,
 ):
     half = LANES
     modes = probe.shape[1]
     length = center.shape[1]
     margin = left.shape[2]
-    top, bottom = slice(0, half), slice(half, 2 * half)
+    odd = lax.axis_index("ty") % 2
+    near = pl.multiple_of((1 - odd) * (margin + length), half)
+    far = pl.multiple_of(odd * (margin + length), half)
 
     pad[:, 0, margin : margin + length, :] = left[...]
     pad[:, 3, margin : margin + length, :] = right[...]
     for b in range(2):
-        pad[:, 1 + b, margin : margin + length, :] = center[:, :, b * half : (b + 1) * half]
-    for b in range(4):
-        pad[:, b, :margin, :] = above[:, :, b * half : (b + 1) * half]
-        pad[:, b, margin + length :, :] = below[:, :, b * half : (b + 1) * half]
+        cols = slice(b * half, (b + 1) * half)
+        pad[:, 1 + b, margin : margin + length, :] = center[:, :, cols]
+        for start, rows, corners in ((near, core_rows, core_corners), (far, chip_rows, chip_corners)):
+            pad[:, 1 + b, pl.ds(start, margin), :] = rows[:, :, cols]
+            pad[:, 3 * b, pl.ds(start, margin), :] = corners[b]
     grid[...] = jnp.zeros_like(grid)
     sums[...] = jnp.zeros_like(sums)
     lane = lax.broadcasted_iota(jnp.int32, (CHUNK, half), 1)
@@ -174,8 +214,8 @@
                         pi = probe[1, m, here, b * half : (b + 1) * half]
                         total[0][b] += pr * br + pi * bi
                         total[1][b] += pr * bi - pi * br
-                        sums[b, 0, m, here, :] += xr * br + xi * bi
-                        sums[b, 1, m, here, :] += xr * bi - xi * br
+                        sums[pl.ds(((b * 2 + 0) * modes + m) * length + rows, CHUNK), :] += xr * br + xi * bi
+                        sums[pl.ds(((b * 2 + 1) * modes + m) * length + rows, CHUNK), :] += xr * bi - xi * br
                 for c in range(2):
                     ra = pltpu.roll(total[c][0], fore_shift, 1)
                     rb = pltpu.roll(total[c][1], fore_shift, 1)
@@ -186,32 +226,67 @@
                         grid[c, block + b, pl.ds(row0 + rows, CHUNK), :] += placed[b]
         return carry
 
-    lax.fori_loop(0, scalars[0], slot_step, 0)
-
-    grad_left[...] = grid[:, 0]
-    grad_right[...] = grid[:, 3]
-    for b in range(2):
-        grad_mid[:, :, b * half : (b + 1) * half] = grid[:, 1 + b]
-    pieces, rows, _ = probe_out.shape
-    code = scalars[1]
-    for b in range(2):
-        for c in range(2):
-            for m in range(modes):
-                first = ((b * 2 + c) * modes + m) * length
-                for at in range(0, length, rows):
-                    probe_out[(first + at) // rows ^ code] = sums[b, c, m, at : at + rows, :]
-
-
-def join_kernel(scalars, ordered, out):
-    pieces, rows, _ = ordered.shape
+    listed = counts[lax.axis_index("ty"), lax.axis_index("tx")]
+    lax.fori_loop(0, listed, slot_step, 0)
+
+    grad_mid[...] = grid[:, :, margin : margin + length, :]
+    for c in range(2):
+        for b in range(4):
+            at = slice((c * 4 + b) * margin, (c * 4 + b + 1) * margin)
+            core_out[at, :] = grid[c, b, pl.ds(near, margin), :]
+            chip_out[at, :] = grid[c, b, pl.ds(far, margin), :]
+    kept, rows, _ = probe_keep.shape
+    code = own_code(digit_groups())
+    first_sent = core_out.shape[0] - kept * rows
+
+    def place_piece(place, carry):
+        piece = place ^ code
+        probe_keep[place] = sums[pl.ds(pl.multiple_of(piece * rows, rows), rows), :]
+        piece = (place + kept) ^ code
+        core_out[pl.ds(pl.multiple_of(first_sent + place * rows, rows), rows), :] = sums[
+            pl.ds(pl.multiple_of(piece * rows, rows), rows), :
+        ]
+        return carry
+
+    lax.fori_loop(0, kept, place_piece, 0)
+
+
+def rows_kernel(grad_mid, core_in, chip_in, to_left, to_right, inner):
+    half = LANES
+    odd = lax.axis_index("ty") % 2
+    for c in range(2):
+        for b in range(4):
+            at = slice((c * 4 + b) * half, (c * 4 + b + 1) * half)
+            core, chip = core_in[at, :], chip_in[at, :]
+            for part in range(2):
+                rows = slice(part * half, (part + 1) * half)
+                value = grad_mid[c, b, rows, :] + jnp.where(odd == 1 - part, core, chip)
+                if b == 0:
+                    to_left[c, rows, :] = value
+                elif b == 3:
+                    to_right[c, rows, :] = value
+                else:
+                    inner[c, rows, (b - 1) * half : b * half] = value
+
+
+def join_kernel(own, other, out):
+    kept, rows, _ = own.shape
     _, modes, length, _ = out.shape
-    code = scalars[1]
-    for b in range(2):
-        for c in range(2):
-            for m in range(modes):
-                first = ((b * 2 + c) * modes + m) * length
-                for at in range(0, length, rows):
-                    out[c, m, at : at + rows, b * LANES : (b + 1) * LANES] = ordered[(first + at) // rows ^ code]
+    code = own_code(digit_groups())
+    each = length // rows
+
+    for first, source in ((0, own), (kept, other)):
+
+        def place_piece(place, carry, first=first, source=source):
+            piece = (place + first) ^ code
+            row = pl.multiple_of(piece % each * rows, rows)
+            m = piece // each % modes
+            c = piece // (each * modes) % 2
+            b = pl.multiple_of(piece // (each * modes * 2) * LANES, LANES)
+            out[c, m, pl.ds(row, rows), pl.ds(b, LANES)] = source[place]
+            return carry
+
+        lax.fori_loop(0, kept, place_piece, 0)
 
 
 def shifted(value, axis, steps):
@@ -245,16 +320,40 @@
     return code
 
 
-def sum_everywhere(value, groups, scale):
-    for axis, bits in groups:
-        places = masks(bits)
-        count = value.shape[0] // len(places)
-        taken = [exchanged(value[j * count : (j + 1) * count], axis, places[j]) for j in range(1, len(places))]
-        value = value[:count] + sum(taken[1:], taken[0])
-    value = value * scale
-    for axis, bits in reversed(groups):
-        value = jnp.concatenate([value] + [exchanged(value, axis, mask) for mask in masks(bits)[1:]], axis=0)
-    return value
+def paired(value, mask_of):
+    count = lax.axis_size("ty")
+    pairs = [(i, i ^ 1) for i in range(count)] if mask_of == "core" else []
+    if mask_of == "chip":
+        for i in range(1, count - 1, 2):
+            pairs += [(i, i + 1), (i + 1, i)]
+    return lax.ppermute(value, "ty", pairs)
+
+
+def reduce_step(value, axis, bits):
+    places = masks(bits)
+    count = value.shape[0] // len(places)
+    taken = [exchanged(value[j * count : (j + 1) * count], axis, places[j]) for j in range(1, len(places))]
+    return value[:count] + sum(taken[1:], taken[0])
+
+
+def gather_step(value, axis, bits):
+    return jnp.concatenate([value] + [exchanged(value, axis, mask) for mask in masks(bits)[1:]], axis=0)
+
+
+def call(body, name, out, operands, scalars=0, scratch=(), limit=SMALL_LIMIT):
+    vmem = pl.BlockSpec(memory_space=pltpu.VMEM)
+    smem = pl.BlockSpec(memory_space=pltpu.SMEM)
+    moved = sum(math.prod(v.shape) * v.dtype.itemsize for v in operands + tuple(out))
+    return pl.pallas_call(
+        body,
+        out_shape=tuple(out),
+        in_specs=[smem] * scalars + [vmem] * (len(operands) - scalars),
+        out_specs=(vmem,) * len(out),
+        scratch_shapes=list(scratch),
+        compiler_params=pltpu.CompilerParams(vmem_limit_bytes=limit),
+        cost_estimate=pl.CostEstimate(flops=0, bytes_accessed=moved, transcendentals=0),
+        name=name,
+    )(*operands)
 
 
 def shards(object_field, probe_modes, intensities, offsets, counts):
@@ -264,62 +363,70 @@
     half = LANES
     devices = lax.axis_size("ty") * lax.axis_size("tx")
     groups = digit_groups()
-    vmem = pl.BlockSpec(memory_space=pltpu.VMEM)
-    smem = pl.BlockSpec(memory_space=pltpu.SMEM)
-    params = pltpu.CompilerParams(vmem_limit_bytes=VMEM_LIMIT)
-
-    left = shifted(object_field[:, :, length - margin :], "tx", 1)
-    right = shifted(object_field[:, :, :margin], "tx", -1)
-    wide = jnp.concatenate([left, object_field, right], axis=2)
-    above = shifted(wide[:, length - margin :, :], "ty", 1)
-    below = shifted(wide[:, :margin, :], "ty", -1)
-
-    listed = counts[lax.axis_index("ty"), lax.axis_index("tx")]
-    scalars = jnp.stack([listed, own_code(groups)]).astype(jnp.int32)
+    f32, bf16 = jnp.float32, jnp.bfloat16
     slots = intensities.shape[2]
-    root = jnp.sqrt(intensities[0, 0]).reshape(slots, half, 2, half, 2).transpose(0, 2, 1, 4, 3).reshape(slots, 2, half, pattern)
     tables = jnp.asarray(fourier_tables(pattern))
+    order = jnp.asarray(column_order(pattern))
+
+    def shape(*sizes):
+        return jax.ShapeDtypeStruct(sizes, f32)
+
+    to_right, to_left, to_core, to_chip = call(
+        edges_kernel, "edges", [shape(2, length, margin)] * 2 + [shape(2, margin, length)] * 2, (object_field,)
+    )
+    left = shifted(to_right, "tx", 1)
+    right = shifted(to_left, "tx", -1)
+    chip_rows = paired(to_chip, "chip")
+    core_rows = paired(to_core, "core")
+    (root,) = call(
+        root_kernel,
+        "root",
+        [shape(slots, 2, half, pattern)],
+        (intensities[0, 0], order),
+        scratch=(pltpu.VMEM((slots, 2, pattern, half), f32),),
+    )
+    to_core, to_chip = call(corners_kernel, "corners", [shape(2, 2, margin, margin)] * 2, (left, right))
+    chip_corners = paired(to_chip, "chip")
+    core_corners = paired(to_core, "core")
+
     rows = 2 * 2 * modes * pattern // devices
-    f32, bf16 = jnp.float32, jnp.bfloat16
-    grad_left, grad_mid, grad_right, probe_part = pl.pallas_call(
+    kept = devices // 2
+    border = 2 * 4 * margin
+    core_out, chip_out, grad_mid, probe_keep = call(
         slots_kernel,
-        out_shape=(
-            jax.ShapeDtypeStruct((2, length + 2 * margin, margin), f32),
-            jax.ShapeDtypeStruct((2, length + 2 * margin, length), f32),
-            jax.ShapeDtypeStruct((2, length + 2 * margin, margin), f32),
-            jax.ShapeDtypeStruct((devices, rows, half), f32),
-        ),
-        in_specs=[smem, smem] + [vmem] * 8,
-        out_specs=(vmem,) * 4,
-        scratch_shapes=[
+        "slots",
+        [shape(border + kept * rows, half), shape(border, half), shape(2, 4, length, half), shape(kept, rows, half)],
+        (counts, offsets[0, 0], object_field, left, right, core_rows, chip_rows, core_corners, chip_corners, probe_modes, root, tables),
+        scalars=2,
+        scratch=(
             pltpu.VMEM((2, 4, length + 2 * margin, half), f32),
             pltpu.VMEM((2, 4, length + 2 * margin, half), f32),
             pltpu.VMEM((2, 2, pattern, half), f32),
             pltpu.VMEM((modes, 2, pattern, pattern), bf16),
             pltpu.VMEM((modes, 2, pattern, pattern), bf16),
             pltpu.VMEM((modes, 2, pattern, pattern), f32),
-            pltpu.VMEM((2, 2, modes, pattern, half), f32),
-        ],
-        compiler_params=params,
-        name="slots",
-    )(scalars, offsets[0, 0], object_field, left, right, above, below, probe_modes, root, tables)
-
-    from_right = shifted(grad_left, "tx", -1)
-    from_left = shifted(grad_right, "tx", 1)
-    middle = grad_mid + jnp.concatenate([from_left, from_right], axis=2)
-    from_below = shifted(middle[:, :margin, :], "ty", -1)
-    from_above = shifted(middle[:, margin + length :, :], "ty", 1)
-    inner = middle[:, margin : margin + length, :] + jnp.concatenate([from_above, from_below], axis=1)
-
-    ordered = sum_everywhere(probe_part, groups, 1.0 / devices)
-    probe_grad = pl.pallas_call(
-        join_kernel,
-        out_shape=jax.ShapeDtypeStruct(probe_modes.shape, f32),
-        in_specs=[smem, vmem],
-        out_specs=vmem,
-        compiler_params=params,
-        name="join",
-    )(scalars, ordered)
+            pltpu.VMEM((2 * 2 * modes * pattern, half), f32),
+        ),
+        limit=VMEM_LIMIT,
+    )
+
+    core_in = paired(core_out, "core")
+    chip_in = paired(chip_out, "chip")
+    value = probe_keep + core_in[border:].reshape(probe_keep.shape)
+    to_left, to_right, inner = call(
+        rows_kernel, "rows", [shape(2, length, half)] * 2 + [shape(2, length, length)], (grad_mid, core_in[:border], chip_in)
+    )
+    from_right = shifted(to_left, "tx", -1)
+    from_left = shifted(to_right, "tx", 1)
+    inner = inner + jnp.concatenate([from_left, from_right], axis=2)
+
+    for axis, bits in groups[1:]:
+        value = reduce_step(value, axis, bits)
+    value = value * (1.0 / devices)
+    for axis, bits in reversed(groups[1:]):
+        value = gather_step(value, axis, bits)
+    other = paired(value, "core")
+    (probe_grad,) = call(join_kernel, "join", [shape(*probe_modes.shape)], (value, other))
     return (inner, probe_grad)
 
 

time: 176 us -> 101 us (0.57)
  the two profiles are of different devices: /device:TPU:1 before, /device:TPU:0 now
where the time goes in v2:
time: 101 us
  waiting for transfers between devices  44.8 us (44%)
  starting transfers between devices  36.4 us (36%)
  Pallas kernels  11.8 us (12%)
  local copies, waits for them, and re-layouts  6.12 us (6%)
    ppermute x12, waiting for transfers between devices, exchanged(): lax.ppermute(value, axis, [(i, i ^ mask) for i in range(lax.axis_size(axi...  26.9 us
    ppermute x12, starting transfers between devices, exchanged(): lax.ppermute(value, axis, [(i, i ^ mask) for i in range(lax.axis_size(axi...  17.5 us
    ppermute x4, waiting for transfers between devices, shifted(): lax.ppermute(value, axis, [(source, source + steps) for source in range(i...  15.6 us
    pallas_call x6, Pallas kernels, call(): pl.pallas_call(body, out_shape=tuple(out), in_specs=[smem] * scalars + [v...  11.8 us
    ppermute x7, starting transfers between devices, paired(): return lax.ppermute(value, 'ty', pairs)  9.45 us
    ppermute x4, starting transfers between devices, shifted(): lax.ppermute(value, axis, [(source, source + steps) for source in range(i...  9.44 us
    unnamed x18, local copies, waits for them, and re-layouts  5.24 us
    ppermute x7, waiting for transfers between devices, paired(): return lax.ppermute(value, 'ty', pairs)  2.3 us
  transfers between devices with their start and end apart: 23, of which 14 were waited for; matrix products, arithmetic and copies ran while one was open for 2% of the time, Pallas kernels for 1%

profile of v2, /device:TPU:0, one launch (start us, length us, event | category | flops | bytes accessed | tf_op | source)
XLA Modules:
  0.0 100.9 jit_solution(10923408926812580587)
XLA Ops:
  0.6 0.0 copy-start
  0.6 0.0 copy-start.1
  0.7 1.2 %copy-done.1 = f32[2,256,256]{2,1,0:T(8,128)S(1)} copy-done((f32[2,256,256]{2,1,0:T(8,128)S(1)}, f32[2,256,256]{2,1,0:T(8,128)}, u32[]{:S(2)}) %copy-start.1) | copy-done | bytes 524312
  1.8 0.9 edges.1
  2.7 4.9 %collective-permute-start = (f32[2,256,128]{2,1,0:T(8,128)S(1)}, f32[2,256,128]{2,1,0:T(8,128)S(1)}, u32[]{:S(2)}, u32[]{:S(2)}) collective-permute-start(f32[2,256,128]{2,1,0:T(8,128)S(1)} %get-tuple-element.15), channel_id=1, source_target_pairs={{0,1},{1,2},{2,3},{4,5},{5,6},{6,7},{8,9},{9,10},{10,11},{12,13},{... | collective-permute-start | bytes 786440 | tf_op jit(solution)/shard_map/ppermute | solution.py:295
  7.6 1.3 %collective-permute-start.1 = (f32[2,256,128]{2,1,0:T(8,128)S(1)}, f32[2,256,128]{2,1,0:T(8,128)S(1)}, u32[]{:S(2)}, u32[]{:S(2)}) collective-permute-start(f32[2,256,128]{2,1,0:T(8,128)S(1)} %get-tuple-element.16), channel_id=1, source_target_pairs={{1,0},{2,1},{3,2},{5,4},{6,5},{7,6},{9,8},{10,9},{11,10},{13,12},{... | collective-permute-start | bytes 786440 | tf_op jit(solution)/shard_map/ppermute | solution.py:295
  8.9 0.1 collective-permute-start.2
  9.0 1.4 %collective-permute-start.3 = (f32[2,128,256]{2,1,0:T(8,128)}, f32[2,128,256]{2,1,0:T(8,128)}, u32[]{:S(2)}, u32[]{:S(2)}) collective-permute-start(f32[2,128,256]{2,1,0:T(8,128)} %get-tuple-element.18), channel_id=1, source_target_pairs={{4,8},{8,4},{12,16},{16,12},{20,24},{24,20},{5,9},{9,5},{13,17},{1... | collective-permute-start | bytes 786440 | tf_op jit(solution)/shard_map/ppermute | solution.py:329
  10.4 2.8 %collective-permute-done.left = f32[2,256,128]{2,1,0:T(8,128)S(1)} collective-permute-done((f32[2,256,128]{2,1,0:T(8,128)S(1)}, f32[2,256,128]{2,1,0:T(8,128)S(1)}, u32[]{:S(2)}, u32[]{:S(2)}) %collective-permute-start) | collective-permute-done | bytes 262176 | tf_op jit(solution)/shard_map/ppermute | solution.py:295
  13.2 4.1 %collective-permute-done.1.right = f32[2,256,128]{2,1,0:T(8,128)S(1)} collective-permute-done((f32[2,256,128]{2,1,0:T(8,128)S(1)}, f32[2,256,128]{2,1,0:T(8,128)S(1)}, u32[]{:S(2)}, u32[]{:S(2)}) %collective-permute-start.1) | collective-permute-done | bytes 262176 | tf_op jit(solution)/shard_map/ppermute | solution.py:295
  17.3 0.8 corners.1
  18.1 0.0 collective-permute-start.4
  18.1 1.4 %collective-permute-start.5 = (f32[2,2,128,128]{3,2,1,0:T(8,128)}, f32[2,2,128,128]{3,2,1,0:T(8,128)}, u32[]{:S(2)}, u32[]{:S(2)}) collective-permute-start(f32[2,2,128,128]{3,2,1,0:T(8,128)} %get-tuple-element.20), channel_id=1, source_target_pairs={{4,8},{8,4},{12,16},{16,12},{20,24},{24,20},{5,9},{9,5},{13,17},{1... | collective-permute-start | bytes 786440 | tf_op jit(solution)/shard_map/ppermute | solution.py:329
  19.5 0.8 copy.10.spots
  20.3 0.8 copy.9.counts
  21.0 1.1 %copy-done.4 = f32[1,1,3,256,256]{4,3,2,1,0:T(8,128)S(1)} copy-done((f32[1,1,3,256,256]{4,3,2,1,0:T(8,128)S(1)}, f32[1,1,3,256,256]{4,3,2,1,0:T(8,128)}, u32[]{:S(2)}) %copy-start.4) | copy-done | bytes 786456
  22.2 0.9 copy-done.5
  23.1 0.5 root.1
  23.6 0.0 collective-permute-done.2.core_rows
  23.6 0.0 collective-permute-done.3.chip_rows
  23.6 0.0 collective-permute-done.4.core_corners
  23.6 0.0 collective-permute-done.5.chip_corners
  23.6 0.0 copy-start.3
  23.7 1.2 %copy-done.3 = f32[2,2,256,256]{3,2,1,0:T(8,128)S(1)} copy-done((f32[2,2,256,256]{3,2,1,0:T(8,128)S(1)}, f32[2,2,256,256]{3,2,1,0:T(8,128)}, u32[]{:S(2)}) %copy-start.3) | copy-done | bytes 1048600
  24.9 7.7 %slots.1 = (f32[2048,128]{1,0:T(8,128)S(1)}, f32[1024,128]{1,0:T(8,128)S(1)}, f32[2,4,256,128]{3,2,1,0:T(8,128)S(1)}, f32[16,64,128]{2,1,0:T(8,128)S(1)}) custom-call(s32[8,4]{1,0:T(8,128)S(1)} %copy.9.counts, s32[3,2]{1,0:T(4,128)S(1)} %copy.10.spots, f32[2,256,256]{2,1,0:T(8,128)S(1)} %copy-done.2, f32[2,256,128]{2,1,0:T(8,128)S(1)} %collective-permute-done.left, ...), custom_call_target="tpu_custom_call" | custom-call | bytes 9175192 | tf_op jit(solution)/shard_map/slots/pallas_call | solution.py:347
  32.6 5.6 %collective-permute-start.6 = (f32[2048,128]{1,0:T(8,128)S(1)}, f32[2048,128]{1,0:T(8,128)S(1)}, u32[]{:S(2)}, u32[]{:S(2)}) collective-permute-start(f32[2048,128]{1,0:T(8,128)S(1)} %get-tuple-element.22), channel_id=1, source_target_pairs={{0,4},{4,0},{8,12},{12,8},{16,20},{20,16},{24,28},{28,24},{1,5},{5... | collective-permute-start | bytes 3145736 | tf_op jit(solution)/shard_map/ppermute | solution.py:329
  38.1 2.3 %collective-permute-done.6 = f32[2048,128]{1,0:T(8,128)S(1)} collective-permute-done((f32[2048,128]{1,0:T(8,128)S(1)}, f32[2048,128]{1,0:T(8,128)S(1)}, u32[]{:S(2)}, u32[]{:S(2)}) %collective-permute-start.6) | collective-permute-done | bytes 1048608 | tf_op jit(solution)/shard_map/ppermute | solution.py:329
  40.4 0.1 fusion.2
  40.5 0.1 add.25
  40.6 0.1 collective-permute-start.11
  40.7 1.4 %collective-permute-start.12 = (f32[4,64,128]{2,1,0:T(8,128)S(1)}, f32[4,64,128]{2,1,0:T(8,128)S(1)}, u32[]{:S(2)}, u32[]{:S(2)}) collective-permute-start(f32[4,64,128]{2,1,0:T(8,128)S(1)} %get-tuple-element.33), channel_id=1, source_target_pairs={{0,24},{4,28},{8,16},{12,20},{16,8},{20,12},{24,0},{28,4},{1,25},{... | collective-permute-start | bytes 393224 | tf_op jit(solution)/shard_map/ppermute | solution.py:299
  42.0 2.1 %collective-permute-start.10 = (f32[4,64,128]{2,1,0:T(8,128)S(1)}, f32[4,64,128]{2,1,0:T(8,128)S(1)}, u32[]{:S(2)}, u32[]{:S(2)}) collective-permute-start(f32[4,64,128]{2,1,0:T(8,128)S(1)} %get-tuple-element.34), channel_id=1, source_target_pairs={{0,16},{4,20},{8,24},{12,28},{16,0},{20,4},{24,8},{28,12},{1,17},{... | collective-permute-start | bytes 393224 | tf_op jit(solution)/shard_map/ppermute | solution.py:299
  44.2 2.8 %collective-permute-done.11 = f32[4,64,128]{2,1,0:T(8,128)S(1)} collective-permute-done((f32[4,64,128]{2,1,0:T(8,128)S(1)}, f32[4,64,128]{2,1,0:T(8,128)S(1)}, u32[]{:S(2)}, u32[]{:S(2)}) %collective-permute-start.11) | collective-permute-done | bytes 131104 | tf_op jit(solution)/shard_map/ppermute | solution.py:299
  47.0 1.7 %collective-permute-done.12 = f32[4,64,128]{2,1,0:T(8,128)S(1)} collective-permute-done((f32[4,64,128]{2,1,0:T(8,128)S(1)}, f32[4,64,128]{2,1,0:T(8,128)S(1)}, u32[]{:S(2)}, u32[]{:S(2)}) %collective-permute-start.12) | collective-permute-done | bytes 131104 | tf_op jit(solution)/shard_map/ppermute | solution.py:299
  48.7 1.7 %collective-permute-done.10 = f32[4,64,128]{2,1,0:T(8,128)S(1)} collective-permute-done((f32[4,64,128]{2,1,0:T(8,128)S(1)}, f32[4,64,128]{2,1,0:T(8,128)S(1)}, u32[]{:S(2)}, u32[]{:S(2)}) %collective-permute-start.10) | collective-permute-done | bytes 131104 | tf_op jit(solution)/shard_map/ppermute | solution.py:299
  50.5 2.1 %collective-permute-start.14 = (f32[1,64,128]{2,1,0:T(8,128)S(1)}, f32[1,64,128]{2,1,0:T(8,128)S(1)}, u32[]{:S(2)}, u32[]{:S(2)}) collective-permute-start(f32[1,64,128]{2,1,0:T(8,128)S(1)} %get-tuple-element.35), channel_id=1, source_target_pairs={{0,1},{1,0},{2,3},{3,2},{4,5},{5,4},{6,7},{7,6},{8,9},{9,8},{10,11... | collective-permute-start | bytes 98312 | tf_op jit(solution)/shard_map/ppermute | solution.py:299
  52.6 3.9 %collective-permute-start.15 = (f32[1,64,128]{2,1,0:T(8,128)S(1)}, f32[1,64,128]{2,1,0:T(8,128)S(1)}, u32[]{:S(2)}, u32[]{:S(2)}) collective-permute-start(f32[1,64,128]{2,1,0:T(8,128)S(1)} %get-tuple-element.36), channel_id=1, source_target_pairs={{0,3},{1,2},{2,1},{3,0},{4,7},{5,6},{6,5},{7,4},{8,11},{9,10},{10,... | collective-permute-start | bytes 98312 | tf_op jit(solution)/shard_map/ppermute | solution.py:299
  56.4 0.0 collective-permute-start.13
  56.4 0.0 collective-permute-done.14
  56.4 2.3 %collective-permute-done.15 = f32[1,64,128]{2,1,0:T(8,128)S(1)} collective-permute-done((f32[1,64,128]{2,1,0:T(8,128)S(1)}, f32[1,64,128]{2,1,0:T(8,128)S(1)}, u32[]{:S(2)}, u32[]{:S(2)}) %collective-permute-start.15) | collective-permute-done | bytes 32800 | tf_op jit(solution)/shard_map/ppermute | solution.py:299
  58.7 2.6 %collective-permute-done.13 = f32[1,64,128]{2,1,0:T(8,128)S(1)} collective-permute-done((f32[1,64,128]{2,1,0:T(8,128)S(1)}, f32[1,64,128]{2,1,0:T(8,128)S(1)}, u32[]{:S(2)}, u32[]{:S(2)}) %collective-permute-start.13) | collective-permute-done | bytes 32800 | tf_op jit(solution)/shard_map/ppermute | solution.py:299
  61.2 1.0 collective-permute-start.18
  62.2 0.0 collective-permute-start.17
  62.2 3.5 %collective-permute-start.16 = (f32[1,64,128]{2,1,0:T(8,128)S(1)}, f32[1,64,128]{2,1,0:T(8,128)S(1)}, u32[]{:S(2)}, u32[]{:S(2)}) collective-permute-start(f32[1,64,128]{2,1,0:T(8,128)S(1)} %get-tuple-element.29), channel_id=1, source_target_pairs={{0,2},{1,3},{2,0},{3,1},{4,6},{5,7},{6,4},{7,5},{8,10},{9,11},{10,... | collective-permute-start | bytes 98312 | tf_op jit(solution)/shard_map/ppermute | solution.py:299
  65.7 0.7 collective-permute-start.7
  66.4 0.6 collective-permute-done.18
  67.0 0.0 collective-permute-done.17
  67.0 0.6 collective-permute-done.16
  67.6 0.4 collective-permute-start.21
  68.1 1.2 %collective-permute-start.20 = (f32[4,64,128]{2,1,0:T(8,128)S(1)}, f32[4,64,128]{2,1,0:T(8,128)S(1)}, u32[]{:S(2)}, u32[]{:S(2)}) collective-permute-start(f32[4,64,128]{2,1,0:T(8,128)S(1)} %pad_maximum_fusion), channel_id=1, source_target_pairs={{0,8},{4,12},{8,0},{12,4},{16,24},{20,28},{24,16},{28,20},{1,9},{5... | collective-permute-start | bytes 393224 | tf_op jit(solution)/shard_map/ppermute | solution.py:299
  69.3 1.9 %collective-permute-start.19 = (f32[4,64,128]{2,1,0:T(8,128)S(1)}, f32[4,64,128]{2,1,0:T(8,128)S(1)}, u32[]{:S(2)}, u32[]{:S(2)}) collective-permute-start(f32[4,64,128]{2,1,0:T(8,128)S(1)} %pad_maximum_fusion), channel_id=1, source_target_pairs={{0,16},{4,20},{8,24},{12,28},{16,0},{20,4},{24,8},{28,12},{1,17},{... | collective-permute-start | bytes 393224 | tf_op jit(solution)/shard_map/ppermute | solution.py:299
  71.2 5.5 %collective-permute-done.19 = f32[4,64,128]{2,1,0:T(8,128)S(1)} collective-permute-done((f32[4,64,128]{2,1,0:T(8,128)S(1)}, f32[4,64,128]{2,1,0:T(8,128)S(1)}, u32[]{:S(2)}, u32[]{:S(2)}) %collective-permute-start.19) | collective-permute-done | bytes 131104 | tf_op jit(solution)/shard_map/ppermute | solution.py:299
  76.7 9.1 %collective-permute-done.20 = f32[4,64,128]{2,1,0:T(8,128)S(1)} collective-permute-done((f32[4,64,128]{2,1,0:T(8,128)S(1)}, f32[4,64,128]{2,1,0:T(8,128)S(1)}, u32[]{:S(2)}, u32[]{:S(2)}) %collective-permute-start.20) | collective-permute-done | bytes 131104 | tf_op jit(solution)/shard_map/ppermute | solution.py:299
  85.8 0.0 collective-permute-done.21
  85.9 0.4 collective-permute-start.22
  86.3 0.0 collective-permute-done.7.chip_in
  86.3 0.1 rows.1
  86.4 1.9 %collective-permute-start.8 = (f32[2,256,128]{2,1,0:T(8,128)S(1)}, f32[2,256,128]{2,1,0:T(8,128)S(1)}, u32[]{:S(2)}, u32[]{:S(2)}) collective-permute-start(f32[2,256,128]{2,1,0:T(8,128)S(1)} %get-tuple-element.25), channel_id=1, source_target_pairs={{0,1},{1,2},{2,3},{4,5},{5,6},{6,7},{8,9},{9,10},{10,11},{12,13},{... | collective-permute-start | bytes 786440 | tf_op jit(solution)/shard_map/ppermute | solution.py:295
  88.3 1.3 %collective-permute-start.9 = (f32[2,256,128]{2,1,0:T(8,128)S(1)}, f32[2,256,128]{2,1,0:T(8,128)S(1)}, u32[]{:S(2)}, u32[]{:S(2)}) collective-permute-start(f32[2,256,128]{2,1,0:T(8,128)S(1)} %get-tuple-element.26), channel_id=1, source_target_pairs={{1,0},{2,1},{3,2},{5,4},{6,5},{7,6},{9,8},{10,9},{11,10},{13,12},{... | collective-permute-start | bytes 786440 | tf_op jit(solution)/shard_map/ppermute | solution.py:295
  89.6 4.6 %collective-permute-done.8 = f32[2,256,128]{2,1,0:T(8,128)S(1)} collective-permute-done((f32[2,256,128]{2,1,0:T(8,128)S(1)}, f32[2,256,128]{2,1,0:T(8,128)S(1)}, u32[]{:S(2)}, u32[]{:S(2)}) %collective-permute-start.8) | collective-permute-done | bytes 262176 | tf_op jit(solution)/shard_map/ppermute | solution.py:295
  94.2 4.1 %collective-permute-done.9 = f32[2,256,128]{2,1,0:T(8,128)S(1)} collective-permute-done((f32[2,256,128]{2,1,0:T(8,128)S(1)}, f32[2,256,128]{2,1,0:T(8,128)S(1)}, u32[]{:S(2)}, u32[]{:S(2)}) %collective-permute-start.9) | collective-permute-done | bytes 262176 | tf_op jit(solution)/shard_map/ppermute | solution.py:295
  98.3 0.8 maximum_add_fusion
  99.2 0.0 collective-permute-done.22.other
  99.2 1.7 %join.1 = f32[2,2,256,256]{3,2,1,0:T(8,128)} custom-call(f32[16,64,128]{2,1,0:T(8,128)S(1)} %constant_dynamic-update-slice_fusion.own, f32[16,64,128]{2,1,0:T(8,128)S(1)} %collective-permute-done.22.other), custom_call_target="tpu_custom_call" | custom-call | bytes 2097152 | tf_op jit(solution)/shard_map/join/pallas_call | solution.py:347
  (16 shorter events, 0.1 us)
Async XLA Ops:
  0.6 23.0 %copy-start = (bf16[8,2,256,256]{3,2,1,0:T(8,128)(2,1)S(1)}, bf16[8,2,256,256]{3,2,1,0:T(8,128)(2,1)}, u32[]{:S(2)}) copy-start(bf16[8,2,256,256]{3,2,1,0:T(8,128)(2,1)} %constant.6.clone.tables) | copy-start | bytes 6291460
  0.6 1.2 %copy-start.1 = (f32[2,256,256]{2,1,0:T(8,128)S(1)}, f32[2,256,256]{2,1,0:T(8,128)}, u32[]{:S(2)}) copy-start(f32[2,256,256]{2,1,0:T(8,128)} %center.3) | copy-start | bytes 1572868
  1.8 21.8 %copy-start.2 = (f32[2,256,256]{2,1,0:T(8,128)S(1)}, f32[2,256,256]{2,1,0:T(8,128)}, u32[]{:S(2)}) copy-start(f32[2,256,256]{2,1,0:T(8,128)} %center.3) | copy-start | bytes 1572868
  2.7 10.5 %collective-permute-start = (f32[2,256,128]{2,1,0:T(8,128)S(1)}, f32[2,256,128]{2,1,0:T(8,128)S(1)}, u32[]{:S(2)}, u32[]{:S(2)}) collective-permute-start(f32[2,256,128]{2,1,0:T(8,128)S(1)} %get-tuple-element.15), channel_id=1, source_target_pairs={{0,1},{1,2},{2,3},{4,5},{5,6},{6,7},{8,9},{9,10},{10,11},{12,13},{... | collective-permute-start | bytes 786440 | tf_op jit(solution)/shard_map/ppermute | solution.py:295
  7.6 9.7 %collective-permute-start.1 = (f32[2,256,128]{2,1,0:T(8,128)S(1)}, f32[2,256,128]{2,1,0:T(8,128)S(1)}, u32[]{:S(2)}, u32[]{:S(2)}) collective-permute-start(f32[2,256,128]{2,1,0:T(8,128)S(1)} %get-tuple-element.16), channel_id=1, source_target_pairs={{1,0},{2,1},{3,2},{5,4},{6,5},{7,6},{9,8},{10,9},{11,10},{13,12},{... | collective-permute-start | bytes 786440 | tf_op jit(solution)/shard_map/ppermute | solution.py:295
  8.9 14.6 %collective-permute-start.2 = (f32[2,128,256]{2,1,0:T(8,128)}, f32[2,128,256]{2,1,0:T(8,128)S(1)}, u32[]{:S(2)}, u32[]{:S(2)}) collective-permute-start(f32[2,128,256]{2,1,0:T(8,128)} %get-tuple-element.17), channel_id=1, source_target_pairs={{0,4},{4,0},{8,12},{12,8},{16,20},{20,16},{24,28},{28,24},{1,5},{5... | collective-permute-start | bytes 786440 | tf_op jit(solution)/shard_map/ppermute | solution.py:329
  9.0 14.6 %collective-permute-start.3 = (f32[2,128,256]{2,1,0:T(8,128)}, f32[2,128,256]{2,1,0:T(8,128)}, u32[]{:S(2)}, u32[]{:S(2)}) collective-permute-start(f32[2,128,256]{2,1,0:T(8,128)} %get-tuple-element.18), channel_id=1, source_target_pairs={{4,8},{8,4},{12,16},{16,12},{20,24},{24,20},{5,9},{9,5},{13,17},{1... | collective-permute-start | bytes 786440 | tf_op jit(solution)/shard_map/ppermute | solution.py:329
  18.1 5.5 %collective-permute-start.4 = (f32[2,2,128,128]{3,2,1,0:T(8,128)}, f32[2,2,128,128]{3,2,1,0:T(8,128)}, u32[]{:S(2)}, u32[]{:S(2)}) collective-permute-start(f32[2,2,128,128]{3,2,1,0:T(8,128)} %get-tuple-element.19), channel_id=1, source_target_pairs={{0,4},{4,0},{8,12},{12,8},{16,20},{20,16},{24,28},{28,24},{1,5},{5... | collective-permute-start | bytes 786440 | tf_op jit(solution)/shard_map/ppermute | solution.py:329
  18.1 5.5 %collective-permute-start.5 = (f32[2,2,128,128]{3,2,1,0:T(8,128)}, f32[2,2,128,128]{3,2,1,0:T(8,128)}, u32[]{:S(2)}, u32[]{:S(2)}) collective-permute-start(f32[2,2,128,128]{3,2,1,0:T(8,128)} %get-tuple-element.20), channel_id=1, source_target_pairs={{4,8},{8,4},{12,16},{16,12},{20,24},{24,20},{5,9},{9,5},{13,17},{1... | collective-permute-start | bytes 786440 | tf_op jit(solution)/shard_map/ppermute | solution.py:329
  21.0 1.1 %copy-start.4 = (f32[1,1,3,256,256]{4,3,2,1,0:T(8,128)S(1)}, f32[1,1,3,256,256]{4,3,2,1,0:T(8,128)}, u32[]{:S(2)}) copy-start(f32[1,1,3,256,256]{4,3,2,1,0:T(8,128)} %param.9) | copy-start | bytes 2359300
  22.2 0.9 copy-start.5
  23.6 1.2 %copy-start.3 = (f32[2,2,256,256]{3,2,1,0:T(8,128)S(1)}, f32[2,2,256,256]{3,2,1,0:T(8,128)}, u32[]{:S(2)}) copy-start(f32[2,2,256,256]{3,2,1,0:T(8,128)} %probe.1) | copy-start | bytes 3145732
  32.6 7.8 %collective-permute-start.6 = (f32[2048,128]{1,0:T(8,128)S(1)}, f32[2048,128]{1,0:T(8,128)S(1)}, u32[]{:S(2)}, u32[]{:S(2)}) collective-permute-start(f32[2048,128]{1,0:T(8,128)S(1)} %get-tuple-element.22), channel_id=1, source_target_pairs={{0,4},{4,0},{8,12},{12,8},{16,20},{20,16},{24,28},{28,24},{1,5},{5... | collective-permute-start | bytes 3145736 | tf_op jit(solution)/shard_map/ppermute | solution.py:329
  40.6 6.4 %collective-permute-start.11 = (f32[4,64,128]{2,1,0:T(8,128)S(1)}, f32[4,64,128]{2,1,0:T(8,128)S(1)}, u32[]{:S(2)}, u32[]{:S(2)}) collective-permute-start(f32[4,64,128]{2,1,0:T(8,128)S(1)} %get-tuple-element.32), channel_id=1, source_target_pairs={{0,8},{4,12},{8,0},{12,4},{16,24},{20,28},{24,16},{28,20},{1,9},{5... | collective-permute-start | bytes 393224 | tf_op jit(solution)/shard_map/ppermute | solution.py:299
  40.7 8.0 %collective-permute-start.12 = (f32[4,64,128]{2,1,0:T(8,128)S(1)}, f32[4,64,128]{2,1,0:T(8,128)S(1)}, u32[]{:S(2)}, u32[]{:S(2)}) collective-permute-start(f32[4,64,128]{2,1,0:T(8,128)S(1)} %get-tuple-element.33), channel_id=1, source_target_pairs={{0,24},{4,28},{8,16},{12,20},{16,8},{20,12},{24,0},{28,4},{1,25},{... | collective-permute-start | bytes 393224 | tf_op jit(solution)/shard_map/ppermute | solution.py:299
  42.0 8.4 %collective-permute-start.10 = (f32[4,64,128]{2,1,0:T(8,128)S(1)}, f32[4,64,128]{2,1,0:T(8,128)S(1)}, u32[]{:S(2)}, u32[]{:S(2)}) collective-permute-start(f32[4,64,128]{2,1,0:T(8,128)S(1)} %get-tuple-element.34), channel_id=1, source_target_pairs={{0,16},{4,20},{8,24},{12,28},{16,0},{20,4},{24,8},{28,12},{1,17},{... | collective-permute-start | bytes 393224 | tf_op jit(solution)/shard_map/ppermute | solution.py:299
  50.5 5.9 %collective-permute-start.14 = (f32[1,64,128]{2,1,0:T(8,128)S(1)}, f32[1,64,128]{2,1,0:T(8,128)S(1)}, u32[]{:S(2)}, u32[]{:S(2)}) collective-permute-start(f32[1,64,128]{2,1,0:T(8,128)S(1)} %get-tuple-element.35), channel_id=1, source_target_pairs={{0,1},{1,0},{2,3},{3,2},{4,5},{5,4},{6,7},{7,6},{8,9},{9,8},{10,11... | collective-permute-start | bytes 98312 | tf_op jit(solution)/shard_map/ppermute | solution.py:299
  52.6 6.1 %collective-permute-start.15 = (f32[1,64,128]{2,1,0:T(8,128)S(1)}, f32[1,64,128]{2,1,0:T(8,128)S(1)}, u32[]{:S(2)}, u32[]{:S(2)}) collective-permute-start(f32[1,64,128]{2,1,0:T(8,128)S(1)} %get-tuple-element.36), channel_id=1, source_target_pairs={{0,3},{1,2},{2,1},{3,0},{4,7},{5,6},{6,5},{7,4},{8,11},{9,10},{10,... | collective-permute-start | bytes 98312 | tf_op jit(solution)/shard_map/ppermute | solution.py:299
  56.4 4.8 %collective-permute-start.13 = (f32[1,64,128]{2,1,0:T(8,128)S(1)}, f32[1,64,128]{2,1,0:T(8,128)S(1)}, u32[]{:S(2)}, u32[]{:S(2)}) collective-permute-start(f32[1,64,128]{2,1,0:T(8,128)S(1)} %get-tuple-element.37), channel_id=1, source_target_pairs={{0,2},{1,3},{2,0},{3,1},{4,6},{5,7},{6,4},{7,5},{8,10},{9,11},{10,... | collective-permute-start | bytes 98312 | tf_op jit(solution)/shard_map/ppermute | solution.py:299
  61.2 5.8 %collective-permute-start.18 = (f32[1,64,128]{2,1,0:T(8,128)S(1)}, f32[1,64,128]{2,1,0:T(8,128)S(1)}, u32[]{:S(2)}, u32[]{:S(2)}) collective-permute-start(f32[1,64,128]{2,1,0:T(8,128)S(1)} %get-tuple-element.29), channel_id=1, source_target_pairs={{0,3},{1,2},{2,1},{3,0},{4,7},{5,6},{6,5},{7,4},{8,11},{9,10},{10,... | collective-permute-start | bytes 98312 | tf_op jit(solution)/shard_map/ppermute | solution.py:299
  62.2 4.8 %collective-permute-start.17 = (f32[1,64,128]{2,1,0:T(8,128)S(1)}, f32[1,64,128]{2,1,0:T(8,128)S(1)}, u32[]{:S(2)}, u32[]{:S(2)}) collective-permute-start(f32[1,64,128]{2,1,0:T(8,128)S(1)} %get-tuple-element.29), channel_id=1, source_target_pairs={{0,1},{1,0},{2,3},{3,2},{4,5},{5,4},{6,7},{7,6},{8,9},{9,8},{10,11... | collective-permute-start | bytes 98312 | tf_op jit(solution)/shard_map/ppermute | solution.py:299
  62.2 5.4 %collective-permute-start.16 = (f32[1,64,128]{2,1,0:T(8,128)S(1)}, f32[1,64,128]{2,1,0:T(8,128)S(1)}, u32[]{:S(2)}, u32[]{:S(2)}) collective-permute-start(f32[1,64,128]{2,1,0:T(8,128)S(1)} %get-tuple-element.29), channel_id=1, source_target_pairs={{0,2},{1,3},{2,0},{3,1},{4,6},{5,7},{6,4},{7,5},{8,10},{9,11},{10,... | collective-permute-start | bytes 98312 | tf_op jit(solution)/shard_map/ppermute | solution.py:299
  65.7 20.6 %collective-permute-start.7 = (f32[1024,128]{1,0:T(8,128)S(1)}, f32[1024,128]{1,0:T(8,128)S(1)}, u32[]{:S(2)}, u32[]{:S(2)}) collective-permute-start(f32[1024,128]{1,0:T(8,128)S(1)} %get-tuple-element.23), channel_id=1, source_target_pairs={{4,8},{8,4},{12,16},{16,12},{20,24},{24,20},{5,9},{9,5},{13,17},{1... | collective-permute-start | bytes 1572872 | tf_op jit(solution)/shard_map/ppermute | solution.py:329
  67.6 18.2 %collective-permute-start.21 = (f32[4,64,128]{2,1,0:T(8,128)S(1)}, f32[4,64,128]{2,1,0:T(8,128)S(1)}, u32[]{:S(2)}, u32[]{:S(2)}) collective-permute-start(f32[4,64,128]{2,1,0:T(8,128)S(1)} %pad_maximum_fusion), channel_id=1, source_target_pairs={{0,24},{4,28},{8,16},{12,20},{16,8},{20,12},{24,0},{28,4},{1,25},{... | collective-permute-start | bytes 393224 | tf_op jit(solution)/shard_map/ppermute | solution.py:299
  68.1 17.8 %collective-permute-start.20 = (f32[4,64,128]{2,1,0:T(8,128)S(1)}, f32[4,64,128]{2,1,0:T(8,128)S(1)}, u32[]{:S(2)}, u32[]{:S(2)}) collective-permute-start(f32[4,64,128]{2,1,0:T(8,128)S(1)} %pad_maximum_fusion), channel_id=1, source_target_pairs={{0,8},{4,12},{8,0},{12,4},{16,24},{20,28},{24,16},{28,20},{1,9},{5... | collective-permute-start | bytes 393224 | tf_op jit(solution)/shard_map/ppermute | solution.py:299
  69.3 7.4 %collective-permute-start.19 = (f32[4,64,128]{2,1,0:T(8,128)S(1)}, f32[4,64,128]{2,1,0:T(8,128)S(1)}, u32[]{:S(2)}, u32[]{:S(2)}) collective-permute-start(f32[4,64,128]{2,1,0:T(8,128)S(1)} %pad_maximum_fusion), channel_id=1, source_target_pairs={{0,16},{4,20},{8,24},{12,28},{16,0},{20,4},{24,8},{28,12},{1,17},{... | collective-permute-start | bytes 393224 | tf_op jit(solution)/shard_map/ppermute | solution.py:299
  85.9 13.3 %collective-permute-start.22 = (f32[16,64,128]{2,1,0:T(8,128)S(1)}, f32[16,64,128]{2,1,0:T(8,128)S(1)}, u32[]{:S(2)}, u32[]{:S(2)}) collective-permute-start(f32[16,64,128]{2,1,0:T(8,128)S(1)} %constant_dynamic-update-slice_fusion.own), channel_id=1, source_target_pairs={{0,4},{4,0},{8,12},{12,8},{16,20},{20,16},{24,28},{28,24},{1,5},{5... | collective-permute-start | bytes 1572872 | tf_op jit(solution)/shard_map/ppermute | solution.py:329
  86.4 7.8 %collective-permute-start.8 = (f32[2,256,128]{2,1,0:T(8,128)S(1)}, f32[2,256,128]{2,1,0:T(8,128)S(1)}, u32[]{:S(2)}, u32[]{:S(2)}) collective-permute-start(f32[2,256,128]{2,1,0:T(8,128)S(1)} %get-tuple-element.25), channel_id=1, source_target_pairs={{0,1},{1,2},{2,3},{4,5},{5,6},{6,7},{8,9},{9,10},{10,11},{12,13},{... | collective-permute-start | bytes 786440 | tf_op jit(solution)/shard_map/ppermute | solution.py:295
  88.3 10.0 %collective-permute-start.9 = (f32[2,256,128]{2,1,0:T(8,128)S(1)}, f32[2,256,128]{2,1,0:T(8,128)S(1)}, u32[]{:S(2)}, u32[]{:S(2)}) collective-permute-start(f32[2,256,128]{2,1,0:T(8,128)S(1)} %get-tuple-element.26), channel_id=1, source_target_pairs={{1,0},{2,1},{3,2},{5,4},{6,5},{7,6},{9,8},{10,9},{11,10},{13,12},{... | collective-permute-start | bytes 786440 | tf_op jit(solution)/shard_map/ppermute | solution.py:295

commit v3 on v2

--- a/solution.py
+++ b/solution.py
@@ -14,6 +14,7 @@
 LANES = 128
 CHUNK = 32
 VMEM_LIMIT = 28 * 1024 * 1024
+MIDDLE_LIMIT = 12 * 1024 * 1024
 SMALL_LIMIT = 8 * 1024 * 1024
 
 
@@ -56,39 +57,49 @@
     return jnp.dot(a, b, preferred_element_type=jnp.float32)
 
 
-def edges_kernel(center, to_right, to_left, to_core, to_chip):
-    half = LANES
-    to_right[...] = center[:, :, half:]
-    to_left[...] = center[:, :, :half]
-    odd = lax.axis_index("ty") % 2
-    near = pl.multiple_of((1 - odd) * half, half)
-    far = pl.multiple_of(odd * half, half)
-    to_core[...] = center[:, pl.ds(near, half), :]
-    to_chip[...] = center[:, pl.ds(far, half), :]
-
-
-def corners_kernel(left, right, to_core, to_chip):
+def edges_kernel(center, kept, to_right, to_left, to_core, to_chip, core_right, core_left, chip_right, chip_left, sems):
     half = LANES
     odd = lax.axis_index("ty") % 2
-    near = pl.multiple_of((1 - odd) * half, half)
-    far = pl.multiple_of(odd * half, half)
-    for side, cols in enumerate((left, right)):
-        to_core[side] = cols[:, pl.ds(near, half), :]
-        to_chip[side] = cols[:, pl.ds(far, half), :]
-
-
-def root_kernel(measured, order, root, halves):
+    near = pl.ds(pl.multiple_of((1 - odd) * half, half), half)
+    far = pl.ds(pl.multiple_of(odd * half, half), half)
+    low, high = pl.ds(0, half), pl.ds(half, half)
+    moves = (
+        (center.at[:, :, high], to_right),
+        (center.at[:, :, low], to_left),
+        (center.at[:, near, :], to_core),
+        (center.at[:, far, :], to_chip),
+        (center.at[:, near, high], core_right),
+        (center.at[:, near, low], core_left),
+        (center.at[:, far, high], chip_right),
+        (center.at[:, far, low], chip_left),
+        (center, kept),
+    )
+    copies = [pltpu.make_async_copy(source, target, sems.at[i]) for i, (source, target) in enumerate(moves)]
+    for copy in copies:
+        copy.start()
+    for copy in copies:
+        copy.wait()
+
+
+def prepare_kernel(measured, probe, order, root, probe_kept, held, halves, sems):
+    first = pltpu.make_async_copy(measured, held, sems.at[0])
+    second = pltpu.make_async_copy(probe, probe_kept, sems.at[1])
+    first.start()
+    second.start()
+    first.wait()
     for slot in range(measured.shape[0]):
         for b in range(2):
-            halves[slot, b] = jnp.sqrt(measured[slot, :, b * LANES : (b + 1) * LANES])
+            halves[slot, b] = jnp.sqrt(held[slot, :, b * LANES : (b + 1) * LANES])
         for parity in range(2):
             rows = pl.ds(parity, LANES, stride=2)
             high, low = split(jnp.concatenate([halves[slot, 0, rows, :], halves[slot, 1, rows, :]], axis=1))
             root[slot, parity] = mul(high, order[...]) + mul(low, order[...])
+    second.wait()
 
 
 def slots_kernel(
-    counts, spots, center, left, right, core_rows, chip_rows, core_corners, chip_corners, probe, root, tables,
+    counts, spots, center, left, right, core_rows, chip_rows,
+    core_from_left, core_from_right, chip_from_left, chip_from_right, probe, root, tables,
     core_out, chip_out, grad_mid, probe_keep,
     pad, grid, patch, rows_high, rows_low, freq, sums,
 ):
@@ -105,16 +116,19 @@
     for b in range(2):
         cols = slice(b * half, (b + 1) * half)
         pad[:, 1 + b, margin : margin + length, :] = center[:, :, cols]
-        for start, rows, corners in ((near, core_rows, core_corners), (far, chip_rows, chip_corners)):
-            pad[:, 1 + b, pl.ds(start, margin), :] = rows[:, :, cols]
-            pad[:, 3 * b, pl.ds(start, margin), :] = corners[b]
+        pad[:, 1 + b, pl.ds(near, margin), :] = core_rows[:, :, cols]
+        pad[:, 1 + b, pl.ds(far, margin), :] = chip_rows[:, :, cols]
+    pad[:, 0, pl.ds(near, margin), :] = core_from_left[...]
+    pad[:, 3, pl.ds(near, margin), :] = core_from_right[...]
+    pad[:, 0, pl.ds(far, margin), :] = chip_from_left[...]
+    pad[:, 3, pl.ds(far, margin), :] = chip_from_right[...]
     grid[...] = jnp.zeros_like(grid)
     sums[...] = jnp.zeros_like(sums)
     lane = lax.broadcasted_iota(jnp.int32, (CHUNK, half), 1)
 
     def slot_step(slot, carry):
-        row0 = spots[slot, 0]
-        col0 = spots[slot, 1]
+        row0 = spots[0, slot]
+        col0 = spots[1, slot]
         block = jnp.minimum(col0 // half, 1)
         shift = col0 - block * half
         back_shift = lax.rem(half - shift, half)
@@ -226,7 +240,7 @@
                         grid[c, block + b, pl.ds(row0 + rows, CHUNK), :] += placed[b]
         return carry
 
-    listed = counts[lax.axis_index("ty"), lax.axis_index("tx")]
+    listed = counts[lax.axis_index("tx"), lax.axis_index("ty")]
     lax.fori_loop(0, listed, slot_step, 0)
 
     grad_mid[...] = grid[:, :, margin : margin + length, :]
@@ -251,7 +265,7 @@
     lax.fori_loop(0, kept, place_piece, 0)
 
 
-def rows_kernel(grad_mid, core_in, chip_in, to_left, to_right, inner):
+def rows_kernel(grad_mid, core_in, chip_in, own, one, two, three, to_left, to_right, inner, joined):
     half = LANES
     odd = lax.axis_index("ty") % 2
     for c in range(2):
@@ -267,6 +281,20 @@
                     to_right[c, rows, :] = value
                 else:
                     inner[c, rows, (b - 1) * half : b * half] = value
+    join_pieces((own, one, two, three), joined)
+
+
+def columns_kernel(inner, from_left, from_right, own, one, two, three, grad, joined):
+    half = LANES
+    grad[:, :, :half] = inner[:, :, :half] + from_left[...]
+    grad[:, :, half:] = inner[:, :, half:] + from_right[...]
+    join_pieces((own, one, two, three), joined)
+
+
+def join_pieces(pieces, joined):
+    count = pieces[0].shape[0]
+    for i, piece in enumerate(pieces):
+        joined[i * count : (i + 1) * count] = piece[...]
 
 
 def join_kernel(own, other, out):
@@ -329,6 +357,17 @@
     return lax.ppermute(value, "ty", pairs)
 
 
+def cornered(value, mask_of, steps):
+    rows, cols = lax.axis_size("ty"), lax.axis_size("tx")
+    pairs = []
+    for a in range(rows):
+        other = a ^ 1 if mask_of == "core" else a + 1 if a % 2 else a - 1
+        for b in range(cols):
+            if 0 <= other < rows and 0 <= b + steps < cols:
+                pairs.append((a * cols + b, other * cols + b + steps))
+    return lax.ppermute(value, ("ty", "tx"), pairs)
+
+
 def reduce_step(value, axis, bits):
     places = masks(bits)
     count = value.shape[0] // len(places)
@@ -336,19 +375,19 @@
     return value[:count] + sum(taken[1:], taken[0])
 
 
-def gather_step(value, axis, bits):
-    return jnp.concatenate([value] + [exchanged(value, axis, mask) for mask in masks(bits)[1:]], axis=0)
-
-
-def call(body, name, out, operands, scalars=0, scratch=(), limit=SMALL_LIMIT):
-    vmem = pl.BlockSpec(memory_space=pltpu.VMEM)
-    smem = pl.BlockSpec(memory_space=pltpu.SMEM)
-    moved = sum(math.prod(v.shape) * v.dtype.itemsize for v in operands + tuple(out))
+def gathered(value, axis, bits):
+    return [value] + [exchanged(value, axis, mask) for mask in masks(bits)[1:]]
+
+
+def call(body, name, out, operands, spaces="", scratch=(), limit=SMALL_LIMIT):
+    kinds = {"v": pltpu.VMEM, "s": pltpu.SMEM, "a": pl.ANY}
+    spaces = spaces + "v" * (len(operands) - len(spaces))
+    moved = sum(math.prod(v.shape) * v.dtype.itemsize for v in tuple(operands) + tuple(out))
     return pl.pallas_call(
         body,
         out_shape=tuple(out),
-        in_specs=[smem] * scalars + [vmem] * (len(operands) - scalars),
-        out_specs=(vmem,) * len(out),
+        in_specs=[pl.BlockSpec(memory_space=kinds[space]) for space in spaces],
+        out_specs=(pl.BlockSpec(memory_space=pltpu.VMEM),) * len(out),
         scratch_shapes=list(scratch),
         compiler_params=pltpu.CompilerParams(vmem_limit_bytes=limit),
         cost_estimate=pl.CostEstimate(flops=0, bytes_accessed=moved, transcendentals=0),
@@ -371,23 +410,37 @@
     def shape(*sizes):
         return jax.ShapeDtypeStruct(sizes, f32)
 
-    to_right, to_left, to_core, to_chip = call(
-        edges_kernel, "edges", [shape(2, length, margin)] * 2 + [shape(2, margin, length)] * 2, (object_field,)
+    center, to_right, to_left, to_core, to_chip, core_right, core_left, chip_right, chip_left = call(
+        edges_kernel,
+        "edges",
+        [shape(2, length, length)] + [shape(2, length, margin)] * 2 + [shape(2, margin, length)] * 2 + [shape(2, margin, margin)] * 4,
+        (object_field,),
+        "a",
+        scratch=(pltpu.SemaphoreType.DMA((9,)),),
     )
     left = shifted(to_right, "tx", 1)
     right = shifted(to_left, "tx", -1)
+    core_rows = paired(to_core, "core")
     chip_rows = paired(to_chip, "chip")
-    core_rows = paired(to_core, "core")
-    (root,) = call(
-        root_kernel,
-        "root",
-        [shape(slots, 2, half, pattern)],
-        (intensities[0, 0], order),
-        scratch=(pltpu.VMEM((slots, 2, pattern, half), f32),),
+    corners = [
+        cornered(core_right, "core", 1),
+        cornered(core_left, "core", -1),
+        cornered(chip_right, "chip", 1),
+        cornered(chip_left, "chip", -1),
+    ]
+    root, probe = call(
+        prepare_kernel,
+        "prepare",
+        [shape(slots, 2, half, pattern), shape(*probe_modes.shape)],
+        (intensities[0, 0], probe_modes, order),
+        "aa",
+        scratch=(
+            pltpu.VMEM((slots, pattern, pattern), f32),
+            pltpu.VMEM((slots, 2, pattern, half), f32),
+            pltpu.SemaphoreType.DMA((2,)),
+        ),
+        limit=MIDDLE_LIMIT,
     )
-    to_core, to_chip = call(corners_kernel, "corners", [shape(2, 2, margin, margin)] * 2, (left, right))
-    chip_corners = paired(to_chip, "chip")
-    core_corners = paired(to_core, "core")
 
     rows = 2 * 2 * modes * pattern // devices
     kept = devices // 2
@@ -396,8 +449,8 @@
         slots_kernel,
         "slots",
         [shape(border + kept * rows, half), shape(border, half), shape(2, 4, length, half), shape(kept, rows, half)],
-        (counts, offsets[0, 0], object_field, left, right, core_rows, chip_rows, core_corners, chip_corners, probe_modes, root, tables),
-        scalars=2,
+        (counts.T, offsets[0, 0].T, center, left, right, core_rows, chip_rows, *corners, probe, root, tables),
+        "ss",
         scratch=(
             pltpu.VMEM((2, 4, length + 2 * margin, half), f32),
             pltpu.VMEM((2, 4, length + 2 * margin, half), f32),
@@ -413,18 +466,31 @@
     core_in = paired(core_out, "core")
     chip_in = paired(chip_out, "chip")
     value = probe_keep + core_in[border:].reshape(probe_keep.shape)
-    to_left, to_right, inner = call(
-        rows_kernel, "rows", [shape(2, length, half)] * 2 + [shape(2, length, length)], (grad_mid, core_in[:border], chip_in)
-    )
-    from_right = shifted(to_left, "tx", -1)
-    from_left = shifted(to_right, "tx", 1)
-    inner = inner + jnp.concatenate([from_left, from_right], axis=2)
-
     for axis, bits in groups[1:]:
         value = reduce_step(value, axis, bits)
     value = value * (1.0 / devices)
-    for axis, bits in reversed(groups[1:]):
-        value = gather_step(value, axis, bits)
+    last = len(groups) - 1
+    for i in range(last, 0, -1):
+        pieces = gathered(value, *groups[i])
+        joined = shape(len(pieces) * value.shape[0], rows, half)
+        if i == last:
+            assert len(pieces) == 4
+            to_left, to_right, inner, value = call(
+                rows_kernel,
+                "rows",
+                [shape(2, length, half)] * 2 + [shape(2, length, length), joined],
+                (grad_mid, core_in[:border], chip_in, *pieces),
+            )
+            from_right = shifted(to_left, "tx", -1)
+            from_left = shifted(to_right, "tx", 1)
+        elif i == 1 and len(pieces) == 4:
+            inner, value = call(
+                columns_kernel, "columns", [shape(2, length, length), joined], (inner, from_left, from_right, *pieces)
+            )
+        else:
+            value = jnp.concatenate(pieces, axis=0)
+    if len(groups) < 3 or len(groups[1][1]) != 2:
+        inner = inner + jnp.concatenate([from_left, from_right], axis=2)
     other = paired(value, "core")
     (probe_grad,) = call(join_kernel, "join", [shape(*probe_modes.shape)], (value, other))
     return (inner, probe_grad)

time: 101 us -> 91.9 us (0.910)
  waiting for transfers between devices: 44.8 us -> 23.8 us
  starting transfers between devices: 36.4 us -> 52.8 us
  Pallas kernels: 11.8 us -> 7.93 us
    ppermute x4, waiting for transfers between devices: 15.6 us -> 0.01 us  [shifted(): lax.ppermute(value, axis, [(source, source + steps) for source in range(i...]
    ppermute x12, waiting for transfers between devices: 26.9 us -> 19.6 us  [exchanged(): lax.ppermute(value, axis, [(i, i ^ mask) for i in range(lax.axis_size(axi...]
    ppermute x0 -> x4, starting transfers between devices: none -> 7 us  [cornered(): return lax.ppermute(value, ('ty', 'tx'), pairs)]
    ppermute x12, starting transfers between devices: 17.5 us -> 22.1 us  [exchanged(): lax.ppermute(value, axis, [(i, i ^ mask) for i in range(lax.axis_size(axi...]
    pallas_call x6, Pallas kernels: 11.8 us -> 7.93 us  [call(): pl.pallas_call(body, out_shape=tuple(out), in_specs=[pl.BlockSpec(memory_...]
    ppermute x7 -> x5, starting transfers between devices: 9.45 us -> 12.3 us  [paired(): return lax.ppermute(value, 'ty', pairs)]
    ppermute x4, starting transfers between devices: 9.44 us -> 11.4 us  [shifted(): lax.ppermute(value, axis, [(source, source + steps) for source in range(i...]
    ppermute x7 -> x5, waiting for transfers between devices: 2.3 us -> 4.2 us  [paired(): return lax.ppermute(value, 'ty', pairs)]
  transfers between devices with their start and end apart: 23 -> 25, of which waited for: 14 -> 13; matrix products, arithmetic and copies ran while one was open for 2% -> 0% of each run, Pallas kernels for 1% -> 1%
where the time goes in v3:
time: 91.9 us; the launch traced here: 91.4 us
  starting transfers between devices  52.8 us (57%)
  waiting for transfers between devices  23.8 us (26%)
  Pallas kernels  7.93 us (9%)
  local copies, waits for them, and re-layouts  5.91 us (6%)
    ppermute x12, starting transfers between devices, exchanged(): lax.ppermute(value, axis, [(i, i ^ mask) for i in range(lax.axis_size(axi...  22.1 us
    ppermute x12, waiting for transfers between devices, exchanged(): lax.ppermute(value, axis, [(i, i ^ mask) for i in range(lax.axis_size(axi...  19.6 us
    ppermute x5, starting transfers between devices, paired(): return lax.ppermute(value, 'ty', pairs)  12.3 us
    ppermute x4, starting transfers between devices, shifted(): lax.ppermute(value, axis, [(source, source + steps) for source in range(i...  11.4 us
    pallas_call x6, Pallas kernels, call(): pl.pallas_call(body, out_shape=tuple(out), in_specs=[pl.BlockSpec(memory_...  7.93 us
    ppermute x4, starting transfers between devices, cornered(): return lax.ppermute(value, ('ty', 'tx'), pairs)  7 us
    unnamed x14, local copies, waits for them, and re-layouts  5.8 us
    ppermute x5, waiting for transfers between devices, paired(): return lax.ppermute(value, 'ty', pairs)  4.2 us
  transfers between devices with their start and end apart: 25, of which 13 were waited for; matrix products, arithmetic and copies ran while one was open for 0% of the time, Pallas kernels for 1%

profile of v3, /device:TPU:0, one launch (start us, length us, event | category | flops | bytes accessed | tf_op | source)
XLA Modules:
  0.0 91.4 jit_solution(2903023834190282471)
XLA Ops:
  0.6 0.0 copy-start
  0.7 1.2 %copy-done.3 = f32[2,256,256]{2,1,0:T(8,128)S(1)} copy-done((f32[2,256,256]{2,1,0:T(8,128)S(1)}, f32[2,256,256]{2,1,0:T(8,128)}, u32[]{:S(2)}) %copy-start.3) | copy-done | bytes 524312
  1.8 0.2 edges.1
  2.1 4.4 %collective-permute-start.4 = (f32[2,128,128]{2,1,0:T(8,128)S(1)}, f32[2,128,128]{2,1,0:T(8,128)S(1)}, u32[]{:S(2)}, u32[]{:S(2)}) collective-permute-start(f32[2,128,128]{2,1,0:T(8,128)S(1)} %get-tuple-element.28), channel_id=1, source_target_pairs={{0,5},{1,6},{2,7},{4,1},{5,2},{6,3},{8,13},{9,14},{10,15},{12,9},{... | collective-permute-start | bytes 393224 | tf_op jit(solution)/shard_map/ppermute | solution.py:368
  6.5 1.3 %collective-permute-start.5 = (f32[2,128,128]{2,1,0:T(8,128)S(1)}, f32[2,128,128]{2,1,0:T(8,128)S(1)}, u32[]{:S(2)}, u32[]{:S(2)}) collective-permute-start(f32[2,128,128]{2,1,0:T(8,128)S(1)} %get-tuple-element.29), channel_id=1, source_target_pairs={{1,4},{2,5},{3,6},{5,0},{6,1},{7,2},{9,12},{10,13},{11,14},{13,8},... | collective-permute-start | bytes 393224 | tf_op jit(solution)/shard_map/ppermute | solution.py:368
  7.8 0.7 collective-permute-start.6
  8.4 4.8 %collective-permute-start = (f32[2,256,128]{2,1,0:T(8,128)S(1)}, f32[2,256,128]{2,1,0:T(8,128)S(1)}, u32[]{:S(2)}, u32[]{:S(2)}) collective-permute-start(f32[2,256,128]{2,1,0:T(8,128)S(1)} %get-tuple-element.24), channel_id=1, source_target_pairs={{0,1},{1,2},{2,3},{4,5},{5,6},{6,7},{8,9},{9,10},{10,11},{12,13},{... | collective-permute-start | bytes 786440 | tf_op jit(solution)/shard_map/ppermute | solution.py:323
  13.3 1.3 %collective-permute-start.1 = (f32[2,256,128]{2,1,0:T(8,128)S(1)}, f32[2,256,128]{2,1,0:T(8,128)S(1)}, u32[]{:S(2)}, u32[]{:S(2)}) collective-permute-start(f32[2,256,128]{2,1,0:T(8,128)S(1)} %get-tuple-element.25), channel_id=1, source_target_pairs={{1,0},{2,1},{3,2},{5,4},{6,5},{7,6},{9,8},{10,9},{11,10},{13,12},{... | collective-permute-start | bytes 786440 | tf_op jit(solution)/shard_map/ppermute | solution.py:323
  14.6 0.0 collective-permute-done.4.core_from_left
  14.6 3.6 %collective-permute-start.2 = (f32[2,128,256]{2,1,0:T(8,128)S(1)}, f32[2,128,256]{2,1,0:T(8,128)S(1)}, u32[]{:S(2)}, u32[]{:S(2)}) collective-permute-start(f32[2,128,256]{2,1,0:T(8,128)S(1)} %get-tuple-element.26), channel_id=1, source_target_pairs={{0,4},{4,0},{8,12},{12,8},{16,20},{20,16},{24,28},{28,24},{1,5},{5... | collective-permute-start | bytes 786440 | tf_op jit(solution)/shard_map/ppermute | solution.py:357
  18.2 0.0 collective-permute-done.5.core_from_right
  18.2 0.7 collective-permute-start.3
  18.9 0.0 collective-permute-done.6.chip_from_left
  18.9 0.7 collective-permute-start.7
  19.6 0.0 copy-start.1
  19.6 1.2 %copy-done.1 = f32[2,2,256,256]{3,2,1,0:T(8,128)S(1)} copy-done((f32[2,2,256,256]{3,2,1,0:T(8,128)S(1)}, f32[2,2,256,256]{3,2,1,0:T(8,128)}, u32[]{:S(2)}) %copy-start.1) | copy-done | bytes 1048600
  20.8 1.1 %copy-done.2 = f32[1,1,3,256,256]{4,3,2,1,0:T(8,128)S(1)} copy-done((f32[1,1,3,256,256]{4,3,2,1,0:T(8,128)S(1)}, f32[1,1,3,256,256]{4,3,2,1,0:T(8,128)}, u32[]{:S(2)}) %copy-start.2) | copy-done | bytes 786456
  22.0 0.9 copy-done.4
  22.9 0.7 prepare.1
  23.6 0.0 collective-permute-done.7.chip_from_right
  23.6 0.0 collective-permute-done.left
  23.6 0.0 collective-permute-done.1.right
  23.6 0.0 collective-permute-done.2.core_rows
  23.6 0.0 collective-permute-done.3.chip_rows
  23.6 0.0 copy-start.5
  23.7 0.7 copy-done.5
  24.3 0.7 copy-done.6
  25.0 4.3 %slots.1 = (f32[2048,128]{1,0:T(8,128)S(1)}, f32[1024,128]{1,0:T(8,128)S(1)}, f32[2,4,256,128]{3,2,1,0:T(8,128)S(1)}, f32[16,64,128]{2,1,0:T(8,128)S(1)}) custom-call(s32[4,8]{1,0:T(4,128)S(1)} %bitcast.7, s32[2,3]{1,0:T(2,128)S(1)} %bitcast.8, f32[2,256,256]{2,1,0:T(8,128)S(1)} %get-tuple-element.23.center, f32[2,256,128]{2,1,0:T(8,128)S(1)} %collective-permute-done.left, ...), custom_call_target="tpu_custom_call" | custom-call | bytes 9175192 | tf_op jit(solution)/shard_map/slots/pallas_call | solution.py:386
  29.3 7.3 %collective-permute-start.8 = (f32[2048,128]{1,0:T(8,128)S(1)}, f32[2048,128]{1,0:T(8,128)S(1)}, u32[]{:S(2)}, u32[]{:S(2)}) collective-permute-start(f32[2048,128]{1,0:T(8,128)S(1)} %get-tuple-element.35), channel_id=1, source_target_pairs={{0,4},{4,0},{8,12},{12,8},{16,20},{20,16},{24,28},{28,24},{1,5},{5... | collective-permute-start | bytes 3145736 | tf_op jit(solution)/shard_map/ppermute | solution.py:357
  36.6 2.3 %collective-permute-done.8 = f32[2048,128]{1,0:T(8,128)S(1)} collective-permute-done((f32[2048,128]{1,0:T(8,128)S(1)}, f32[2048,128]{1,0:T(8,128)S(1)}, u32[]{:S(2)}, u32[]{:S(2)}) %collective-permute-start.8) | collective-permute-done | bytes 1048608 | tf_op jit(solution)/shard_map/ppermute | solution.py:357
  38.9 0.1 fusion.1
  39.0 0.1 add.21
  39.1 1.8 %collective-permute-start.11 = (f32[4,64,128]{2,1,0:T(8,128)S(1)}, f32[4,64,128]{2,1,0:T(8,128)S(1)}, u32[]{:S(2)}, u32[]{:S(2)}) collective-permute-start(f32[4,64,128]{2,1,0:T(8,128)S(1)} %get-tuple-element.46), channel_id=1, source_target_pairs={{0,8},{4,12},{8,0},{12,4},{16,24},{20,28},{24,16},{28,20},{1,9},{5... | collective-permute-start | bytes 393224 | tf_op jit(solution)/shard_map/ppermute | solution.py:327
  40.9 2.4 %collective-permute-start.12 = (f32[4,64,128]{2,1,0:T(8,128)S(1)}, f32[4,64,128]{2,1,0:T(8,128)S(1)}, u32[]{:S(2)}, u32[]{:S(2)}) collective-permute-start(f32[4,64,128]{2,1,0:T(8,128)S(1)} %get-tuple-element.47), channel_id=1, source_target_pairs={{0,24},{4,28},{8,16},{12,20},{16,8},{20,12},{24,0},{28,4},{1,25},{... | collective-permute-start | bytes 393224 | tf_op jit(solution)/shard_map/ppermute | solution.py:327
  43.3 0.7 collective-permute-start.9
  44.0 1.5 %collective-permute-done.11 = f32[4,64,128]{2,1,0:T(8,128)S(1)} collective-permute-done((f32[4,64,128]{2,1,0:T(8,128)S(1)}, f32[4,64,128]{2,1,0:T(8,128)S(1)}, u32[]{:S(2)}, u32[]{:S(2)}) %collective-permute-start.11) | collective-permute-done | bytes 131104 | tf_op jit(solution)/shard_map/ppermute | solution.py:327
  45.5 4.3 %collective-permute-done.12 = f32[4,64,128]{2,1,0:T(8,128)S(1)} collective-permute-done((f32[4,64,128]{2,1,0:T(8,128)S(1)}, f32[4,64,128]{2,1,0:T(8,128)S(1)}, u32[]{:S(2)}, u32[]{:S(2)}) %collective-permute-start.12) | collective-permute-done | bytes 131104 | tf_op jit(solution)/shard_map/ppermute | solution.py:327
  49.7 1.4 %collective-permute-done.10 = f32[4,64,128]{2,1,0:T(8,128)S(1)} collective-permute-done((f32[4,64,128]{2,1,0:T(8,128)S(1)}, f32[4,64,128]{2,1,0:T(8,128)S(1)}, u32[]{:S(2)}, u32[]{:S(2)}) %collective-permute-start.10) | collective-permute-done | bytes 131104 | tf_op jit(solution)/shard_map/ppermute | solution.py:327
  51.2 7.7 %collective-permute-start.14 = (f32[1,64,128]{2,1,0:T(8,128)S(1)}, f32[1,64,128]{2,1,0:T(8,128)S(1)}, u32[]{:S(2)}, u32[]{:S(2)}) collective-permute-start(f32[1,64,128]{2,1,0:T(8,128)S(1)} %get-tuple-element.49), channel_id=1, source_target_pairs={{0,1},{1,0},{2,3},{3,2},{4,5},{5,4},{6,7},{7,6},{8,9},{9,8},{10,11... | collective-permute-start | bytes 98312 | tf_op jit(solution)/shard_map/ppermute | solution.py:327
  58.9 0.3 collective-permute-start.15
  59.1 1.3 %collective-permute-start.13 = (f32[1,64,128]{2,1,0:T(8,128)S(1)}, f32[1,64,128]{2,1,0:T(8,128)S(1)}, u32[]{:S(2)}, u32[]{:S(2)}) collective-permute-start(f32[1,64,128]{2,1,0:T(8,128)S(1)} %get-tuple-element.51), channel_id=1, source_target_pairs={{0,2},{1,3},{2,0},{3,1},{4,6},{5,7},{6,4},{7,5},{8,10},{9,11},{10,... | collective-permute-start | bytes 98312 | tf_op jit(solution)/shard_map/ppermute | solution.py:327
  60.4 0.4 collective-permute-done.14
  60.8 3.8 %collective-permute-done.15 = f32[1,64,128]{2,1,0:T(8,128)S(1)} collective-permute-done((f32[1,64,128]{2,1,0:T(8,128)S(1)}, f32[1,64,128]{2,1,0:T(8,128)S(1)}, u32[]{:S(2)}, u32[]{:S(2)}) %collective-permute-start.15) | collective-permute-done | bytes 32800 | tf_op jit(solution)/shard_map/ppermute | solution.py:327
  64.6 0.0 collective-permute-done.13
  64.6 3.0 %collective-permute-start.18 = (f32[1,64,128]{2,1,0:T(8,128)S(1)}, f32[1,64,128]{2,1,0:T(8,128)S(1)}, u32[]{:S(2)}, u32[]{:S(2)}) collective-permute-start(f32[1,64,128]{2,1,0:T(8,128)S(1)} %fusion.own), channel_id=1, source_target_pairs={{0,3},{1,2},{2,1},{3,0},{4,7},{5,6},{6,5},{7,4},{8,11},{9,10},{10,... | collective-permute-start | bytes 98312 | tf_op jit(solution)/shard_map/ppermute | solution.py:327
  67.6 0.0 collective-permute-start.17
  67.6 1.5 %collective-permute-start.16 = (f32[1,64,128]{2,1,0:T(8,128)S(1)}, f32[1,64,128]{2,1,0:T(8,128)S(1)}, u32[]{:S(2)}, u32[]{:S(2)}) collective-permute-start(f32[1,64,128]{2,1,0:T(8,128)S(1)} %fusion.own), channel_id=1, source_target_pairs={{0,2},{1,3},{2,0},{3,1},{4,6},{5,7},{6,4},{7,5},{8,10},{9,11},{10,... | collective-permute-start | bytes 98312 | tf_op jit(solution)/shard_map/ppermute | solution.py:327
  69.0 1.3 %collective-permute-done.18.three = f32[1,64,128]{2,1,0:T(8,128)S(1)} collective-permute-done((f32[1,64,128]{2,1,0:T(8,128)S(1)}, f32[1,64,128]{2,1,0:T(8,128)S(1)}, u32[]{:S(2)}, u32[]{:S(2)}) %collective-permute-start.18) | collective-permute-done | bytes 32800 | tf_op jit(solution)/shard_map/ppermute | solution.py:327
  70.4 1.1 %collective-permute-done.17.two = f32[1,64,128]{2,1,0:T(8,128)S(1)} collective-permute-done((f32[1,64,128]{2,1,0:T(8,128)S(1)}, f32[1,64,128]{2,1,0:T(8,128)S(1)}, u32[]{:S(2)}, u32[]{:S(2)}) %collective-permute-start.17) | collective-permute-done | bytes 32800 | tf_op jit(solution)/shard_map/ppermute | solution.py:327
  71.5 0.9 collective-permute-done.16.one
  72.4 0.1 rows.1
  72.5 3.9 %collective-permute-start.19 = (f32[2,256,128]{2,1,0:T(8,128)S(1)}, f32[2,256,128]{2,1,0:T(8,128)S(1)}, u32[]{:S(2)}, u32[]{:S(2)}) collective-permute-start(f32[2,256,128]{2,1,0:T(8,128)S(1)} %get-tuple-element.39), channel_id=1, source_target_pairs={{0,1},{1,2},{2,3},{4,5},{5,6},{6,7},{8,9},{9,10},{10,11},{12,13},{... | collective-permute-start | bytes 786440 | tf_op jit(solution)/shard_map/ppermute | solution.py:323
  76.5 1.3 %collective-permute-start.20 = (f32[2,256,128]{2,1,0:T(8,128)S(1)}, f32[2,256,128]{2,1,0:T(8,128)S(1)}, u32[]{:S(2)}, u32[]{:S(2)}) collective-permute-start(f32[2,256,128]{2,1,0:T(8,128)S(1)} %get-tuple-element.40), channel_id=1, source_target_pairs={{1,0},{2,1},{3,2},{5,4},{6,5},{7,6},{9,8},{10,9},{11,10},{13,12},{... | collective-permute-start | bytes 786440 | tf_op jit(solution)/shard_map/ppermute | solution.py:323
  77.8 2.0 %collective-permute-start.23 = (f32[4,64,128]{2,1,0:T(8,128)S(1)}, f32[4,64,128]{2,1,0:T(8,128)S(1)}, u32[]{:S(2)}, u32[]{:S(2)}) collective-permute-start(f32[4,64,128]{2,1,0:T(8,128)S(1)} %get-tuple-element.41.own), channel_id=1, source_target_pairs={{0,24},{4,28},{8,16},{12,20},{16,8},{20,12},{24,0},{28,4},{1,25},{... | collective-permute-start | bytes 393224 | tf_op jit(solution)/shard_map/ppermute | solution.py:327
  79.8 2.2 %collective-permute-start.22 = (f32[4,64,128]{2,1,0:T(8,128)S(1)}, f32[4,64,128]{2,1,0:T(8,128)S(1)}, u32[]{:S(2)}, u32[]{:S(2)}) collective-permute-start(f32[4,64,128]{2,1,0:T(8,128)S(1)} %get-tuple-element.41.own), channel_id=1, source_target_pairs={{0,8},{4,12},{8,0},{12,4},{16,24},{20,28},{24,16},{28,20},{1,9},{5... | collective-permute-start | bytes 393224 | tf_op jit(solution)/shard_map/ppermute | solution.py:327
  81.9 0.0 collective-permute-start.21
  81.9 1.8 %collective-permute-done.23.three = f32[4,64,128]{2,1,0:T(8,128)S(1)} collective-permute-done((f32[4,64,128]{2,1,0:T(8,128)S(1)}, f32[4,64,128]{2,1,0:T(8,128)S(1)}, u32[]{:S(2)}, u32[]{:S(2)}) %collective-permute-start.23) | collective-permute-done | bytes 131104 | tf_op jit(solution)/shard_map/ppermute | solution.py:327
  83.7 2.6 %collective-permute-done.22.two = f32[4,64,128]{2,1,0:T(8,128)S(1)} collective-permute-done((f32[4,64,128]{2,1,0:T(8,128)S(1)}, f32[4,64,128]{2,1,0:T(8,128)S(1)}, u32[]{:S(2)}, u32[]{:S(2)}) %collective-permute-start.22) | collective-permute-done | bytes 131104 | tf_op jit(solution)/shard_map/ppermute | solution.py:327
  86.3 0.6 collective-permute-done.21.one
  86.9 0.0 collective-permute-done.19.from_left
  86.9 0.0 collective-permute-done.20.from_right
  86.9 0.9 columns.1
  87.8 1.9 %collective-permute-done.24.other = f32[16,64,128]{2,1,0:T(8,128)S(1)} collective-permute-done((f32[16,64,128]{2,1,0:T(8,128)S(1)}, f32[16,64,128]{2,1,0:T(8,128)S(1)}, u32[]{:S(2)}, u32[]{:S(2)}) %collective-permute-start.24) | collective-permute-done | bytes 524320 | tf_op jit(solution)/shard_map/ppermute | solution.py:357
  89.7 1.7 %join.1 = f32[2,2,256,256]{3,2,1,0:T(8,128)} custom-call(f32[16,64,128]{2,1,0:T(8,128)S(1)} %get-tuple-element.43.own, f32[16,64,128]{2,1,0:T(8,128)S(1)} %collective-permute-done.24.other), custom_call_target="tpu_custom_call" | custom-call | bytes 2097152 | tf_op jit(solution)/shard_map/join/pallas_call | solution.py:386
  (12 shorter events, 0.1 us)
Async XLA Ops:
  0.6 23.0 %copy-start = (bf16[8,2,256,256]{3,2,1,0:T(8,128)(2,1)S(1)}, bf16[8,2,256,256]{3,2,1,0:T(8,128)(2,1)}, u32[]{:S(2)}) copy-start(bf16[8,2,256,256]{3,2,1,0:T(8,128)(2,1)} %constant.6.clone.tables) | copy-start | bytes 6291460
  0.6 1.2 %copy-start.3 = (f32[2,256,256]{2,1,0:T(8,128)S(1)}, f32[2,256,256]{2,1,0:T(8,128)}, u32[]{:S(2)}) copy-start(f32[2,256,256]{2,1,0:T(8,128)} %center.1) | copy-start | bytes 1572868
  2.1 12.5 %collective-permute-start.4 = (f32[2,128,128]{2,1,0:T(8,128)S(1)}, f32[2,128,128]{2,1,0:T(8,128)S(1)}, u32[]{:S(2)}, u32[]{:S(2)}) collective-permute-start(f32[2,128,128]{2,1,0:T(8,128)S(1)} %get-tuple-element.28), channel_id=1, source_target_pairs={{0,5},{1,6},{2,7},{4,1},{5,2},{6,3},{8,13},{9,14},{10,15},{12,9},{... | collective-permute-start | bytes 393224 | tf_op jit(solution)/shard_map/ppermute | solution.py:368
  6.5 11.8 %collective-permute-start.5 = (f32[2,128,128]{2,1,0:T(8,128)S(1)}, f32[2,128,128]{2,1,0:T(8,128)S(1)}, u32[]{:S(2)}, u32[]{:S(2)}) collective-permute-start(f32[2,128,128]{2,1,0:T(8,128)S(1)} %get-tuple-element.29), channel_id=1, source_target_pairs={{1,4},{2,5},{3,6},{5,0},{6,1},{7,2},{9,12},{10,13},{11,14},{13,8},... | collective-permute-start | bytes 393224 | tf_op jit(solution)/shard_map/ppermute | solution.py:368
  7.8 11.2 %collective-permute-start.6 = (f32[2,128,128]{2,1,0:T(8,128)S(1)}, f32[2,128,128]{2,1,0:T(8,128)S(1)}, u32[]{:S(2)}, u32[]{:S(2)}) collective-permute-start(f32[2,128,128]{2,1,0:T(8,128)S(1)} %get-tuple-element.30), channel_id=1, source_target_pairs={{4,9},{5,10},{6,11},{8,5},{9,6},{10,7},{12,17},{13,18},{14,19},{16... | collective-permute-start | bytes 393224 | tf_op jit(solution)/shard_map/ppermute | solution.py:368
  8.4 15.2 %collective-permute-start = (f32[2,256,128]{2,1,0:T(8,128)S(1)}, f32[2,256,128]{2,1,0:T(8,128)S(1)}, u32[]{:S(2)}, u32[]{:S(2)}) collective-permute-start(f32[2,256,128]{2,1,0:T(8,128)S(1)} %get-tuple-element.24), channel_id=1, source_target_pairs={{0,1},{1,2},{2,3},{4,5},{5,6},{6,7},{8,9},{9,10},{10,11},{12,13},{... | collective-permute-start | bytes 786440 | tf_op jit(solution)/shard_map/ppermute | solution.py:323
  13.3 10.3 %collective-permute-start.1 = (f32[2,256,128]{2,1,0:T(8,128)S(1)}, f32[2,256,128]{2,1,0:T(8,128)S(1)}, u32[]{:S(2)}, u32[]{:S(2)}) collective-permute-start(f32[2,256,128]{2,1,0:T(8,128)S(1)} %get-tuple-element.25), channel_id=1, source_target_pairs={{1,0},{2,1},{3,2},{5,4},{6,5},{7,6},{9,8},{10,9},{11,10},{13,12},{... | collective-permute-start | bytes 786440 | tf_op jit(solution)/shard_map/ppermute | solution.py:323
  14.6 9.0 %collective-permute-start.2 = (f32[2,128,256]{2,1,0:T(8,128)S(1)}, f32[2,128,256]{2,1,0:T(8,128)S(1)}, u32[]{:S(2)}, u32[]{:S(2)}) collective-permute-start(f32[2,128,256]{2,1,0:T(8,128)S(1)} %get-tuple-element.26), channel_id=1, source_target_pairs={{0,4},{4,0},{8,12},{12,8},{16,20},{20,16},{24,28},{28,24},{1,5},{5... | collective-permute-start | bytes 786440 | tf_op jit(solution)/shard_map/ppermute | solution.py:357
  18.2 5.4 %collective-permute-start.3 = (f32[2,128,256]{2,1,0:T(8,128)S(1)}, f32[2,128,256]{2,1,0:T(8,128)S(1)}, u32[]{:S(2)}, u32[]{:S(2)}) collective-permute-start(f32[2,128,256]{2,1,0:T(8,128)S(1)} %get-tuple-element.27), channel_id=1, source_target_pairs={{4,8},{8,4},{12,16},{16,12},{20,24},{24,20},{5,9},{9,5},{13,17},{1... | collective-permute-start | bytes 786440 | tf_op jit(solution)/shard_map/ppermute | solution.py:357
  18.9 4.7 %collective-permute-start.7 = (f32[2,128,128]{2,1,0:T(8,128)S(1)}, f32[2,128,128]{2,1,0:T(8,128)S(1)}, u32[]{:S(2)}, u32[]{:S(2)}) collective-permute-start(f32[2,128,128]{2,1,0:T(8,128)S(1)} %get-tuple-element.31), channel_id=1, source_target_pairs={{5,8},{6,9},{7,10},{9,4},{10,5},{11,6},{13,16},{14,17},{15,18},{17... | collective-permute-start | bytes 393224 | tf_op jit(solution)/shard_map/ppermute | solution.py:368
  19.6 1.2 %copy-start.1 = (f32[2,2,256,256]{3,2,1,0:T(8,128)S(1)}, f32[2,2,256,256]{3,2,1,0:T(8,128)}, u32[]{:S(2)}) copy-start(f32[2,2,256,256]{3,2,1,0:T(8,128)} %probe.1) | copy-start | bytes 3145732
  20.8 1.1 %copy-start.2 = (f32[1,1,3,256,256]{4,3,2,1,0:T(8,128)S(1)}, f32[1,1,3,256,256]{4,3,2,1,0:T(8,128)}, u32[]{:S(2)}) copy-start(f32[1,1,3,256,256]{4,3,2,1,0:T(8,128)} %param.9) | copy-start | bytes 2359300
  22.0 0.9 copy-start.4
  23.6 0.7 copy-start.5
  24.3 0.7 copy-start.6
  29.3 9.6 %collective-permute-start.8 = (f32[2048,128]{1,0:T(8,128)S(1)}, f32[2048,128]{1,0:T(8,128)S(1)}, u32[]{:S(2)}, u32[]{:S(2)}) collective-permute-start(f32[2048,128]{1,0:T(8,128)S(1)} %get-tuple-element.35), channel_id=1, source_target_pairs={{0,4},{4,0},{8,12},{12,8},{16,20},{20,16},{24,28},{28,24},{1,5},{5... | collective-permute-start | bytes 3145736 | tf_op jit(solution)/shard_map/ppermute | solution.py:357
  39.1 6.4 %collective-permute-start.11 = (f32[4,64,128]{2,1,0:T(8,128)S(1)}, f32[4,64,128]{2,1,0:T(8,128)S(1)}, u32[]{:S(2)}, u32[]{:S(2)}) collective-permute-start(f32[4,64,128]{2,1,0:T(8,128)S(1)} %get-tuple-element.46), channel_id=1, source_target_pairs={{0,8},{4,12},{8,0},{12,4},{16,24},{20,28},{24,16},{28,20},{1,9},{5... | collective-permute-start | bytes 393224 | tf_op jit(solution)/shard_map/ppermute | solution.py:327
  40.9 8.9 %collective-permute-start.12 = (f32[4,64,128]{2,1,0:T(8,128)S(1)}, f32[4,64,128]{2,1,0:T(8,128)S(1)}, u32[]{:S(2)}, u32[]{:S(2)}) collective-permute-start(f32[4,64,128]{2,1,0:T(8,128)S(1)} %get-tuple-element.47), channel_id=1, source_target_pairs={{0,24},{4,28},{8,16},{12,20},{16,8},{20,12},{24,0},{28,4},{1,25},{... | collective-permute-start | bytes 393224 | tf_op jit(solution)/shard_map/ppermute | solution.py:327
  43.3 7.8 %collective-permute-start.10 = (f32[4,64,128]{2,1,0:T(8,128)S(1)}, f32[4,64,128]{2,1,0:T(8,128)S(1)}, u32[]{:S(2)}, u32[]{:S(2)}) collective-permute-start(f32[4,64,128]{2,1,0:T(8,128)S(1)} %get-tuple-element.48), channel_id=1, source_target_pairs={{0,16},{4,20},{8,24},{12,28},{16,0},{20,4},{24,8},{28,12},{1,17},{... | collective-permute-start | bytes 393224 | tf_op jit(solution)/shard_map/ppermute | solution.py:327
  43.3 25.7 %collective-permute-start.9 = (f32[1024,128]{1,0:T(8,128)S(1)}, f32[1024,128]{1,0:T(8,128)S(1)}, u32[]{:S(2)}, u32[]{:S(2)}) collective-permute-start(f32[1024,128]{1,0:T(8,128)S(1)} %get-tuple-element.36), channel_id=1, source_target_pairs={{4,8},{8,4},{12,16},{16,12},{20,24},{24,20},{5,9},{9,5},{13,17},{1... | collective-permute-start | bytes 1572872 | tf_op jit(solution)/shard_map/ppermute | solution.py:357
  51.2 9.6 %collective-permute-start.14 = (f32[1,64,128]{2,1,0:T(8,128)S(1)}, f32[1,64,128]{2,1,0:T(8,128)S(1)}, u32[]{:S(2)}, u32[]{:S(2)}) collective-permute-start(f32[1,64,128]{2,1,0:T(8,128)S(1)} %get-tuple-element.49), channel_id=1, source_target_pairs={{0,1},{1,0},{2,3},{3,2},{4,5},{5,4},{6,7},{7,6},{8,9},{9,8},{10,11... | collective-permute-start | bytes 98312 | tf_op jit(solution)/shard_map/ppermute | solution.py:327
  58.9 5.7 %collective-permute-start.15 = (f32[1,64,128]{2,1,0:T(8,128)S(1)}, f32[1,64,128]{2,1,0:T(8,128)S(1)}, u32[]{:S(2)}, u32[]{:S(2)}) collective-permute-start(f32[1,64,128]{2,1,0:T(8,128)S(1)} %get-tuple-element.50), channel_id=1, source_target_pairs={{0,3},{1,2},{2,1},{3,0},{4,7},{5,6},{6,5},{7,4},{8,11},{9,10},{10,... | collective-permute-start | bytes 98312 | tf_op jit(solution)/shard_map/ppermute | solution.py:327
  59.1 5.5 %collective-permute-start.13 = (f32[1,64,128]{2,1,0:T(8,128)S(1)}, f32[1,64,128]{2,1,0:T(8,128)S(1)}, u32[]{:S(2)}, u32[]{:S(2)}) collective-permute-start(f32[1,64,128]{2,1,0:T(8,128)S(1)} %get-tuple-element.51), channel_id=1, source_target_pairs={{0,2},{1,3},{2,0},{3,1},{4,6},{5,7},{6,4},{7,5},{8,10},{9,11},{10,... | collective-permute-start | bytes 98312 | tf_op jit(solution)/shard_map/ppermute | solution.py:327
  64.6 5.8 %collective-permute-start.18 = (f32[1,64,128]{2,1,0:T(8,128)S(1)}, f32[1,64,128]{2,1,0:T(8,128)S(1)}, u32[]{:S(2)}, u32[]{:S(2)}) collective-permute-start(f32[1,64,128]{2,1,0:T(8,128)S(1)} %fusion.own), channel_id=1, source_target_pairs={{0,3},{1,2},{2,1},{3,0},{4,7},{5,6},{6,5},{7,4},{8,11},{9,10},{10,... | collective-permute-start | bytes 98312 | tf_op jit(solution)/shard_map/ppermute | solution.py:327
  67.6 3.9 %collective-permute-start.17 = (f32[1,64,128]{2,1,0:T(8,128)S(1)}, f32[1,64,128]{2,1,0:T(8,128)S(1)}, u32[]{:S(2)}, u32[]{:S(2)}) collective-permute-start(f32[1,64,128]{2,1,0:T(8,128)S(1)} %fusion.own), channel_id=1, source_target_pairs={{0,1},{1,0},{2,3},{3,2},{4,5},{5,4},{6,7},{7,6},{8,9},{9,8},{10,11... | collective-permute-start | bytes 98312 | tf_op jit(solution)/shard_map/ppermute | solution.py:327
  67.6 4.8 %collective-permute-start.16 = (f32[1,64,128]{2,1,0:T(8,128)S(1)}, f32[1,64,128]{2,1,0:T(8,128)S(1)}, u32[]{:S(2)}, u32[]{:S(2)}) collective-permute-start(f32[1,64,128]{2,1,0:T(8,128)S(1)} %fusion.own), channel_id=1, source_target_pairs={{0,2},{1,3},{2,0},{3,1},{4,6},{5,7},{6,4},{7,5},{8,10},{9,11},{10,... | collective-permute-start | bytes 98312 | tf_op jit(solution)/shard_map/ppermute | solution.py:327
  72.5 14.4 %collective-permute-start.19 = (f32[2,256,128]{2,1,0:T(8,128)S(1)}, f32[2,256,128]{2,1,0:T(8,128)S(1)}, u32[]{:S(2)}, u32[]{:S(2)}) collective-permute-start(f32[2,256,128]{2,1,0:T(8,128)S(1)} %get-tuple-element.39), channel_id=1, source_target_pairs={{0,1},{1,2},{2,3},{4,5},{5,6},{6,7},{8,9},{9,10},{10,11},{12,13},{... | collective-permute-start | bytes 786440 | tf_op jit(solution)/shard_map/ppermute | solution.py:323
  76.5 10.4 %collective-permute-start.20 = (f32[2,256,128]{2,1,0:T(8,128)S(1)}, f32[2,256,128]{2,1,0:T(8,128)S(1)}, u32[]{:S(2)}, u32[]{:S(2)}) collective-permute-start(f32[2,256,128]{2,1,0:T(8,128)S(1)} %get-tuple-element.40), channel_id=1, source_target_pairs={{1,0},{2,1},{3,2},{5,4},{6,5},{7,6},{9,8},{10,9},{11,10},{13,12},{... | collective-permute-start | bytes 786440 | tf_op jit(solution)/shard_map/ppermute | solution.py:323
  77.8 5.9 %collective-permute-start.23 = (f32[4,64,128]{2,1,0:T(8,128)S(1)}, f32[4,64,128]{2,1,0:T(8,128)S(1)}, u32[]{:S(2)}, u32[]{:S(2)}) collective-permute-start(f32[4,64,128]{2,1,0:T(8,128)S(1)} %get-tuple-element.41.own), channel_id=1, source_target_pairs={{0,24},{4,28},{8,16},{12,20},{16,8},{20,12},{24,0},{28,4},{1,25},{... | collective-permute-start | bytes 393224 | tf_op jit(solution)/shard_map/ppermute | solution.py:327
  79.8 6.5 %collective-permute-start.22 = (f32[4,64,128]{2,1,0:T(8,128)S(1)}, f32[4,64,128]{2,1,0:T(8,128)S(1)}, u32[]{:S(2)}, u32[]{:S(2)}) collective-permute-start(f32[4,64,128]{2,1,0:T(8,128)S(1)} %get-tuple-element.41.own), channel_id=1, source_target_pairs={{0,8},{4,12},{8,0},{12,4},{16,24},{20,28},{24,16},{28,20},{1,9},{5... | collective-permute-start | bytes 393224 | tf_op jit(solution)/shard_map/ppermute | solution.py:327
  81.9 5.0 %collective-permute-start.21 = (f32[4,64,128]{2,1,0:T(8,128)S(1)}, f32[4,64,128]{2,1,0:T(8,128)S(1)}, u32[]{:S(2)}, u32[]{:S(2)}) collective-permute-start(f32[4,64,128]{2,1,0:T(8,128)S(1)} %get-tuple-element.41.own), channel_id=1, source_target_pairs={{0,16},{4,20},{8,24},{12,28},{16,0},{20,4},{24,8},{28,12},{1,17},{... | collective-permute-start | bytes 393224 | tf_op jit(solution)/shard_map/ppermute | solution.py:327
  87.8 1.9 %collective-permute-start.24 = (f32[16,64,128]{2,1,0:T(8,128)S(1)}, f32[16,64,128]{2,1,0:T(8,128)S(1)}, u32[]{:S(2)}, u32[]{:S(2)}) collective-permute-start(f32[16,64,128]{2,1,0:T(8,128)S(1)} %get-tuple-element.43.own), channel_id=1, source_target_pairs={{0,4},{4,0},{8,12},{12,8},{16,20},{20,16},{24,28},{28,24},{1,5},{5... | collective-permute-start | bytes 1572872 | tf_op jit(solution)/shard_map/ppermute | solution.py:357

commit v4 on v3

--- a/solution.py
+++ b/solution.py
@@ -13,6 +13,7 @@
 FLOOR = 0.5
 LANES = 128
 CHUNK = 32
+HEAVY = 200_000_000
 VMEM_LIMIT = 28 * 1024 * 1024
 MIDDLE_LIMIT = 12 * 1024 * 1024
 SMALL_LIMIT = 8 * 1024 * 1024
@@ -57,22 +58,26 @@
     return jnp.dot(a, b, preferred_element_type=jnp.float32)
 
 
-def edges_kernel(center, kept, to_right, to_left, to_core, to_chip, core_right, core_left, chip_right, chip_left, sems):
+def near_and_far(unit):
+    odd = lax.axis_index("ty") % 2
+    return pl.multiple_of((1 - odd) * unit, LANES), pl.multiple_of(odd * unit, LANES)
+
+
+def inner_and_outer():
+    odd = lax.axis_index("tx") % 2
+    return pl.multiple_of((1 - odd) * LANES, LANES), pl.multiple_of(odd * LANES, LANES)
+
+
+def edges_kernel(field, center, core_rows, chip_rows, inner_corner, outer_corner, sems):
     half = LANES
-    odd = lax.axis_index("ty") % 2
-    near = pl.ds(pl.multiple_of((1 - odd) * half, half), half)
-    far = pl.ds(pl.multiple_of(odd * half, half), half)
-    low, high = pl.ds(0, half), pl.ds(half, half)
+    near, far = (pl.ds(start, half) for start in near_and_far(half))
+    inner, outer = (pl.ds(start, half) for start in inner_and_outer())
     moves = (
-        (center.at[:, :, high], to_right),
-        (center.at[:, :, low], to_left),
-        (center.at[:, near, :], to_core),
-        (center.at[:, far, :], to_chip),
-        (center.at[:, near, high], core_right),
-        (center.at[:, near, low], core_left),
-        (center.at[:, far, high], chip_right),
-        (center.at[:, far, low], chip_left),
-        (center, kept),
+        (field.at[:, near, :], core_rows),
+        (field.at[:, far, inner], inner_corner),
+        (field.at[:, far, outer], outer_corner),
+        (field.at[:, far, :], chip_rows),
+        (field, center),
     )
     copies = [pltpu.make_async_copy(source, target, sems.at[i]) for i, (source, target) in enumerate(moves)]
     for copy in copies:
@@ -81,11 +86,26 @@
         copy.wait()
 
 
-def prepare_kernel(measured, probe, order, root, probe_kept, held, halves, sems):
+def sides_kernel(center, core_rows, inner_side, outer_side):
+    half = LANES
+    length = center.shape[1]
+    odd = lax.axis_index("ty") % 2
+    own, other = pl.multiple_of(odd * half, half), pl.multiple_of((1 - odd) * length, half)
+    for target, start in zip((inner_side, outer_side), inner_and_outer()):
+        cols = pl.ds(start, half)
+        target[:, pl.ds(own, length), :] = center[:, :, cols]
+        target[:, pl.ds(other, half), :] = core_rows[:, :, cols]
+
+
+def prepare_kernel(counts, spots, order, measured, probe, root, probe_kept, scalars, held, halves, sems):
     first = pltpu.make_async_copy(measured, held, sems.at[0])
     second = pltpu.make_async_copy(probe, probe_kept, sems.at[1])
     first.start()
     second.start()
+    scalars[0] = counts[lax.axis_index("tx"), lax.axis_index("ty")]
+    for slot in range(spots.shape[1]):
+        for axis in range(2):
+            scalars[1 + 2 * slot + axis] = spots[axis, slot]
     first.wait()
     for slot in range(measured.shape[0]):
         for b in range(2):
@@ -98,37 +118,37 @@
 
 
 def slots_kernel(
-    counts, spots, center, left, right, core_rows, chip_rows,
-    core_from_left, core_from_right, chip_from_left, chip_from_right, probe, root, tables,
-    core_out, chip_out, grad_mid, probe_keep,
+    scalars, center, core_rows, chip_rows, inner_side, outer_side, inner_corner, outer_corner, probe, root, tables,
+    probe_sent, probe_keep, inner_side_out, outer_side_out, inner_corner_out, outer_corner_out, chip_out, grad_mid,
     pad, grid, patch, rows_high, rows_low, freq, sums,
 ):
     half = LANES
     modes = probe.shape[1]
     length = center.shape[1]
-    margin = left.shape[2]
-    odd = lax.axis_index("ty") % 2
-    near = pl.multiple_of((1 - odd) * (margin + length), half)
-    far = pl.multiple_of(odd * (margin + length), half)
-
-    pad[:, 0, margin : margin + length, :] = left[...]
-    pad[:, 3, margin : margin + length, :] = right[...]
+    margin = core_rows.shape[1]
+    tall = inner_side.shape[1]
+    near, far = near_and_far(margin + length)
+    long_start = pl.multiple_of((1 - lax.axis_index("ty") % 2) * margin, half)
+    near, far, both = pl.ds(near, margin), pl.ds(far, margin), pl.ds(long_start, tall)
+    inner = (1 - lax.axis_index("tx") % 2) * 3
+    outer = 3 - inner
+
     for b in range(2):
         cols = slice(b * half, (b + 1) * half)
         pad[:, 1 + b, margin : margin + length, :] = center[:, :, cols]
-        pad[:, 1 + b, pl.ds(near, margin), :] = core_rows[:, :, cols]
-        pad[:, 1 + b, pl.ds(far, margin), :] = chip_rows[:, :, cols]
-    pad[:, 0, pl.ds(near, margin), :] = core_from_left[...]
-    pad[:, 3, pl.ds(near, margin), :] = core_from_right[...]
-    pad[:, 0, pl.ds(far, margin), :] = chip_from_left[...]
-    pad[:, 3, pl.ds(far, margin), :] = chip_from_right[...]
+        pad[:, 1 + b, near, :] = core_rows[:, :, cols]
+        pad[:, 1 + b, far, :] = chip_rows[:, :, cols]
+    pad[:, inner, both, :] = inner_side[...]
+    pad[:, outer, both, :] = outer_side[...]
+    pad[:, inner, far, :] = inner_corner[...]
+    pad[:, outer, far, :] = outer_corner[...]
     grid[...] = jnp.zeros_like(grid)
     sums[...] = jnp.zeros_like(sums)
     lane = lax.broadcasted_iota(jnp.int32, (CHUNK, half), 1)
 
     def slot_step(slot, carry):
-        row0 = spots[0, slot]
-        col0 = spots[1, slot]
+        row0 = scalars[1 + 2 * slot]
+        col0 = scalars[2 + 2 * slot]
         block = jnp.minimum(col0 // half, 1)
         shift = col0 - block * half
         back_shift = lax.rem(half - shift, half)
@@ -240,55 +260,50 @@
                         grid[c, block + b, pl.ds(row0 + rows, CHUNK), :] += placed[b]
         return carry
 
-    listed = counts[lax.axis_index("tx"), lax.axis_index("ty")]
-    lax.fori_loop(0, listed, slot_step, 0)
-
-    grad_mid[...] = grid[:, :, margin : margin + length, :]
-    for c in range(2):
-        for b in range(4):
-            at = slice((c * 4 + b) * margin, (c * 4 + b + 1) * margin)
-            core_out[at, :] = grid[c, b, pl.ds(near, margin), :]
-            chip_out[at, :] = grid[c, b, pl.ds(far, margin), :]
+    lax.fori_loop(0, scalars[0], slot_step, 0)
+
     kept, rows, _ = probe_keep.shape
     code = own_code(digit_groups())
-    first_sent = core_out.shape[0] - kept * rows
 
     def place_piece(place, carry):
-        piece = place ^ code
-        probe_keep[place] = sums[pl.ds(pl.multiple_of(piece * rows, rows), rows), :]
-        piece = (place + kept) ^ code
-        core_out[pl.ds(pl.multiple_of(first_sent + place * rows, rows), rows), :] = sums[
-            pl.ds(pl.multiple_of(piece * rows, rows), rows), :
-        ]
+        for first, target in ((0, probe_keep), (kept, probe_sent)):
+            piece = (place + first) ^ code
+            target[place] = sums[pl.ds(pl.multiple_of(piece * rows, rows), rows), :]
         return carry
 
     lax.fori_loop(0, kept, place_piece, 0)
-
-
-def rows_kernel(grad_mid, core_in, chip_in, own, one, two, three, to_left, to_right, inner, joined):
+    inner_side_out[...] = grid[:, inner, both, :]
+    outer_side_out[...] = grid[:, outer, both, :]
+    inner_corner_out[...] = grid[:, inner, far, :]
+    outer_corner_out[...] = grid[:, outer, far, :]
+    for b in range(2):
+        cols = slice(b * half, (b + 1) * half)
+        chip_out[:, :, cols] = grid[:, 1 + b, far, :]
+        grad_mid[:, :, cols] = grid[:, 1 + b, both, :]
+
+
+def rows_kernel(grad_mid, inner_side, outer_side, chip_in, inner_corner, outer_corner, own, other, core_out, inner_grad, joined):
     half = LANES
+    length = inner_grad.shape[1]
     odd = lax.axis_index("ty") % 2
-    for c in range(2):
-        for b in range(4):
-            at = slice((c * 4 + b) * half, (c * 4 + b + 1) * half)
-            core, chip = core_in[at, :], chip_in[at, :]
-            for part in range(2):
-                rows = slice(part * half, (part + 1) * half)
-                value = grad_mid[c, b, rows, :] + jnp.where(odd == 1 - part, core, chip)
-                if b == 0:
-                    to_left[c, rows, :] = value
-                elif b == 3:
-                    to_right[c, rows, :] = value
-                else:
-                    inner[c, rows, (b - 1) * half : b * half] = value
-    join_pieces((own, one, two, three), joined)
-
-
-def columns_kernel(inner, from_left, from_right, own, one, two, three, grad, joined):
-    half = LANES
-    grad[:, :, :half] = inner[:, :, :half] + from_left[...]
-    grad[:, :, half:] = inner[:, :, half:] + from_right[...]
-    join_pieces((own, one, two, three), joined)
+    near_rows = pl.ds(pl.multiple_of((1 - odd) * length, half), half)
+    near, far = (pl.ds(start, half) for start in near_and_far(half))
+    near_own = pl.ds(pl.multiple_of(half, half), half)
+    far_own = pl.ds(pl.multiple_of(odd * length, half), half)
+    for side, corner, start in zip((inner_side, outer_side), (inner_corner, outer_corner), inner_and_outer()):
+        cols = pl.ds(start, half)
+        core_out[:, :, cols] = grad_mid[:, near_rows, cols] + side[:, near_rows, :]
+        inner_grad[:, near, cols] = grad_mid[:, near_own, cols] + side[:, near_own, :]
+        inner_grad[:, far, cols] = (grad_mid[:, far_own, cols] + side[:, far_own, :]) + (chip_in[:, :, cols] + corner[...])
+    join_pieces((own, other), joined)
+
+
+def columns_kernel(inner_grad, core_in, *refs):
+    pieces, (grad, joined) = refs[:-2], refs[-2:]
+    near, far = (pl.ds(start, LANES) for start in near_and_far(LANES))
+    grad[:, near, :] = inner_grad[:, near, :] + core_in[...]
+    grad[:, far, :] = inner_grad[:, far, :]
+    join_pieces(pieces, joined)
 
 
 def join_pieces(pieces, joined):
@@ -317,22 +332,15 @@
         lax.fori_loop(0, kept, place_piece, 0)
 
 
-def shifted(value, axis, steps):
-    count = lax.axis_size(axis)
-    initial, last = (max(0, -steps), min(count, count - steps))
-    return lax.ppermute(value, axis, [(source, source + steps) for source in range(initial, last)])
-
-
 def exchanged(value, axis, mask):
     return lax.ppermute(value, axis, [(i, i ^ mask) for i in range(lax.axis_size(axis))])
 
 
 def digit_groups():
     groups = [("ty", [1])]
-    for axis, first in (("ty", 1), ("tx", 0)):
-        bits = [1 << i for i in range(first, lax.axis_size(axis).bit_length() - 1)]
-        groups += [(axis, bits[i : i + 2]) for i in range(0, len(bits), 2)]
-    return groups
+    bits = [1 << i for i in range(1, lax.axis_size("ty").bit_length() - 1)]
+    groups += [("ty", bits[i : i + 2]) for i in range(0, len(bits), 2)]
+    return groups + [("tx", [1])]
 
 
 def masks(bits):
@@ -348,46 +356,65 @@
     return code
 
 
-def paired(value, mask_of):
-    count = lax.axis_size("ty")
-    pairs = [(i, i ^ 1) for i in range(count)] if mask_of == "core" else []
-    if mask_of == "chip":
-        for i in range(1, count - 1, 2):
-            pairs += [(i, i + 1), (i + 1, i)]
-    return lax.ppermute(value, "ty", pairs)
-
-
-def cornered(value, mask_of, steps):
+def pair_partner(index, kind):
+    return index ^ 1 if kind == "inner" else index + 1 if index % 2 else index - 1
+
+
+def paired(value, axis, kind):
+    count = lax.axis_size(axis)
+    pairs = [(i, pair_partner(i, kind)) for i in range(count)]
+    return lax.ppermute(value, axis, [(i, j) for i, j in pairs if 0 <= j < count])
+
+
+def cornered(value, kind):
     rows, cols = lax.axis_size("ty"), lax.axis_size("tx")
     pairs = []
     for a in range(rows):
-        other = a ^ 1 if mask_of == "core" else a + 1 if a % 2 else a - 1
         for b in range(cols):
-            if 0 <= other < rows and 0 <= b + steps < cols:
-                pairs.append((a * cols + b, other * cols + b + steps))
+            i, j = pair_partner(a, "outer"), pair_partner(b, kind)
+            if 0 <= i < rows and 0 <= j < cols:
+                pairs.append((a * cols + b, i * cols + j))
     return lax.ppermute(value, ("ty", "tx"), pairs)
 
 
-def reduce_step(value, axis, bits):
+def add_kernel(scale, own, *refs):
+    others, out = refs[:-1], refs[-1]
+    count = out.shape[0]
+    total = own[:count]
+    for other in others:
+        total += other[...]
+    out[...] = total * scale
+
+
+def added(own, others, scale=1.0, weight=0):
+    out = jax.ShapeDtypeStruct(others[0].shape, jnp.float32)
+    (result,) = call(functools.partial(add_kernel, scale), "add", [out], (own, *others), weight=weight)
+    return result
+
+
+def reduce_step(value, axis, bits, scale=1.0, weight=0):
     places = masks(bits)
     count = value.shape[0] // len(places)
     taken = [exchanged(value[j * count : (j + 1) * count], axis, places[j]) for j in range(1, len(places))]
-    return value[:count] + sum(taken[1:], taken[0])
+    return added(value, taken, scale, weight)
 
 
 def gathered(value, axis, bits):
     return [value] + [exchanged(value, axis, mask) for mask in masks(bits)[1:]]
 
 
-def call(body, name, out, operands, spaces="", scratch=(), limit=SMALL_LIMIT):
-    kinds = {"v": pltpu.VMEM, "s": pltpu.SMEM, "a": pl.ANY}
-    spaces = spaces + "v" * (len(operands) - len(spaces))
-    moved = sum(math.prod(v.shape) * v.dtype.itemsize for v in tuple(operands) + tuple(out))
+def call(body, name, out, operands, spaces="", results="", scratch=(), limit=SMALL_LIMIT, weight=0):
+    kinds = {"v": pltpu.VMEM, "s": pltpu.SMEM, "h": pltpu.HBM}
+
+    def specs(letters, count):
+        return tuple(pl.BlockSpec(memory_space=kinds[x]) for x in letters + "v" * (count - len(letters)))
+
+    moved = weight + sum(math.prod(v.shape) * v.dtype.itemsize for v in tuple(operands) + tuple(out))
     return pl.pallas_call(
         body,
         out_shape=tuple(out),
-        in_specs=[pl.BlockSpec(memory_space=kinds[space]) for space in spaces],
-        out_specs=(pl.BlockSpec(memory_space=pltpu.VMEM),) * len(out),
+        in_specs=specs(spaces, len(operands)),
+        out_specs=specs(results, len(out)),
         scratch_shapes=list(scratch),
         compiler_params=pltpu.CompilerParams(vmem_limit_bytes=limit),
         cost_estimate=pl.CostEstimate(flops=0, bytes_accessed=moved, transcendentals=0),
@@ -410,30 +437,29 @@
     def shape(*sizes):
         return jax.ShapeDtypeStruct(sizes, f32)
 
-    center, to_right, to_left, to_core, to_chip, core_right, core_left, chip_right, chip_left = call(
+    tile, rows_shape, side, corner = shape(2, length, length), shape(2, margin, length), shape(2, length + margin, margin), shape(2, margin, margin)
+    center, core_rows, chip_rows, inner_corner, outer_corner = call(
         edges_kernel,
         "edges",
-        [shape(2, length, length)] + [shape(2, length, margin)] * 2 + [shape(2, margin, length)] * 2 + [shape(2, margin, margin)] * 4,
+        [tile, rows_shape, rows_shape, corner, corner],
         (object_field,),
-        "a",
-        scratch=(pltpu.SemaphoreType.DMA((9,)),),
+        "h",
+        scratch=(pltpu.SemaphoreType.DMA((5,)),),
     )
-    left = shifted(to_right, "tx", 1)
-    right = shifted(to_left, "tx", -1)
-    core_rows = paired(to_core, "core")
-    chip_rows = paired(to_chip, "chip")
-    corners = [
-        cornered(core_right, "core", 1),
-        cornered(core_left, "core", -1),
-        cornered(chip_right, "chip", 1),
-        cornered(chip_left, "chip", -1),
-    ]
-    root, probe = call(
+    core_rows = paired(core_rows, "ty", "inner")
+    inner_corner = cornered(inner_corner, "inner")
+    outer_corner = cornered(outer_corner, "outer")
+    chip_rows = paired(chip_rows, "ty", "outer")
+    inner_side, outer_side = call(sides_kernel, "sides", [side, side], (center, core_rows), weight=HEAVY)
+    inner_side = paired(inner_side, "tx", "inner")
+    outer_side = paired(outer_side, "tx", "outer")
+    root, probe, scalars = call(
         prepare_kernel,
         "prepare",
-        [shape(slots, 2, half, pattern), shape(*probe_modes.shape)],
-        (intensities[0, 0], probe_modes, order),
-        "aa",
+        [shape(slots, 2, half, pattern), shape(*probe_modes.shape), jax.ShapeDtypeStruct((1 + 2 * slots,), jnp.int32)],
+        (counts.T, offsets[0, 0].T, order, intensities[0, 0], probe_modes),
+        "ssvhh",
+        "vvs",
         scratch=(
             pltpu.VMEM((slots, pattern, pattern), f32),
             pltpu.VMEM((slots, 2, pattern, half), f32),
@@ -442,15 +468,15 @@
         limit=MIDDLE_LIMIT,
     )
 
-    rows = 2 * 2 * modes * pattern // devices
-    kept = devices // 2
-    border = 2 * 4 * margin
-    core_out, chip_out, grad_mid, probe_keep = call(
+    pieces = 1 << sum(len(bits) for _, bits in groups)
+    rows = 2 * 2 * modes * pattern // pieces
+    kept = shape(pieces // 2, rows, half)
+    probe_sent, value, inner_side, outer_side, inner_corner, outer_corner, chip_rows, grad_mid = call(
         slots_kernel,
         "slots",
-        [shape(border + kept * rows, half), shape(border, half), shape(2, 4, length, half), shape(kept, rows, half)],
-        (counts.T, offsets[0, 0].T, center, left, right, core_rows, chip_rows, *corners, probe, root, tables),
-        "ss",
+        [kept, kept, side, side, corner, corner, rows_shape, shape(2, length + margin, length)],
+        (scalars, center, core_rows, chip_rows, inner_side, outer_side, inner_corner, outer_corner, probe, root, tables),
+        "s",
         scratch=(
             pltpu.VMEM((2, 4, length + 2 * margin, half), f32),
             pltpu.VMEM((2, 4, length + 2 * margin, half), f32),
@@ -463,37 +489,37 @@
         limit=VMEM_LIMIT,
     )
 
-    core_in = paired(core_out, "core")
-    chip_in = paired(chip_out, "chip")
-    value = probe_keep + core_in[border:].reshape(probe_keep.shape)
-    for axis, bits in groups[1:]:
+    value = added(value, [paired(probe_sent, "ty", "inner")], weight=HEAVY)
+    inner_side = paired(inner_side, "tx", "inner")
+    outer_side = paired(outer_side, "tx", "outer")
+    for axis, bits in groups[1:-1]:
         value = reduce_step(value, axis, bits)
-    value = value * (1.0 / devices)
-    last = len(groups) - 1
-    for i in range(last, 0, -1):
-        pieces = gathered(value, *groups[i])
-        joined = shape(len(pieces) * value.shape[0], rows, half)
-        if i == last:
-            assert len(pieces) == 4
-            to_left, to_right, inner, value = call(
-                rows_kernel,
-                "rows",
-                [shape(2, length, half)] * 2 + [shape(2, length, length), joined],
-                (grad_mid, core_in[:border], chip_in, *pieces),
+    value = reduce_step(value, *groups[-1], scale=1.0 / devices, weight=HEAVY)
+    for i in range(1, lax.axis_size("tx").bit_length() - 1):
+        value = added(value, [exchanged(value, "tx", 1 << i)])
+    chip_rows = paired(chip_rows, "ty", "outer")
+    inner_corner = cornered(inner_corner, "inner")
+    outer_corner = cornered(outer_corner, "outer")
+    for i in range(len(groups) - 1, 0, -1):
+        parts = gathered(value, *groups[i])
+        joined = shape(len(parts) * value.shape[0], rows, half)
+        if i == len(groups) - 1:
+            core_rows, inner_grad, value = call(
+                rows_kernel, "rows", [rows_shape, tile, joined], (grad_mid, inner_side, outer_side, chip_rows, inner_corner, outer_corner, *parts)
             )
-            from_right = shifted(to_left, "tx", -1)
-            from_left = shifted(to_right, "tx", 1)
-        elif i == 1 and len(pieces) == 4:
-            inner, value = call(
-                columns_kernel, "columns", [shape(2, length, length), joined], (inner, from_left, from_right, *pieces)
+            core_rows = paired(core_rows, "ty", "inner")
+        elif i == 1:
+            object_grad, value = call(
+                columns_kernel,
+                "columns",
+                [tile, joined],
+                (inner_grad, core_rows, *parts),
             )
         else:
-            value = jnp.concatenate(pieces, axis=0)
-    if len(groups) < 3 or len(groups[1][1]) != 2:
-        inner = inner + jnp.concatenate([from_left, from_right], axis=2)
-    other = paired(value, "core")
+            value = jnp.concatenate(parts, axis=0)
+    other = paired(value, "ty", "inner")
     (probe_grad,) = call(join_kernel, "join", [shape(*probe_modes.shape)], (value, other))
-    return (inner, probe_grad)
+    return (object_grad, probe_grad)
 
 
 def solution(mesh):

time: 91.9 us -> 79.4 us (0.86)
  starting transfers between devices: 52.8 us -> 38.9 us
    ppermute x9 -> x10, starting transfers between devices: 23.7 us -> 17.5 us  [paired(): lax.ppermute(value, axis, [(i, j) for i, j in pairs if 0 <= j < count])]
    ppermute x4, starting transfers between devices: 7 us -> 2.65 us  [cornered(): return lax.ppermute(value, ('ty', 'tx'), pairs)]
    ppermute x12 -> x9, starting transfers between devices: 22.1 us -> 18.8 us  [exchanged(): lax.ppermute(value, axis, [(i, i ^ mask) for i in range(lax.axis_size(axi...]
    pallas_call x6 -> x11, Pallas kernels: 7.93 us -> 8.72 us  [call(): pl.pallas_call(body, out_shape=tuple(out), in_specs=specs(spaces, len(ope...]
    ppermute x9 -> x10, waiting for transfers between devices: 4.21 us -> 4.77 us  [paired(): lax.ppermute(value, axis, [(i, j) for i, j in pairs if 0 <= j < count])]
    ppermute x12 -> x9, waiting for transfers between devices: 19.6 us -> 19.6 us  [exchanged(): lax.ppermute(value, axis, [(i, i ^ mask) for i in range(lax.axis_size(axi...]
  transfers between devices with their start and end apart: 25 -> 23, of which waited for: 13 -> 10; matrix products, arithmetic and copies ran while one was open for 0% -> 0% of each run, Pallas kernels for 1% -> 2%
where the time goes in v4:
time: 79.4 us; the launch traced here: 78.7 us
  starting transfers between devices  38.9 us (49%)
  waiting for transfers between devices  24.4 us (31%)
  Pallas kernels  8.72 us (11%)
  local copies, waits for them, and re-layouts  5.84 us (7%)
  between operations  0.85 us (1%)
    ppermute x9, waiting for transfers between devices, exchanged(): lax.ppermute(value, axis, [(i, i ^ mask) for i in range(lax.axis_size(axi...  19.6 us
    ppermute x9, starting transfers between devices, exchanged(): lax.ppermute(value, axis, [(i, i ^ mask) for i in range(lax.axis_size(axi...  18.8 us
    ppermute x10, starting transfers between devices, paired(): lax.ppermute(value, axis, [(i, j) for i, j in pairs if 0 <= j < count])  17.5 us
    pallas_call x11, Pallas kernels, call(): pl.pallas_call(body, out_shape=tuple(out), in_specs=specs(spaces, len(ope...  8.72 us
    unnamed x14, local copies, waits for them, and re-layouts  5.81 us
    ppermute x10, waiting for transfers between devices, paired(): lax.ppermute(value, axis, [(i, j) for i, j in pairs if 0 <= j < count])  4.77 us
    ppermute x4, starting transfers between devices, cornered(): return lax.ppermute(value, ('ty', 'tx'), pairs)  2.65 us
  transfers between devices with their start and end apart: 23, of which 10 were waited for; matrix products, arithmetic and copies ran while one was open for 0% of the time, Pallas kernels for 2%

profile of v4, /device:TPU:0, one launch (start us, length us, event | category | flops | bytes accessed | tf_op | source)
XLA Modules:
  0.0 78.7 jit_solution(12537936241877543432)
XLA Ops:
  0.6 0.0 copy-start
  0.6 0.0 copy-start.3
  0.7 1.2 %copy-done.3 = f32[2,256,256]{2,1,0:T(8,128)S(1)} copy-done((f32[2,256,256]{2,1,0:T(8,128)S(1)}, f32[2,256,256]{2,1,0:T(8,128)}, u32[]{:S(2)}) %copy-start.3) | copy-done | bytes 524312
  1.8 0.1 edges.1
  2.0 0.5 collective-permute-start
  2.5 1.2 %collective-permute-done.core_rows = f32[2,128,256]{2,1,0:T(8,128)S(1)} collective-permute-done((f32[2,128,256]{2,1,0:T(8,128)S(1)}, f32[2,128,256]{2,1,0:T(8,128)S(1)}, u32[]{:S(2)}, u32[]{:S(2)}) %collective-permute-start) | collective-permute-done | bytes 262176 | tf_op jit(solution)/shard_map/ppermute | solution.py:366
  3.7 0.1 sides.1
  3.7 3.0 %collective-permute-start.2 = (f32[2,384,128]{2,1,0:T(8,128)S(1)}, f32[2,384,128]{2,1,0:T(8,128)S(1)}, u32[]{:S(2)}, u32[]{:S(2)}) collective-permute-start(f32[2,384,128]{2,1,0:T(8,128)S(1)} %get-tuple-element.29), channel_id=1, source_target_pairs={{0,1},{1,0},{2,3},{3,2},{4,5},{5,4},{6,7},{7,6},{8,9},{9,8},{10,11... | collective-permute-start | bytes 1179656 | tf_op jit(solution)/shard_map/ppermute | solution.py:366
  6.7 0.7 collective-permute-start.3
  7.4 0.7 collective-permute-start.1
  8.1 0.7 collective-permute-start.4
  8.8 0.7 collective-permute-start.5
  9.5 0.0 copy-start.1
  9.5 1.2 %copy-done.1 = f32[2,2,256,256]{3,2,1,0:T(8,128)S(1)} copy-done((f32[2,2,256,256]{3,2,1,0:T(8,128)S(1)}, f32[2,2,256,256]{3,2,1,0:T(8,128)}, u32[]{:S(2)}) %copy-start.1) | copy-done | bytes 1048600
  10.7 1.1 %copy-done.2 = f32[1,1,3,256,256]{4,3,2,1,0:T(8,128)S(1)} copy-done((f32[1,1,3,256,256]{4,3,2,1,0:T(8,128)S(1)}, f32[1,1,3,256,256]{4,3,2,1,0:T(8,128)}, u32[]{:S(2)}) %copy-start.2) | copy-done | bytes 786456
  11.8 0.9 %copy-done.4 = bf16[256,256]{1,0:T(8,128)(2,1)S(1)} copy-done((bf16[256,256]{1,0:T(8,128)(2,1)S(1)}, bf16[256,256]{1,0:T(8,128)(2,1)}, u32[]{:S(2)}) %copy-start.4) | copy-done | bytes 131096
  12.7 0.7 copy-done.5
  13.4 0.7 copy-done.6
  14.1 1.9 %prepare.1 = (f32[3,2,128,256]{3,2,1,0:T(8,128)S(1)}, f32[2,2,256,256]{3,2,1,0:T(8,128)S(1)}, s32[7]{0:T(128)S(1)}) custom-call(s32[4,8]{1,0:T(4,128)S(1)} %bitcast.6, s32[2,3]{1,0:T(2,128)S(1)} %bitcast.7, bf16[256,256]{1,0:T(8,128)(2,1)S(1)} %copy-done.4, f32[3,256,256]{2,1,0:T(8,128)S(1)} %bitcast.5, f32[2,2,256,256]{3,2,1,0:T(8,128)S(1)} %copy-done.1), custom_call_target="tpu_custom_call" | custom-call | bytes 3801268 | tf_op jit(solution)/shard_map/prepare/pallas_call | solution.py:413
  16.0 0.0 collective-permute-done.4.inner_corner
  16.0 0.0 collective-permute-done.5.outer_corner
  16.0 0.0 collective-permute-done.1.chip_rows
  16.0 0.1 collective-permute-done.2.inner_side
  16.1 0.0 collective-permute-done.3.outer_side
  16.2 0.0 copy-done
  16.2 4.2 %slots.1 = (f32[8,128,128]{2,1,0:T(8,128)S(1)}, f32[8,128,128]{2,1,0:T(8,128)S(1)}, f32[2,384,128]{2,1,0:T(8,128)S(1)}, f32[2,384,128]{2,1,0:T(8,128)S(1)}, f32[...) custom-call(s32[7]{0:T(128)S(1)} %get-tuple-element.25.scalars, ...), custom_call_target="tpu_custom_call" | custom-call | bytes 9175068 | tf_op jit(solution)/shard_map/slots/pallas_call | solution.py:413
  20.3 7.9 %collective-permute-start.11 = (f32[8,128,128]{2,1,0:T(8,128)S(1)}, f32[8,128,128]{2,1,0:T(8,128)S(1)}, u32[]{:S(2)}, u32[]{:S(2)}) collective-permute-start(f32[8,128,128]{2,1,0:T(8,128)S(1)} %get-tuple-element.42), channel_id=1, source_target_pairs={{0,4},{4,0},{8,12},{12,8},{16,20},{20,16},{24,28},{28,24},{1,5},{5... | collective-permute-start | bytes 1572872 | tf_op jit(solution)/shard_map/ppermute | solution.py:366
  28.2 1.5 %collective-permute-done.11.refs_0_ = f32[8,128,128]{2,1,0:T(8,128)S(1)} collective-permute-done((f32[8,128,128]{2,1,0:T(8,128)S(1)}, f32[8,128,128]{2,1,0:T(8,128)S(1)}, u32[]{:S(2)}, u32[]{:S(2)}) %collective-permute-start.11) | collective-permute-done | bytes 524320 | tf_op jit(solution)/shard_map/ppermute | solution.py:366
  29.7 0.1 add.4.own
  29.8 3.0 %collective-permute-start.14 = (f32[2,128,128]{2,1,0:T(8,128)S(1)}, f32[2,128,128]{2,1,0:T(8,128)S(1)}, u32[]{:S(2)}, u32[]{:S(2)}) collective-permute-start(f32[2,128,128]{2,1,0:T(8,128)S(1)} %get-tuple-element.48), channel_id=1, source_target_pairs={{0,24},{4,28},{8,16},{12,20},{16,8},{20,12},{24,0},{28,4},{1,25},{... | collective-permute-start | bytes 393224 | tf_op jit(solution)/shard_map/ppermute | solution.py:336
  32.8 4.5 %collective-permute-start.13 = (f32[2,128,128]{2,1,0:T(8,128)S(1)}, f32[2,128,128]{2,1,0:T(8,128)S(1)}, u32[]{:S(2)}, u32[]{:S(2)}) collective-permute-start(f32[2,128,128]{2,1,0:T(8,128)S(1)} %get-tuple-element.49), channel_id=1, source_target_pairs={{0,8},{4,12},{8,0},{12,4},{16,24},{20,28},{24,16},{28,20},{1,9},{5... | collective-permute-start | bytes 393224 | tf_op jit(solution)/shard_map/ppermute | solution.py:336
  37.3 0.0 collective-permute-start.12
  37.3 2.7 %collective-permute-start.6 = (f32[2,384,128]{2,1,0:T(8,128)S(1)}, f32[2,384,128]{2,1,0:T(8,128)S(1)}, u32[]{:S(2)}, u32[]{:S(2)}) collective-permute-start(f32[2,384,128]{2,1,0:T(8,128)S(1)} %get-tuple-element.36), channel_id=1, source_target_pairs={{0,1},{1,0},{2,3},{3,2},{4,5},{5,4},{6,7},{7,6},{8,9},{9,8},{10,11... | collective-permute-start | bytes 1179656 | tf_op jit(solution)/shard_map/ppermute | solution.py:366
  40.1 0.7 collective-permute-start.7
  40.7 0.0 collective-permute-done.14.refs_2_
  40.7 2.9 %collective-permute-done.13.refs_1_ = f32[2,128,128]{2,1,0:T(8,128)S(1)} collective-permute-done((f32[2,128,128]{2,1,0:T(8,128)S(1)}, f32[2,128,128]{2,1,0:T(8,128)S(1)}, u32[]{:S(2)}, u32[]{:S(2)}) %collective-permute-start.13) | collective-permute-done | bytes 131104 | tf_op jit(solution)/shard_map/ppermute | solution.py:336
  43.7 0.0 collective-permute-done.12.refs_0_
  43.7 1.8 %collective-permute-start.15 = (f32[1,128,128]{2,1,0:T(8,128)S(1)}, f32[1,128,128]{2,1,0:T(8,128)S(1)}, u32[]{:S(2)}, u32[]{:S(2)}) collective-permute-start(f32[1,128,128]{2,1,0:T(8,128)S(1)} %slice.19), channel_id=1, source_target_pairs={{0,1},{1,0},{2,3},{3,2},{4,5},{5,4},{6,7},{7,6},{8,9},{9,8},{10,11... | collective-permute-start | bytes 196616 | tf_op jit(solution)/shard_map/ppermute | solution.py:336
  45.5 0.7 collective-permute-start.8
  46.2 4.3 %collective-permute-done.15.refs_0_ = f32[1,128,128]{2,1,0:T(8,128)S(1)} collective-permute-done((f32[1,128,128]{2,1,0:T(8,128)S(1)}, f32[1,128,128]{2,1,0:T(8,128)S(1)}, u32[]{:S(2)}, u32[]{:S(2)}) %collective-permute-start.15) | collective-permute-done | bytes 65568 | tf_op jit(solution)/shard_map/ppermute | solution.py:336
  50.5 1.5 %collective-permute-start.16 = (f32[1,128,128]{2,1,0:T(8,128)S(1)}, f32[1,128,128]{2,1,0:T(8,128)S(1)}, u32[]{:S(2)}, u32[]{:S(2)}) collective-permute-start(f32[1,128,128]{2,1,0:T(8,128)S(1)} %add.6.own), channel_id=1, source_target_pairs={{0,2},{1,3},{2,0},{3,1},{4,6},{5,7},{6,4},{7,5},{8,10},{9,11},{10,... | collective-permute-start | bytes 196616 | tf_op jit(solution)/shard_map/ppermute | solution.py:336
  52.1 0.7 collective-permute-start.9
  52.8 3.1 %collective-permute-done.16.refs_0_ = f32[1,128,128]{2,1,0:T(8,128)S(1)} collective-permute-done((f32[1,128,128]{2,1,0:T(8,128)S(1)}, f32[1,128,128]{2,1,0:T(8,128)S(1)}, u32[]{:S(2)}, u32[]{:S(2)}) %collective-permute-start.16) | collective-permute-done | bytes 65568 | tf_op jit(solution)/shard_map/ppermute | solution.py:336
  55.9 0.7 collective-permute-start.10
  56.6 0.0 collective-permute-done.9.inner_corner
  56.6 1.7 %collective-permute-start.17 = (f32[1,128,128]{2,1,0:T(8,128)S(1)}, f32[1,128,128]{2,1,0:T(8,128)S(1)}, u32[]{:S(2)}, u32[]{:S(2)}) collective-permute-start(f32[1,128,128]{2,1,0:T(8,128)S(1)} %add.7.own), channel_id=1, source_target_pairs={{0,1},{1,0},{2,3},{3,2},{4,5},{5,4},{6,7},{7,6},{8,9},{9,8},{10,11... | collective-permute-start | bytes 196616 | tf_op jit(solution)/shard_map/ppermute | solution.py:336
  58.3 0.0 collective-permute-done.10.outer_corner
  58.3 0.0 collective-permute-done.8.chip_in
  58.3 0.0 collective-permute-done.6.inner_side
  58.3 0.0 collective-permute-done.7.outer_side
  58.3 2.6 %collective-permute-done.17.other = f32[1,128,128]{2,1,0:T(8,128)S(1)} collective-permute-done((f32[1,128,128]{2,1,0:T(8,128)S(1)}, f32[1,128,128]{2,1,0:T(8,128)S(1)}, u32[]{:S(2)}, u32[]{:S(2)}) %collective-permute-start.17) | collective-permute-done | bytes 65568 | tf_op jit(solution)/shard_map/ppermute | solution.py:336
  60.9 0.1 rows.1
  61.1 0.6 collective-permute-start.18
  61.7 4.2 %collective-permute-start.21 = (f32[2,128,128]{2,1,0:T(8,128)S(1)}, f32[2,128,128]{2,1,0:T(8,128)S(1)}, u32[]{:S(2)}, u32[]{:S(2)}) collective-permute-start(f32[2,128,128]{2,1,0:T(8,128)S(1)} %get-tuple-element.45.refs_0_), channel_id=1, source_target_pairs={{0,24},{4,28},{8,16},{12,20},{16,8},{20,12},{24,0},{28,4},{1,25},{... | collective-permute-start | bytes 393224 | tf_op jit(solution)/shard_map/ppermute | solution.py:336
  65.9 2.0 %collective-permute-start.20 = (f32[2,128,128]{2,1,0:T(8,128)S(1)}, f32[2,128,128]{2,1,0:T(8,128)S(1)}, u32[]{:S(2)}, u32[]{:S(2)}) collective-permute-start(f32[2,128,128]{2,1,0:T(8,128)S(1)} %get-tuple-element.45.refs_0_), channel_id=1, source_target_pairs={{0,8},{4,12},{8,0},{12,4},{16,24},{20,28},{24,16},{28,20},{1,9},{5... | collective-permute-start | bytes 393224 | tf_op jit(solution)/shard_map/ppermute | solution.py:336
  67.9 0.0 collective-permute-start.19
  67.9 2.3 %collective-permute-done.21.refs_3_ = f32[2,128,128]{2,1,0:T(8,128)S(1)} collective-permute-done((f32[2,128,128]{2,1,0:T(8,128)S(1)}, f32[2,128,128]{2,1,0:T(8,128)S(1)}, u32[]{:S(2)}, u32[]{:S(2)}) %collective-permute-start.21) | collective-permute-done | bytes 131104 | tf_op jit(solution)/shard_map/ppermute | solution.py:336
  70.3 4.3 %collective-permute-done.20.refs_2_ = f32[2,128,128]{2,1,0:T(8,128)S(1)} collective-permute-done((f32[2,128,128]{2,1,0:T(8,128)S(1)}, f32[2,128,128]{2,1,0:T(8,128)S(1)}, u32[]{:S(2)}, u32[]{:S(2)}) %collective-permute-start.20) | collective-permute-done | bytes 131104 | tf_op jit(solution)/shard_map/ppermute | solution.py:336
  74.6 0.0 collective-permute-done.19.refs_1_
  74.6 0.0 collective-permute-done.18.core_in
  74.6 0.9 %columns.1 = (f32[2,256,256]{2,1,0:T(8,128)}, f32[8,128,128]{2,1,0:T(8,128)S(1)}) custom-call(f32[2,256,256]{2,1,0:T(8,128)S(1)} %get-tuple-element.43.inner_grad, f32[2,128,256]{2,1,0:T(8,128)S(1)} %collective-permute-done.18.core_in, f32[2,128,128]{2,1,0:T(8,128)S(1)} %get-tuple-element.45.refs_0_, f32[2,128,128]{2,1,0:T(8,128)S(1)} %collective-permute-done.19.refs_1_, ...), custom_call_target="tpu_custom_call" | custom-call | bytes 2359296 | tf_op jit(solution)/shard_map/columns/pallas_call | solution.py:413
  75.5 0.0 collective-permute-start.22
  75.5 1.9 %collective-permute-done.22.other = f32[8,128,128]{2,1,0:T(8,128)S(1)} collective-permute-done((f32[8,128,128]{2,1,0:T(8,128)S(1)}, f32[8,128,128]{2,1,0:T(8,128)S(1)}, u32[]{:S(2)}, u32[]{:S(2)}) %collective-permute-start.22) | collective-permute-done | bytes 524320 | tf_op jit(solution)/shard_map/ppermute | solution.py:366
  77.4 1.3 %join.1 = f32[2,2,256,256]{3,2,1,0:T(8,128)} custom-call(f32[8,128,128]{2,1,0:T(8,128)S(1)} %get-tuple-element.47.own, f32[8,128,128]{2,1,0:T(8,128)S(1)} %collective-permute-done.22.other), custom_call_target="tpu_custom_call" | custom-call | bytes 2097152 | tf_op jit(solution)/shard_map/join/pallas_call | solution.py:413
  (9 shorter events, 0.1 us)
Async XLA Ops:
  0.6 15.5 %copy-start = (bf16[8,2,256,256]{3,2,1,0:T(8,128)(2,1)S(1)}, bf16[8,2,256,256]{3,2,1,0:T(8,128)(2,1)}, u32[]{:S(2)}) copy-start(bf16[8,2,256,256]{3,2,1,0:T(8,128)(2,1)} %constant.4.clone.tables) | copy-start | bytes 6291460
  0.6 1.2 %copy-start.3 = (f32[2,256,256]{2,1,0:T(8,128)S(1)}, f32[2,256,256]{2,1,0:T(8,128)}, u32[]{:S(2)}) copy-start(f32[2,256,256]{2,1,0:T(8,128)} %field.1) | copy-start | bytes 1572868
  2.0 1.7 %collective-permute-start = (f32[2,128,256]{2,1,0:T(8,128)S(1)}, f32[2,128,256]{2,1,0:T(8,128)S(1)}, u32[]{:S(2)}, u32[]{:S(2)}) collective-permute-start(f32[2,128,256]{2,1,0:T(8,128)S(1)} %get-tuple-element.27), channel_id=1, source_target_pairs={{0,4},{4,0},{8,12},{12,8},{16,20},{20,16},{24,28},{28,24},{1,5},{5... | collective-permute-start | bytes 786440 | tf_op jit(solution)/shard_map/ppermute | solution.py:366
  3.7 12.4 %collective-permute-start.2 = (f32[2,384,128]{2,1,0:T(8,128)S(1)}, f32[2,384,128]{2,1,0:T(8,128)S(1)}, u32[]{:S(2)}, u32[]{:S(2)}) collective-permute-start(f32[2,384,128]{2,1,0:T(8,128)S(1)} %get-tuple-element.29), channel_id=1, source_target_pairs={{0,1},{1,0},{2,3},{3,2},{4,5},{5,4},{6,7},{7,6},{8,9},{9,8},{10,11... | collective-permute-start | bytes 1179656 | tf_op jit(solution)/shard_map/ppermute | solution.py:366
  6.7 9.4 %collective-permute-start.3 = (f32[2,384,128]{2,1,0:T(8,128)S(1)}, f32[2,384,128]{2,1,0:T(8,128)S(1)}, u32[]{:S(2)}, u32[]{:S(2)}) collective-permute-start(f32[2,384,128]{2,1,0:T(8,128)S(1)} %get-tuple-element.30), channel_id=1, source_target_pairs={{1,2},{2,1},{5,6},{6,5},{9,10},{10,9},{13,14},{14,13},{17,18},{18,... | collective-permute-start | bytes 1179656 | tf_op jit(solution)/shard_map/ppermute | solution.py:366
  7.4 8.6 %collective-permute-start.1 = (f32[2,128,256]{2,1,0:T(8,128)S(1)}, f32[2,128,256]{2,1,0:T(8,128)S(1)}, u32[]{:S(2)}, u32[]{:S(2)}) collective-permute-start(f32[2,128,256]{2,1,0:T(8,128)S(1)} %get-tuple-element.28), channel_id=1, source_target_pairs={{4,8},{8,4},{12,16},{16,12},{20,24},{24,20},{5,9},{9,5},{13,17},{1... | collective-permute-start | bytes 786440 | tf_op jit(solution)/shard_map/ppermute | solution.py:366
  8.1 7.9 %collective-permute-start.4 = (f32[2,128,128]{2,1,0:T(8,128)S(1)}, f32[2,128,128]{2,1,0:T(8,128)S(1)}, u32[]{:S(2)}, u32[]{:S(2)}) collective-permute-start(f32[2,128,128]{2,1,0:T(8,128)S(1)} %get-tuple-element.31), channel_id=1, source_target_pairs={{4,9},{5,8},{6,11},{7,10},{8,5},{9,4},{10,7},{11,6},{12,17},{13,16... | collective-permute-start | bytes 393224 | tf_op jit(solution)/shard_map/ppermute | solution.py:377
  8.8 7.2 %collective-permute-start.5 = (f32[2,128,128]{2,1,0:T(8,128)S(1)}, f32[2,128,128]{2,1,0:T(8,128)S(1)}, u32[]{:S(2)}, u32[]{:S(2)}) collective-permute-start(f32[2,128,128]{2,1,0:T(8,128)S(1)} %get-tuple-element.32), channel_id=1, source_target_pairs={{5,10},{6,9},{9,6},{10,5},{13,18},{14,17},{17,14},{18,13},{21,26},... | collective-permute-start | bytes 393224 | tf_op jit(solution)/shard_map/ppermute | solution.py:377
  9.5 1.2 %copy-start.1 = (f32[2,2,256,256]{3,2,1,0:T(8,128)S(1)}, f32[2,2,256,256]{3,2,1,0:T(8,128)}, u32[]{:S(2)}) copy-start(f32[2,2,256,256]{3,2,1,0:T(8,128)} %probe.1) | copy-start | bytes 3145732
  10.7 1.1 %copy-start.2 = (f32[1,1,3,256,256]{4,3,2,1,0:T(8,128)S(1)}, f32[1,1,3,256,256]{4,3,2,1,0:T(8,128)}, u32[]{:S(2)}) copy-start(f32[1,1,3,256,256]{4,3,2,1,0:T(8,128)} %param.9) | copy-start | bytes 2359300
  11.8 0.9 %copy-start.4 = (bf16[256,256]{1,0:T(8,128)(2,1)S(1)}, bf16[256,256]{1,0:T(8,128)(2,1)}, u32[]{:S(2)}) copy-start(bf16[256,256]{1,0:T(8,128)(2,1)} %constant.5.clone.order) | copy-start | bytes 393220
  12.7 0.7 copy-start.5
  13.4 0.7 copy-start.6
  20.3 9.4 %collective-permute-start.11 = (f32[8,128,128]{2,1,0:T(8,128)S(1)}, f32[8,128,128]{2,1,0:T(8,128)S(1)}, u32[]{:S(2)}, u32[]{:S(2)}) collective-permute-start(f32[8,128,128]{2,1,0:T(8,128)S(1)} %get-tuple-element.42), channel_id=1, source_target_pairs={{0,4},{4,0},{8,12},{12,8},{16,20},{20,16},{24,28},{28,24},{1,5},{5... | collective-permute-start | bytes 1572872 | tf_op jit(solution)/shard_map/ppermute | solution.py:366
  29.8 10.9 %collective-permute-start.14 = (f32[2,128,128]{2,1,0:T(8,128)S(1)}, f32[2,128,128]{2,1,0:T(8,128)S(1)}, u32[]{:S(2)}, u32[]{:S(2)}) collective-permute-start(f32[2,128,128]{2,1,0:T(8,128)S(1)} %get-tuple-element.48), channel_id=1, source_target_pairs={{0,24},{4,28},{8,16},{12,20},{16,8},{20,12},{24,0},{28,4},{1,25},{... | collective-permute-start | bytes 393224 | tf_op jit(solution)/shard_map/ppermute | solution.py:336
  32.8 10.8 %collective-permute-start.13 = (f32[2,128,128]{2,1,0:T(8,128)S(1)}, f32[2,128,128]{2,1,0:T(8,128)S(1)}, u32[]{:S(2)}, u32[]{:S(2)}) collective-permute-start(f32[2,128,128]{2,1,0:T(8,128)S(1)} %get-tuple-element.49), channel_id=1, source_target_pairs={{0,8},{4,12},{8,0},{12,4},{16,24},{20,28},{24,16},{28,20},{1,9},{5... | collective-permute-start | bytes 393224 | tf_op jit(solution)/shard_map/ppermute | solution.py:336
  37.3 6.4 %collective-permute-start.12 = (f32[2,128,128]{2,1,0:T(8,128)S(1)}, f32[2,128,128]{2,1,0:T(8,128)S(1)}, u32[]{:S(2)}, u32[]{:S(2)}) collective-permute-start(f32[2,128,128]{2,1,0:T(8,128)S(1)} %get-tuple-element.50), channel_id=1, source_target_pairs={{0,16},{4,20},{8,24},{12,28},{16,0},{20,4},{24,8},{28,12},{1,17},{... | collective-permute-start | bytes 393224 | tf_op jit(solution)/shard_map/ppermute | solution.py:336
  37.3 21.0 %collective-permute-start.6 = (f32[2,384,128]{2,1,0:T(8,128)S(1)}, f32[2,384,128]{2,1,0:T(8,128)S(1)}, u32[]{:S(2)}, u32[]{:S(2)}) collective-permute-start(f32[2,384,128]{2,1,0:T(8,128)S(1)} %get-tuple-element.36), channel_id=1, source_target_pairs={{0,1},{1,0},{2,3},{3,2},{4,5},{5,4},{6,7},{7,6},{8,9},{9,8},{10,11... | collective-permute-start | bytes 1179656 | tf_op jit(solution)/shard_map/ppermute | solution.py:366
  40.1 18.2 %collective-permute-start.7 = (f32[2,384,128]{2,1,0:T(8,128)S(1)}, f32[2,384,128]{2,1,0:T(8,128)S(1)}, u32[]{:S(2)}, u32[]{:S(2)}) collective-permute-start(f32[2,384,128]{2,1,0:T(8,128)S(1)} %get-tuple-element.37), channel_id=1, source_target_pairs={{1,2},{2,1},{5,6},{6,5},{9,10},{10,9},{13,14},{14,13},{17,18},{18,... | collective-permute-start | bytes 1179656 | tf_op jit(solution)/shard_map/ppermute | solution.py:366
  43.7 6.8 %collective-permute-start.15 = (f32[1,128,128]{2,1,0:T(8,128)S(1)}, f32[1,128,128]{2,1,0:T(8,128)S(1)}, u32[]{:S(2)}, u32[]{:S(2)}) collective-permute-start(f32[1,128,128]{2,1,0:T(8,128)S(1)} %slice.19), channel_id=1, source_target_pairs={{0,1},{1,0},{2,3},{3,2},{4,5},{5,4},{6,7},{7,6},{8,9},{9,8},{10,11... | collective-permute-start | bytes 196616 | tf_op jit(solution)/shard_map/ppermute | solution.py:336
  45.5 12.8 %collective-permute-start.8 = (f32[2,128,256]{2,1,0:T(8,128)S(1)}, f32[2,128,256]{2,1,0:T(8,128)S(1)}, u32[]{:S(2)}, u32[]{:S(2)}) collective-permute-start(f32[2,128,256]{2,1,0:T(8,128)S(1)} %get-tuple-element.38), channel_id=1, source_target_pairs={{4,8},{8,4},{12,16},{16,12},{20,24},{24,20},{5,9},{9,5},{13,17},{1... | collective-permute-start | bytes 786440 | tf_op jit(solution)/shard_map/ppermute | solution.py:366
  50.5 5.3 %collective-permute-start.16 = (f32[1,128,128]{2,1,0:T(8,128)S(1)}, f32[1,128,128]{2,1,0:T(8,128)S(1)}, u32[]{:S(2)}, u32[]{:S(2)}) collective-permute-start(f32[1,128,128]{2,1,0:T(8,128)S(1)} %add.6.own), channel_id=1, source_target_pairs={{0,2},{1,3},{2,0},{3,1},{4,6},{5,7},{6,4},{7,5},{8,10},{9,11},{10,... | collective-permute-start | bytes 196616 | tf_op jit(solution)/shard_map/ppermute | solution.py:336
  52.1 4.5 %collective-permute-start.9 = (f32[2,128,128]{2,1,0:T(8,128)S(1)}, f32[2,128,128]{2,1,0:T(8,128)S(1)}, u32[]{:S(2)}, u32[]{:S(2)}) collective-permute-start(f32[2,128,128]{2,1,0:T(8,128)S(1)} %get-tuple-element.39), channel_id=1, source_target_pairs={{4,9},{5,8},{6,11},{7,10},{8,5},{9,4},{10,7},{11,6},{12,17},{13,16... | collective-permute-start | bytes 393224 | tf_op jit(solution)/shard_map/ppermute | solution.py:377
  55.9 2.4 %collective-permute-start.10 = (f32[2,128,128]{2,1,0:T(8,128)S(1)}, f32[2,128,128]{2,1,0:T(8,128)S(1)}, u32[]{:S(2)}, u32[]{:S(2)}) collective-permute-start(f32[2,128,128]{2,1,0:T(8,128)S(1)} %get-tuple-element.40), channel_id=1, source_target_pairs={{5,10},{6,9},{9,6},{10,5},{13,18},{14,17},{17,14},{18,13},{21,26},... | collective-permute-start | bytes 393224 | tf_op jit(solution)/shard_map/ppermute | solution.py:377
  56.6 4.3 %collective-permute-start.17 = (f32[1,128,128]{2,1,0:T(8,128)S(1)}, f32[1,128,128]{2,1,0:T(8,128)S(1)}, u32[]{:S(2)}, u32[]{:S(2)}) collective-permute-start(f32[1,128,128]{2,1,0:T(8,128)S(1)} %add.7.own), channel_id=1, source_target_pairs={{0,1},{1,0},{2,3},{3,2},{4,5},{5,4},{6,7},{7,6},{8,9},{9,8},{10,11... | collective-permute-start | bytes 196616 | tf_op jit(solution)/shard_map/ppermute | solution.py:336
  61.1 13.6 %collective-permute-start.18 = (f32[2,128,256]{2,1,0:T(8,128)S(1)}, f32[2,128,256]{2,1,0:T(8,128)S(1)}, u32[]{:S(2)}, u32[]{:S(2)}) collective-permute-start(f32[2,128,256]{2,1,0:T(8,128)S(1)} %get-tuple-element.44), channel_id=1, source_target_pairs={{0,4},{4,0},{8,12},{12,8},{16,20},{20,16},{24,28},{28,24},{1,5},{5... | collective-permute-start | bytes 786440 | tf_op jit(solution)/shard_map/ppermute | solution.py:366
  61.7 8.6 %collective-permute-start.21 = (f32[2,128,128]{2,1,0:T(8,128)S(1)}, f32[2,128,128]{2,1,0:T(8,128)S(1)}, u32[]{:S(2)}, u32[]{:S(2)}) collective-permute-start(f32[2,128,128]{2,1,0:T(8,128)S(1)} %get-tuple-element.45.refs_0_), channel_id=1, source_target_pairs={{0,24},{4,28},{8,16},{12,20},{16,8},{20,12},{24,0},{28,4},{1,25},{... | collective-permute-start | bytes 393224 | tf_op jit(solution)/shard_map/ppermute | solution.py:336
  65.9 8.7 %collective-permute-start.20 = (f32[2,128,128]{2,1,0:T(8,128)S(1)}, f32[2,128,128]{2,1,0:T(8,128)S(1)}, u32[]{:S(2)}, u32[]{:S(2)}) collective-permute-start(f32[2,128,128]{2,1,0:T(8,128)S(1)} %get-tuple-element.45.refs_0_), channel_id=1, source_target_pairs={{0,8},{4,12},{8,0},{12,4},{16,24},{20,28},{24,16},{28,20},{1,9},{5... | collective-permute-start | bytes 393224 | tf_op jit(solution)/shard_map/ppermute | solution.py:336
  67.9 6.7 %collective-permute-start.19 = (f32[2,128,128]{2,1,0:T(8,128)S(1)}, f32[2,128,128]{2,1,0:T(8,128)S(1)}, u32[]{:S(2)}, u32[]{:S(2)}) collective-permute-start(f32[2,128,128]{2,1,0:T(8,128)S(1)} %get-tuple-element.45.refs_0_), channel_id=1, source_target_pairs={{0,16},{4,20},{8,24},{12,28},{16,0},{20,4},{24,8},{28,12},{1,17},{... | collective-permute-start | bytes 393224 | tf_op jit(solution)/shard_map/ppermute | solution.py:336
  75.5 1.9 %collective-permute-start.22 = (f32[8,128,128]{2,1,0:T(8,128)S(1)}, f32[8,128,128]{2,1,0:T(8,128)S(1)}, u32[]{:S(2)}, u32[]{:S(2)}) collective-permute-start(f32[8,128,128]{2,1,0:T(8,128)S(1)} %get-tuple-element.47.own), channel_id=1, source_target_pairs={{0,4},{4,0},{8,12},{12,8},{16,20},{20,16},{24,28},{28,24},{1,5},{5... | collective-permute-start | bytes 1572872 | tf_op jit(solution)/shard_map/ppermute | solution.py:366
